TPU v7x, 32 devices: a whole 2x2x4 slice. The times are simulated.
32 devices in a mesh: rows: 8 (over y, x, core), imgs: 4 (over z).
Axes of the slice: x: 2, y: 2, z: 4, core: 2. Of those that a mesh axis runs over, the one named last changes fastest.
Arguments:
- images: bfloat16 [4, 128, 256, 180], P('imgs', 'rows'), may hold values from -6 to 6
- widths: int32 [4], P('imgs'), may hold values from 64 to 256, as said below
- norm1_gain: float32 [180], replicated, may hold values from 0.5 to 1.5
- norm1_bias: float32 [180], replicated, may hold values from -3 to 3
- qkv_weight: bfloat16 [180, 540], replicated, may hold values from -0.4375 to 0.4375
- qv_bias: float32 [360], replicated, may hold values from -3 to 3
- bias_table: float32 [225, 6], replicated, may hold values from -4 to 4
- proj_weight: bfloat16 [180, 180], replicated, may hold values from -1.25 to 1.25
- proj_bias: float32 [180], replicated, may hold values from -3 to 3
- norm2_gain: float32 [180], replicated, may hold values from 0.5 to 1.5
- norm2_bias: float32 [180], replicated, may hold values from -3 to 3
- fc1_weight: bfloat16 [180, 360], replicated, may hold values from -0.4375 to 0.4375
- fc1_bias: float32 [360], replicated, may hold values from -3 to 3
- fc2_weight: bfloat16 [360, 180], replicated, may hold values from -0.4375 to 0.4375
- fc2_bias: float32 [180], replicated, may hold values from -3 to 3
- conv_weight: bfloat16 [3, 3, 180, 180], replicated, may hold values from -0.15625 to 0.15625
- conv_bias: float32 [180], replicated, may hold values from -3 to 3
- cotangent: bfloat16 [4, 128, 256, 180], P('imgs', 'rows'), may hold values from -6 to 6
Outputs:
- result: bfloat16 [4, 128, 256, 180], P('imgs', 'rows')
- input_grad: bfloat16 [4, 128, 256, 180], P('imgs', 'rows')
- norm1_gain_grad: float32 [180], replicated
- norm1_bias_grad: float32 [180], replicated
- qkv_weight_grad: float32 [180, 540], replicated
- qv_bias_grad: float32 [360], replicated
- bias_table_grad: float32 [225, 6], replicated
- proj_weight_grad: float32 [180, 180], replicated
- proj_bias_grad: float32 [180], replicated
- norm2_gain_grad: float32 [180], replicated
- norm2_bias_grad: float32 [180], replicated
- fc1_weight_grad: float32 [180, 360], replicated
- fc1_bias_grad: float32 [360], replicated
- fc2_weight_grad: float32 [360, 180], replicated
- fc2_bias_grad: float32 [180], replicated
- conv_weight_grad: float32 [3, 3, 180, 180], replicated
- conv_bias_grad: float32 [180], replicated
Inputs may be any that keep to these rules, and one draw needn't show every extreme that they name: `widths`: every width is a multiple of 8; one image of all is exactly 256 wide.
All inputs are finite; a program needn't handle non-finite values.
Results may differ from a plain program's by a relative error of at most 0.015.
Values may be sent and summed in bfloat16 or wider, within the bound.
A program may use at most 192 MiB of HBM per device.

v0:
```python
import jax
import jax.numpy as jnp
from jax import lax
from jax.sharding import PartitionSpec as P

HEADS = 6
HEAD_DIM = 30
WIN = 8
SHIFT = 4


def passed_along(value, axis, steps):
    count = lax.axis_size(axis)
    pairs = [(source, (source + steps) % count) for source in range(count)]
    return lax.ppermute(value, axis, pairs)


def extended(shard, sides, width):
    for axis, dim in sides:
        size, length = (lax.axis_size(axis), shard.shape[dim])
        up = [(i, (i + 1) % size) for i in range(size - 1)]
        down = [(j, i) for i, j in up]
        last = lax.slice_in_dim(shard, length - width, length, axis=dim)
        leading = lax.slice_in_dim(shard, 0, width, axis=dim)
        before = lax.ppermute(last, axis, up)
        after = lax.ppermute(leading, axis, down)
        shard = jnp.concatenate([before, shard, after], axis=dim)
    return shard


def layer_norm(values, gain, shift):
    mean = jnp.mean(values, axis=-1, keepdims=True)
    centred = values - mean
    spread = jnp.mean(centred * centred, axis=-1, keepdims=True)
    return centred * lax.rsqrt(spread + 1e-05) * gain + shift


def exact_gelu(values):
    return jax.nn.gelu(values, approximate=False)


def to_windows(field, side):
    count, height, width, chans = field.shape
    tiles = field.reshape(count, height // side, side, width // side, side, chans)
    return tiles.transpose(0, 1, 3, 2, 4, 5).reshape(
        count, height // side * (width // side), side * side, chans
    )


def from_windows(tiles, height, width, side):
    count = tiles.shape[0]
    chans = tiles.shape[-1]
    field = tiles.reshape(count, height // side, width // side, side, side, chans)
    return field.transpose(0, 1, 3, 2, 4, 5).reshape(count, height, width, chans)


def relative_index(side):
    coords = jnp.arange(side * side)
    row_of = coords // side
    col_of = coords % side
    return (
        (row_of[:, None] - row_of[None, :] + side - 1) * (2 * side - 1)
        + col_of[:, None]
        - col_of[None, :]
        + side
        - 1
    )


def column_index(widths, width, offset):
    columns = jnp.arange(width)[None, :]
    limit = widths[:, None]
    return jnp.where(columns < limit, (columns + offset) % limit, columns)


def move_columns(field, index):
    return jax.vmap(lambda plane, picks: jnp.take(plane, picks, axis=1))(field, index)


def region_mask(first_row, rows_here, height, widths, width, side, offset):
    glob_rows = first_row + jnp.arange(rows_here)
    row_band = jnp.where(glob_rows < height - side, 0, jnp.where(glob_rows < height - offset, 1, 2))
    columns = jnp.arange(width)[None, :]
    limit = widths[:, None]
    col_band = jnp.where(columns < limit - side, 0, jnp.where(columns < limit - offset, 1, 2))
    region = (row_band[None, :, None] * 3 + col_band[:, None, :]).astype(jnp.int32)
    tiles = to_windows(region[:, :, :, None], side)[:, :, :, 0]
    return jnp.where(tiles[:, :, :, None] == tiles[:, :, None, :], 0.0, -100.0).astype(jnp.float32)


def on_device(
    images,
    widths,
    norm1_gain,
    norm1_bias,
    qkv_weight,
    qv_bias,
    bias_table,
    proj_weight,
    proj_bias,
    norm2_gain,
    norm2_bias,
    fc1_weight,
    fc1_bias,
    fc2_weight,
    fc2_bias,
    conv_weight,
    conv_bias,
    cotangent,
):
    f32 = jnp.float32
    bf16 = jnp.bfloat16
    highest = lax.Precision.HIGHEST
    count, rows_here, width, chans = images.shape
    side = WIN
    offset = SHIFT
    heads = HEADS
    head_size = chans // heads
    scale = HEAD_DIM ** (-0.5)
    stripes = lax.axis_size("rows")
    height = rows_here * stripes
    first_row = lax.axis_index("rows") * rows_here
    windows = rows_here // side * (width // side)
    area = side * side
    inside = (jnp.arange(width)[None, :] < widths[:, None]).astype(f32)[:, None, :, None]
    ahead = column_index(widths, width, offset)
    behind = column_index(widths, width, -offset)
    lookup = relative_index(side)
    table_hot = (lookup.reshape(-1)[:, None] == jnp.arange(bias_table.shape[0])[None, :]).astype(
        f32
    )
    rel_bias = (
        jnp.dot(table_hot, bias_table, precision=highest)
        .reshape(area, area, heads)
        .transpose(2, 0, 1)
    )
    masking = region_mask(first_row, rows_here, height, widths, width, side, offset)
    extra = rel_bias[None, None] + masking[:, :, None]
    source = images.astype(f32)
    normed, norm1_back = jax.vjp(layer_norm, source, norm1_gain, norm1_bias)
    normed_low = normed.astype(bf16)
    below = passed_along(normed_low[:, :offset], "rows", -1)
    shifted = move_columns(jnp.concatenate([normed_low[:, offset:], below], axis=1), ahead)
    tokens_win = to_windows(shifted, side)
    qkv_bias = jnp.concatenate([qv_bias[:chans], jnp.zeros((chans,), f32), qv_bias[chans:]])
    projected = (
        jnp.einsum("bnic,co->bnio", tokens_win, qkv_weight, preferred_element_type=f32) + qkv_bias
    ).astype(bf16)
    split = projected.reshape(count, windows, area, 3, heads, head_size)
    queries = split[:, :, :, 0]
    keys = split[:, :, :, 1]
    values = split[:, :, :, 2]

    def window_scores():
        return (
            jnp.einsum("bnihd,bnjhd->bnhij", queries, keys, preferred_element_type=f32) * scale
            + extra
        )

    scores = window_scores()
    top = jnp.max(scores, axis=-1, keepdims=True)
    expo = jnp.exp(scores - top)
    total = jnp.sum(expo, axis=-1, keepdims=True)
    probs = expo / total
    log_total = top + jnp.log(total)
    mixed = jnp.einsum("bnhij,bnjhd->bnihd", probs.astype(bf16), values, preferred_element_type=f32)
    mixed = mixed.reshape(count, windows, area, chans).astype(bf16)
    mixed_img = move_columns(from_windows(mixed, rows_here, width, side), behind)
    above = passed_along(mixed_img[:, rows_here - offset :], "rows", 1)
    restored = jnp.concatenate([above, mixed_img[:, : rows_here - offset]], axis=1)
    first_sum = (
        source
        + jnp.einsum("brwc,co->brwo", restored, proj_weight, preferred_element_type=f32)
        + proj_bias
    )
    normed2, norm2_back = jax.vjp(layer_norm, first_sum, norm2_gain, norm2_bias)
    normed2_low = normed2.astype(bf16)
    hidden = (
        jnp.einsum("brwc,ch->brwh", normed2_low, fc1_weight, preferred_element_type=f32) + fc1_bias
    )
    activated, gelu_back = jax.vjp(exact_gelu, hidden)
    act_low = activated.astype(bf16)
    second_sum = (
        first_sum
        + jnp.einsum("brwh,hc->brwc", act_low, fc2_weight, preferred_element_type=f32)
        + fc2_bias
    )
    layer_low = (second_sum * inside).astype(bf16)
    framed = extended(layer_low, (("rows", 1),), 1)
    framed = jnp.pad(framed, ((0, 0), (0, 0), (1, 1), (0, 0)))
    conv_out = jnp.zeros((count, rows_here, width, chans), f32)
    for row_tap in range(3):
        for col_tap in range(3):
            conv_out = conv_out + jnp.einsum(
                "brwc,co->brwo",
                framed[:, row_tap : row_tap + rows_here, col_tap : col_tap + width],
                conv_weight[row_tap, col_tap],
                preferred_element_type=f32,
            )
    result = ((conv_out + conv_bias + source) * inside).astype(bf16)
    out_grad = cotangent.astype(f32) * inside
    cot_low = out_grad.astype(bf16)
    conv_bias_grad = jnp.sum(out_grad, axis=(0, 1, 2))
    conv_weight_grad = jnp.stack(
        [
            jnp.stack(
                [
                    jnp.einsum(
                        "brwc,brwo->co",
                        framed[:, row_tap : row_tap + rows_here, col_tap : col_tap + width],
                        cot_low,
                        preferred_element_type=f32,
                    )
                    for col_tap in range(3)
                ]
            )
            for row_tap in range(3)
        ]
    )
    cot_frame = extended(cot_low, (("rows", 1),), 1)
    cot_frame = jnp.pad(cot_frame, ((0, 0), (0, 0), (1, 1), (0, 0)))
    layer_grad = jnp.zeros((count, rows_here, width, chans), f32)
    for row_tap in range(3):
        for col_tap in range(3):
            layer_grad = layer_grad + jnp.einsum(
                "brwo,co->brwc",
                cot_frame[
                    :, 2 - row_tap : 2 - row_tap + rows_here, 2 - col_tap : 2 - col_tap + width
                ],
                conv_weight[row_tap, col_tap],
                preferred_element_type=f32,
            )
    layer_grad = layer_grad * inside
    mlp_grad = layer_grad.astype(bf16)
    fc2_bias_grad = jnp.sum(mlp_grad.astype(f32), axis=(0, 1, 2))
    fc2_weight_grad = jnp.einsum("brwh,brwc->hc", act_low, mlp_grad, preferred_element_type=f32)
    act_grad = (
        jnp.einsum("brwc,hc->brwh", mlp_grad, fc2_weight, preferred_element_type=f32)
        .astype(bf16)
        .astype(f32)
    )
    hidden_grad = gelu_back(act_grad)[0].astype(bf16)
    fc1_bias_grad = jnp.sum(hidden_grad.astype(f32), axis=(0, 1, 2))
    fc1_weight_grad = jnp.einsum(
        "brwc,brwh->ch", normed2_low, hidden_grad, preferred_element_type=f32
    )
    normed2_grad = (
        jnp.einsum("brwh,ch->brwc", hidden_grad, fc1_weight, preferred_element_type=f32)
        .astype(bf16)
        .astype(f32)
    )
    ln2_grad, norm2_gain_grad, norm2_bias_grad = norm2_back(normed2_grad)
    first_grad = layer_grad + ln2_grad
    attn_grad = first_grad.astype(bf16)
    proj_bias_grad = jnp.sum(attn_grad.astype(f32), axis=(0, 1, 2))
    proj_weight_grad = jnp.einsum("brwc,brwo->co", restored, attn_grad, preferred_element_type=f32)
    restored_grad = jnp.einsum(
        "brwo,co->brwc", attn_grad, proj_weight, preferred_element_type=f32
    ).astype(bf16)
    spill = passed_along(restored_grad[:, :offset], "rows", -1)
    heads_shifted = move_columns(jnp.concatenate([restored_grad[:, offset:], spill], axis=1), ahead)
    mixed_grad = to_windows(heads_shifted, side).reshape(count, windows, area, heads, head_size)
    again = jnp.exp(window_scores() - log_total)
    again_low = again.astype(bf16)
    probs_grad = jnp.einsum("bnihd,bnjhd->bnhij", mixed_grad, values, preferred_element_type=f32)
    score_grad = (
        again * (probs_grad - jnp.sum(again * probs_grad, axis=-1, keepdims=True))
    ).astype(bf16)
    query_grad = (
        jnp.einsum("bnhij,bnjhd->bnihd", score_grad, keys, preferred_element_type=f32) * scale
    )
    key_grad = (
        jnp.einsum("bnhij,bnihd->bnjhd", score_grad, queries, preferred_element_type=f32) * scale
    )
    value_grad = jnp.einsum("bnhij,bnihd->bnjhd", again_low, mixed_grad, preferred_element_type=f32)
    rel_grad = jnp.sum(score_grad.astype(f32), axis=(0, 1))
    bias_table_grad = jnp.dot(
        table_hot.T, rel_grad.transpose(1, 2, 0).reshape(area * area, heads), precision=highest
    )
    projected_grad = (
        jnp.stack([query_grad, key_grad, value_grad], axis=3)
        .reshape(count, windows, area, 3 * chans)
        .astype(bf16)
    )
    column_sums = jnp.sum(projected_grad.astype(f32), axis=(0, 1, 2))
    qv_bias_grad = jnp.concatenate([column_sums[:chans], column_sums[2 * chans :]])
    qkv_weight_grad = jnp.einsum(
        "bnic,bnio->co", tokens_win, projected_grad, preferred_element_type=f32
    )
    tokens_grad = jnp.einsum(
        "bnio,co->bnic", projected_grad, qkv_weight, preferred_element_type=f32
    ).astype(bf16)
    shifted_grad = move_columns(from_windows(tokens_grad, rows_here, width, side), behind)
    wrapped = passed_along(shifted_grad[:, rows_here - offset :], "rows", 1)
    normed_grad = jnp.concatenate([wrapped, shifted_grad[:, : rows_here - offset]], axis=1).astype(
        f32
    )
    ln1_grad, norm1_gain_grad, norm1_bias_grad = norm1_back(normed_grad)
    input_grad = (out_grad + first_grad + ln1_grad).astype(bf16)
    summed = lax.psum(
        (
            norm1_gain_grad,
            norm1_bias_grad,
            qkv_weight_grad,
            qv_bias_grad,
            bias_table_grad,
            proj_weight_grad,
            proj_bias_grad,
            norm2_gain_grad,
            norm2_bias_grad,
            fc1_weight_grad,
            fc1_bias_grad,
            fc2_weight_grad,
            fc2_bias_grad,
            conv_weight_grad,
            conv_bias_grad,
        ),
        ("rows", "imgs"),
    )
    return (
        result,
        input_grad,
        summed[0],
        summed[1],
        summed[2],
        summed[3],
        summed[4],
        summed[5],
        summed[6],
        summed[7],
        summed[8],
        summed[9],
        summed[10],
        summed[11],
        summed[12],
        summed[13],
        summed[14],
    )


def solution(mesh):
    in_specs = (
        P("imgs", "rows", None, None),
        P("imgs"),
        P(),
        P(),
        P(),
        P(),
        P(),
        P(),
        P(),
        P(),
        P(),
        P(),
        P(),
        P(),
        P(),
        P(),
        P(),
        P("imgs", "rows", None, None),
    )
    out_specs = (
        P("imgs", "rows", None, None),
        P("imgs", "rows", None, None),
        P(),
        P(),
        P(),
        P(),
        P(),
        P(),
        P(),
        P(),
        P(),
        P(),
        P(),
        P(),
        P(),
        P(),
        P(),
    )
    return jax.shard_map(
        on_device, mesh=mesh, in_specs=in_specs, out_specs=out_specs, check_vma=False
    )
```

profile of v0, /device:TPU:0, one launch (start us, length us, event | category | flops | bytes accessed | tf_op | source)
XLA Modules:
  0.0 575.5 jit_solution(1134113049931069166)
XLA Ops:
  68.7 4.2 add_convert_fusion
  72.9 15.4 %copy.231 = bf16[64,64,540]{1,0,2:T(8,128)(2,1)} copy(bf16[64,64,540]{2,1,0:T(8,128)(2,1)} %add_convert_fusion) | data formatting | bytes 8847360 | tf_op jit(solution)/shard_map/convert_element_type | solution.py:148
  88.4 7.1 %fusion.233 = (bf16[1,64,64,1,6,30]{2,1,5,4,3,0:T(8,128)(2,1)}, bf16[1,64,64,1,6,30]{2,1,5,4,3,0:T(8,128)(2,1)}, bf16[1,64,64,1,6,30]{2,1,5,4,3,0:T(8,128)(2,1)}) fusion(bf16[1,64,64,3,6,30]{2,1,5,4,3,0:T(8,128)(2,1)} %bitcast.487), kind=kLoop, calls=%fused_computation.325 | loop fusion | bytes 8847360 | tf_op jit(solution)/shard_map/slice | solution.py:152
  95.5 14.1 %fusion.238 = (f32[64,6,64]{2,1,0:T(8,128)S(1)}, f32[64,6,64,64]{2,3,1,0:T(8,128)S(1)}) fusion(f32[64,64,64]{1,2,0:T(8,128)} %compare_select_fusion, f32[6,64,64]{1,2,0:T(8,128)S(1)} %bitcast.497, bf16[1,64,64,1,6,30]{2,1,5,4,3,0:T(8,128)(2,1)} %get-tuple-element.136, bf16[1,64,64,1,6,30]{2,1,5,4,3,0:T(8,128)(2,1)} %get-tuple-element.135), kind=kOutput, calls=%fused_computation.330 | convolution fusion | flops 100638720 | bytes 10485760 | tf_op jit(solution)/shard_map/bnihd,bnjhd->bnhij/dot_general | solution.py:156
  109.6 4.3 fusion
  114.6 10.4 %convert_bitcast_fusion.1 = bf16[1,64,64,6,30]{2,4,3,1,0:T(8,128)(2,1)} fusion(f32[64,6,64,64]{2,3,1,0:T(8,128)S(1)} %get-tuple-element.148, f32[64,6,64]{2,1,0:T(8,128)S(1)} %fusion, f32[64,6,64]{2,1,0:T(8,128)S(1)} %get-tuple-element.147, bf16[1,64,64,1,6,30]{2,1,5,4,3,0:T(8,128)(2,1)} %get-tuple-element.134), kind=kOutput, calls=%fused_computation.80 | convolution fusion | flops 99827712 | bytes 9437184 | tf_op jit(solution)/shard_map/bnhij,bnjhd->bnihd/dot_general | solution.py:166
  125.0 4.8 copy.239
  129.8 5.2 convert_element_type.188
  135.0 14.0 %copy.240 = bf16[1,2,8,32,8,180]{5,4,3,2,1,0:T(8,128)(2,1)} copy(bf16[1,2,8,32,8,180]{3,1,4,2,5,0:T(2,128)(2,1)} %bitcast.489) | data formatting | bytes 2949120 | tf_op jit(solution)/shard_map/transpose | solution.py:54
  154.0 4.6 copy.242
  160.8 10.0 %convert_reduce_fusion.6 = (f32[180]{0:T(256)}, f32[16,256,180]{1,2,0:T(8,128)S(1)}) fusion(f32[256]{0:T(256)S(1)} %compare_convert_fusion, bf16[3,3,180,180]{3,2,1,0:T(8,128)(2,1)} %param.37, bf16[1,18,258,180]{2,3,1,0:T(8,128)(2,1)S(1)} %copy-done.6, f32[16,256,180]{1,2,0:T(8,128)} %fusion.63, f32[16,256,180]{1,2,0:T(8,128)} %fusion.66, ...), kind=kOutput, calls=%fused_computation.99 | convolution fusion | flops 274267968 | bytes 28669648 | tf_op jit(solution)/shard_map/brwo,co->brwc/dot_general | solution.py:225
  178.3 15.4 %multiply_convert_fusion.1 = (bf16[16,256,360]{1,2,0:T(8,128)(2,1)S(1)}, f32[16,256,360]{1,2,0:T(8,128)}) fusion(f32[16,256,360]{1,2,0:T(8,128)S(1)} %get-tuple-element.151, f32[360]{0:T(512)S(1)} %copy-done.70, u16[256,360]{0,1:T(8,128)(2,1)S(1)} %get-tuple-element.105, u16[256,360]{0,1:T(8,128)(2,1)S(1)} %get-tuple-element.104), kind=kLoop, calls=%fused_computation.40 | loop fusion | flops 104693760 | bytes 15115680 | tf_op jit(solution)/shard_map/convert_element_type | solution.py:182
  198.8 6.1 %convert_reduce_fusion.2 = (f32[360]{0:T(512)}, bf16[16,256,360]{1,2,0:T(8,128)(2,1)S(1)}) fusion(f32[16,256,360]{1,2,0:T(8,128)} %get-tuple-element.133, bf16[360,180]{0,1:T(8,128)(2,1)S(1)} %copy-done.46, f32[16,256,180]{1,2,0:T(8,128)S(1)} %get-tuple-element.159, f32[16,256,360]{1,2,0:T(8,128)S(1)} %get-tuple-element.151, f32[360]{0:T(512)S(1)} %copy-done.70), kind=kOutput, calls=%fused_computation.39 | convolution fusion | flops 559595136 | bytes 17827200 | tf_op jit(solution)/shard_map/brwc,hc->brwh/dot_general | solution.py:238
  248.2 8.0 %fusion.42 = bf16[1,16,256,180]{2,3,1,0:T(8,128)(2,1)S(1)} fusion(f32[16,256,180]{1,2,0:T(8,128)S(1)} %fusion.149, f32[16,256,180]{1,2,0:T(8,128)} %fusion.110, f32[16,256,180]{1,2,0:T(8,128)} %fusion.109, f32[16,256,180]{1,2,0:T(8,128)S(1)} %fusion.101, f32[16,256,180]{1,2,0:T(8,128)} %fusion.108, f32[16,256,180]{1,2,0:T(8,128)} %fusion.107, ...), kind=kOutput, calls=%fused_computation.93 | convolution fusion | flops 275005440 | bytes 28669952 | tf_op jit(solution)/shard_map/brwc,co->brwo/dot_general | solution.py:194
  262.9 4.4 copy.263
  275.1 13.6 %copy.265 = bf16[1,2,32,8,8,180]{2,1,4,3,5,0:T(2,128)(2,1)} copy(bf16[1,2,32,8,8,180]{5,4,2,3,1,0:T(8,128)(2,1)} %bitcast.493) | data formatting | bytes 2949120 | tf_op jit(solution)/shard_map/transpose | solution.py:45
  288.7 10.4 %reshape.912 = bf16[64,64,6,30]{0,1,3,2:T(8,128)(2,1)} reshape(bf16[1,2,32,8,8,180]{2,1,4,3,5,0:T(2,128)(2,1)} %copy.265) | data formatting | bytes 2949120 | tf_op jit(solution)/shard_map/reshape.133
  299.1 5.7 copy.266
  304.9 10.7 %fusion.53 = bf16[1,64,64,1,6,30]{2,5,4,1,3,0:T(8,128)(2,1)} fusion(bf16[64,64,6,30]{1,3,2,0:T(8,128)(2,1)} %copy.266, f32[64,6,64,64]{2,3,1,0:T(8,128)} %copy-done.1, f32[64,6,64]{2,1,0:T(8,128)S(1)} %log_add_fusion), kind=kOutput, calls=%fused_computation.113 | convolution fusion | flops 97517568 | bytes 9338880 | tf_op jit(solution)/shard_map/bnhij,bnihd->bnjhd/dot_general | solution.py:275
  315.5 17.7 %multiply_reduce_fusion = (f32[64,6,64]{2,1,0:T(8,128)}, f32[64,6,64,64]{2,3,1,0:T(8,128)}) fusion(f32[64,6,64,64]{2,3,1,0:T(8,128)} %copy-done.1, f32[64,6,64]{2,1,0:T(8,128)S(1)} %log_add_fusion, bf16[64,64,6,30]{1,3,2,0:T(8,128)(2,1)S(1)} %copy-done.13, bf16[1,64,64,1,6,30]{2,1,5,4,3,0:T(8,128)(2,1)} %get-tuple-element.134), kind=kOutput, calls=%fused_computation.8 | convolution fusion | flops 99065856 | bytes 15728640 | tf_op jit(solution)/shard_map/bnihd,bnjhd->bnhij/dot_general | solution.py:265
  333.2 11.3 %convert_reduce_fusion.1 = (f32[6,64,64]{1,2,0:T(8,128)}, bf16[64,6,64,64]{2,3,1,0:T(8,128)(2,1)S(1)}) fusion(f32[64,6,64,64]{2,3,1,0:T(8,128)} %get-tuple-element.155, f32[64,6,64]{2,1,0:T(8,128)} %get-tuple-element.154, f32[64,6,64,64]{2,3,1,0:T(8,128)} %copy-done.1, f32[64,6,64]{2,1,0:T(8,128)S(1)} %log_add_fusion), kind=kLoop, calls=%fused_computation.6 | loop fusion | flops 9412608 | bytes 16023552 | tf_op jit(solution)/shard_map/reduce_sum | solution.py:276
  344.5 8.3 %multiply_bitcast_fusion = bf16[1,64,64,1,6,30]{2,5,4,1,3,0:T(8,128)(2,1)} fusion(bf16[64,6,64,64]{2,3,1,0:T(8,128)(2,1)S(1)} %get-tuple-element.129, bf16[1,64,64,1,6,30]{2,1,5,4,3,0:T(8,128)(2,1)S(1)} %copy-done.12), kind=kOutput, calls=%fused_computation.22 | convolution fusion | flops 95846400 | bytes 6094848 | tf_op jit(solution)/shard_map/bnhij,bnihd->bnjhd/dot_general | solution.py:273
  352.7 7.1 %multiply_bitcast_fusion.1 = bf16[1,64,64,1,6,30]{2,5,4,1,3,0:T(8,128)(2,1)S(1)} fusion(bf16[64,6,64,64]{2,3,1,0:T(8,128)(2,1)S(1)} %get-tuple-element.129, bf16[1,64,64,1,6,30]{2,1,5,4,3,0:T(8,128)(2,1)S(1)} %copy-done.11), kind=kOutput, calls=%fused_computation.23 | convolution fusion | flops 95846400 | bytes 6094848 | tf_op jit(solution)/shard_map/bnhij,bnjhd->bnihd/dot_general | solution.py:270
  359.9 6.4 %convert_reduce_fusion = (f32[3,6,30]{2,1,0:T(8,128)S(1)}, bf16[1,64,64,3,6,30]{2,5,4,1,3,0:T(8,128)(2,1)}) fusion(bf16[1,64,64,1,6,30]{2,5,4,1,3,0:T(8,128)(2,1)S(1)} %copy-done.17, bf16[1,64,64,1,6,30]{2,5,4,1,3,0:T(8,128)(2,1)S(1)} %copy-done.18, bf16[1,64,64,1,6,30]{2,5,4,1,3,0:T(8,128)(2,1)S(1)} %multiply_bitcast_fusion.1), kind=kLoop, calls=%fused_computation.5 | loop fusion | flops 8846820 | bytes 8849520 | tf_op jit(solution)/shard_map/reduce_sum | solution.py:285
  366.4 12.8 %copy.271 = bf16[1,64,64,3,6,30]{2,1,5,4,3,0:T(8,128)(2,1)} copy(bf16[1,64,64,3,6,30]{2,5,4,1,3,0:T(8,128)(2,1)} %get-tuple-element.131) | data formatting | bytes 8847360 | tf_op jit(solution)/shard_map/convert_element_type | solution.py:283
  379.2 13.6 %copy.272 = bf16[64,64,540]{2,1,0:T(8,128)(2,1)} copy(bf16[64,64,540]{1,0,2:T(8,128)(2,1)} %bitcast.488) | data formatting | bytes 8847360 | tf_op jit(solution)/shard_map/convert_element_type | solution.py:283
  392.8 5.3 convolution_bitcast_fusion
  398.1 4.3 convolution_convert_fusion
  408.9 4.7 copy.275
  429.9 4.1 add_convert_fusion.1
  435.4 40.1 %all-reduce.2 = (f32[180]{0:T(256)}, f32[180]{0:T(256)}, f32[360]{0:T(512)}, f32[225,6]{0,1:T(8,128)}, f32[180]{0:T(256)}, /*index=5*/f32[180]{0:T(256)}, f32[18...) all-reduce(f32[180]{0:T(256)S(1)} %get-tuple-element.108, ...), channel_id=1, replica_groups=mesh['rows'=8,'imgs'=4] {'rows','imgs'}, use_global_device_ids=true, to_apply=%region_12.15 | all-reduce | flops 3330 | bytes 26640 | tf_op jit(solution)/shard_map/psum | solution.py:300
  475.5 84.7 %all-reduce.6.cloned.1.call-done = (f32[180,540]{1,0:T(8,128)}, f32[180,180]{1,0:T(8,128)}, f32[180,360]{1,0:T(8,128)}, f32[360,180]{0,1:T(8,128)}, f32[3,3,180,180]{3,2,1,0:T(8,128)}) async-done(((f32[180,540]{1,0:T(8,128)}, f32[180,180]{1,0:T(8,128)}, f32[180,360]{1,0:T(8,128)}, f32[360,180]{0,1:T(8,128)}, f32[3,3,180,180]{3,2,1,0:T(8,128)}), (f32[180,540]{1,0:T(8,128)}, f32[180,180]{1,0:T(8,128)}, ...) | async-done | bytes 2203216 | tf_op jit(solution)/shard_map/psum | solution.py:300
  (304 shorter events, 170.4 us)
Async XLA Ops:
  7.2 61.5 %copy-start = (bf16[180,540]{1,0:T(8,128)(2,1)S(1)}, bf16[180,540]{1,0:T(8,128)(2,1)}, u32[]{:S(2)}) copy-start(bf16[180,540]{1,0:T(8,128)(2,1)} %param.26) | copy-start | bytes 583204
  7.2 553.0 %all-reduce.6.cloned.1.call-start = ((), (), s32[]{:S(2)}) async-start(), calls=%async_computation | async-start | bytes 5840896 | tf_op jit(solution)/shard_map/psum | solution.py:300
  9.2 8.4 %copy-start.15 = (bf16[1,16,256,180]{2,1,3,0:T(8,128)(2,1)S(1)}, bf16[1,16,256,180]{2,1,3,0:T(8,128)(2,1)}, u32[]{:S(2)}) copy-start(bf16[1,16,256,180]{2,1,3,0:T(8,128)(2,1)} %param.39) | copy-start | bytes 4423684
  9.2 8.3 %copy-start.31 = (f32[16,256]{1,0:T(8,128)}, f32[16,256]{1,0:T(8,128)S(1)}, u32[]{:S(2)}) copy-start(f32[16,256]{1,0:T(8,128)S(1)} %broadcast_multiply_fusion.1) | copy-start | bytes 49156
  12.7 11.9 %copy-start.20 = (bf16[1,16,256,180]{2,3,1,0:T(8,128)(2,1)}, bf16[1,16,256,180]{2,3,1,0:T(8,128)(2,1)S(1)}, u32[]{:S(2)}) copy-start(bf16[1,16,256,180]{2,3,1,0:T(8,128)(2,1)S(1)} %fusion.31) | copy-start | bytes 4423684
  13.5 12.1 %copy-start.72 = (f32[360]{0:T(512)S(1)}, f32[360]{0:T(512)}, u32[]{:S(2)}) copy-start(f32[360]{0:T(512)} %param.27) | copy-start | bytes 4324
  13.5 43.1 %collective-permute-start = (bf16[1,4,256,180]{2,3,1,0:T(8,128)(2,1)}, bf16[1,4,256,180]{2,3,1,0:T(8,128)(2,1)}, u32[]{:S(2)}, u32[]{:S(2)}) collective-permute-start(bf16[1,4,256,180]{2,3,1,0:T(8,128)(2,1)} %slice.231), channel_id=1, source_target_pairs={{0,28},{4,0},{8,4},{12,8},{16,12},{20,16},{24,20},{28,24},{1,29},{... | collective-permute-start | bytes 1105928 | tf_op jit(solution)/shard_map/ppermute | solution.py:15
  17.6 142.8 %copy-start.49 = (f32[256]{0:T(256)}, f32[256]{0:T(256)S(1)}, u32[]{:S(2)}) copy-start(f32[256]{0:T(256)S(1)} %compare_convert_fusion) | copy-start | bytes 3076
  17.6 9.2 %copy-start.79 = (f32[225,6]{0,1:T(8,128)S(1)}, f32[225,6]{0,1:T(8,128)}, u32[]{:S(2)}) copy-start(f32[225,6]{0,1:T(8,128)} %param.28) | copy-start | bytes 16204
  19.5 16.7 %collective-permute-start.5 = (bf16[1,1,256,180]{2,3,1,0:T(8,128)(2,1)}, bf16[1,1,256,180]{2,3,1,0:T(8,128)(2,1)S(1)}, u32[]{:S(2)}, u32[]{:S(2)}) collective-permute-start(bf16[1,1,256,180]{2,3,1,0:T(8,128)(2,1)} %get-tuple-element.137), channel_id=1, source_target_pairs={{4,0},{8,4},{12,8},{16,12},{20,16},{24,20},{28,24},{5,1},{9,5},{13... | collective-permute-start | bytes 276488 | tf_op jit(solution)/shard_map/ppermute | solution.py:26
  20.8 15.4 %collective-permute-start.4 = (bf16[1,1,256,180]{2,3,1,0:T(8,128)(2,1)}, bf16[1,1,256,180]{2,3,1,0:T(8,128)(2,1)}, u32[]{:S(2)}, u32[]{:S(2)}) collective-permute-start(bf16[1,1,256,180]{2,3,1,0:T(8,128)(2,1)} %get-tuple-element.138), channel_id=1, source_target_pairs={{0,4},{4,8},{8,12},{12,16},{16,20},{20,24},{24,28},{1,5},{5,9},{9,... | collective-permute-start | bytes 276488 | tf_op jit(solution)/shard_map/ppermute | solution.py:25
  39.5 14.8 %copy-start.5 = (bf16[1,18,258,180]{2,3,1,0:T(8,128)(2,1)}, bf16[1,18,258,180]{2,3,1,0:T(8,128)(2,1)S(1)}, u32[]{:S(2)}) copy-start(bf16[1,18,258,180]{2,3,1,0:T(8,128)(2,1)S(1)} %select_maximum_fusion) | copy-start | bytes 5015524
  160.2 10.7 %copy-start.25 = (f32[64,6,64]{2,1,0:T(8,128)S(1)}, f32[64,6,64]{2,1,0:T(8,128)}, u32[]{:S(2)}) copy-start(f32[64,6,64]{2,1,0:T(8,128)} %copy-done.24) | copy-start | bytes 294916
  160.2 10.7 %copy-start.29 = (f32[64,6,64]{2,1,0:T(8,128)S(1)}, f32[64,6,64]{2,1,0:T(8,128)}, u32[]{:S(2)}) copy-start(f32[64,6,64]{2,1,0:T(8,128)} %copy-done.28) | copy-start | bytes 294916
  160.3 10.7 %collective-permute-start.1 = (bf16[1,4,256,180]{2,3,1,0:T(8,128)(2,1)S(1)}, bf16[1,4,256,180]{2,3,1,0:T(8,128)(2,1)S(1)}, u32[]{:S(2)}, u32[]{:S(2)}) collective-permute-start(bf16[1,4,256,180]{2,3,1,0:T(8,128)(2,1)S(1)} %slice.239), channel_id=1, source_target_pairs={{0,4},{4,8},{8,12},{12,16},{16,20},{20,24},{24,28},{28,0},{1,5},{5... | collective-permute-start | bytes 1105928 | tf_op jit(solution)/shard_map/ppermute | solution.py:15
  170.8 43.7 %copy-start.7 = (f32[16,256,180]{1,2,0:T(8,128)}, f32[16,256,180]{1,2,0:T(8,128)S(1)}, u32[]{:S(2)}) copy-start(f32[16,256,180]{1,2,0:T(8,128)S(1)} %get-tuple-element.159) | copy-start | bytes 8847364
  178.3 15.4 %copy-start.46 = (bf16[360,180]{0,1:T(8,128)(2,1)S(1)}, bf16[360,180]{0,1:T(8,128)(2,1)}, u32[]{:S(2)}) copy-start(bf16[360,180]{0,1:T(8,128)(2,1)} %param.35) | copy-start | bytes 388804
  178.3 15.4 %copy-start.50 = (f32[256]{0:T(256)S(1)}, f32[256]{0:T(256)}, u32[]{:S(2)}) copy-start(f32[256]{0:T(256)} %copy-done.49) | copy-start | bytes 3076
  178.3 15.4 %copy-start.74 = (f32[180]{0:T(256)S(1)}, f32[180]{0:T(256)}, u32[]{:S(2)}) copy-start(f32[180]{0:T(256)} %param.36) | copy-start | bytes 2164
  208.7 13.8 %collective-permute-start.2 = (bf16[1,1,256,180]{2,3,1,0:T(8,128)(2,1)S(1)}, bf16[1,1,256,180]{2,3,1,0:T(8,128)(2,1)S(1)}, u32[]{:S(2)}, u32[]{:S(2)}) collective-permute-start(bf16[1,1,256,180]{2,3,1,0:T(8,128)(2,1)S(1)} %get-tuple-element.139), channel_id=1, source_target_pairs={{0,4},{4,8},{8,12},{12,16},{16,20},{20,24},{24,28},{1,5},{5,9},{9,... | collective-permute-start | bytes 276488 | tf_op jit(solution)/shard_map/ppermute | solution.py:25
  210.0 12.5 %collective-permute-start.3 = (bf16[1,1,256,180]{2,3,1,0:T(8,128)(2,1)S(1)}, bf16[1,1,256,180]{2,3,1,0:T(8,128)(2,1)S(1)}, u32[]{:S(2)}, u32[]{:S(2)}) collective-permute-start(bf16[1,1,256,180]{2,3,1,0:T(8,128)(2,1)S(1)} %get-tuple-element.140), channel_id=1, source_target_pairs={{4,0},{8,4},{12,8},{16,12},{20,16},{24,20},{28,24},{5,1},{9,5},{13... | collective-permute-start | bytes 276488 | tf_op jit(solution)/shard_map/ppermute | solution.py:26
  217.3 44.2 %collective-permute-start.6 = (bf16[1,4,256,180]{2,3,1,0:T(8,128)(2,1)S(1)}, bf16[1,4,256,180]{2,3,1,0:T(8,128)(2,1)S(1)}, u32[]{:S(2)}, u32[]{:S(2)}) collective-permute-start(bf16[1,4,256,180]{2,3,1,0:T(8,128)(2,1)S(1)} %slice.258), channel_id=1, source_target_pairs={{0,28},{4,0},{8,4},{12,8},{16,12},{20,16},{24,20},{28,24},{1,29},{... | collective-permute-start | bytes 1105928 | tf_op jit(solution)/shard_map/ppermute | solution.py:15
  304.8 10.7 %copy-start.13 = (bf16[64,64,6,30]{1,3,2,0:T(8,128)(2,1)S(1)}, bf16[64,64,6,30]{1,3,2,0:T(8,128)(2,1)}, u32[]{:S(2)}) copy-start(bf16[64,64,6,30]{1,3,2,0:T(8,128)(2,1)} %copy.266) | copy-start | bytes 4423684
  333.2 11.3 %copy-start.12 = (bf16[1,64,64,1,6,30]{2,1,5,4,3,0:T(8,128)(2,1)S(1)}, bf16[1,64,64,1,6,30]{2,1,5,4,3,0:T(8,128)(2,1)}, u32[]{:S(2)}) copy-start(bf16[1,64,64,1,6,30]{2,1,5,4,3,0:T(8,128)(2,1)} %get-tuple-element.135) | copy-start | bytes 4423684
  405.1 8.5 %copy-start.61 = (pred[256]{0:T(512)(128)(4,1)S(1)}, pred[256]{0:T(512)(128)(4,1)}, u32[]{:S(2)}) copy-start(pred[256]{0:T(512)(128)(4,1)} %get-tuple-element.162) | copy-start | bytes 772
  416.0 8.2 %collective-permute-start.7 = (bf16[1,4,256,180]{2,3,1,0:T(8,128)(2,1)}, bf16[1,4,256,180]{2,3,1,0:T(8,128)(2,1)}, u32[]{:S(2)}, u32[]{:S(2)}) collective-permute-start(bf16[1,4,256,180]{2,3,1,0:T(8,128)(2,1)} %slice.259), channel_id=1, source_target_pairs={{0,4},{4,8},{8,12},{12,16},{16,20},{20,24},{24,28},{28,0},{1,5},{5... | collective-permute-start | bytes 1105928 | tf_op jit(solution)/shard_map/ppermute | solution.py:15
  420.6 9.2 %copy-start.8 = (f32[16,256,180]{1,2,0:T(8,128)S(1)}, f32[16,256,180]{1,2,0:T(8,128)}, u32[]{:S(2)}) copy-start(f32[16,256,180]{1,2,0:T(8,128)} %copy-done.7) | copy-start | bytes 8847364
  420.6 9.2 %copy-start.10 = (bf16[16,256,180]{1,2,0:T(8,128)(2,1)S(1)}, bf16[16,256,180]{1,2,0:T(8,128)(2,1)}, u32[]{:S(2)}) copy-start(bf16[16,256,180]{1,2,0:T(8,128)(2,1)} %copy-done.9) | copy-start | bytes 4423684
  420.6 9.2 %copy-start.34 = (f32[16,256]{1,0:T(8,128)S(1)}, f32[16,256]{1,0:T(8,128)}, u32[]{:S(2)}) copy-start(f32[16,256]{1,0:T(8,128)} %copy-done.33) | copy-start | bytes 49156
  420.6 9.2 %copy-start.43 = (f32[16,256]{1,0:T(8,128)S(1)}, f32[16,256]{1,0:T(8,128)}, u32[]{:S(2)}) copy-start(f32[16,256]{1,0:T(8,128)} %copy-done.42) | copy-start | bytes 49156
  420.6 9.2 %copy-start.52 = (f32[256]{0:T(256)S(1)}, f32[256]{0:T(256)}, u32[]{:S(2)}) copy-start(f32[256]{0:T(256)} %copy-done.49) | copy-start | bytes 3076
  420.6 9.2 %copy-start.54 = (f32[180]{0:T(256)S(1)}, f32[180]{0:T(256)}, u32[]{:S(2)}) copy-start(f32[180]{0:T(256)} %param.31) | copy-start | bytes 2164
  (60 other events, 237.1 us)
Sparse Core Ops, SparseCore 0:
  419.2 140.9 all-reduce.5
where the time goes:
time: 581 us; the launch traced here: 575 us
  matrix products  170 us (29%)
  local copies, waits for them, and re-layouts  165 us (28%)
  waiting for transfers between devices  88.3 us (15%)
  other arithmetic  80.4 us (14%)
  blocking collectives  40.1 us (7%)
  between operations  16.3 us (3%)
  starting transfers between devices  15 us (3%)
    psum x1, waiting for transfers between devices, on_device(): lax.psum((norm1_gain_grad, norm1_bias_grad, qkv_weight_grad, qv_bias_grad...  84.7 us
    psum x1, blocking collectives, on_device(): lax.psum((norm1_gain_grad, norm1_bias_grad, qkv_weight_grad, qv_bias_grad...  40.1 us
    dot_general x9, matrix products, on_device(): jnp.einsum('brwo,co->brwc', cot_frame[:, 2 - row_tap:2 - row_tap + rows_h...  30.4 us
    convert_element_type x2, local copies, waits for them, and re-layouts, on_device(): projected_grad = jnp.stack([query_grad, key_grad, value_grad], axis=3).re...  26.5 us
    dot_general x9, matrix products, on_device(): jnp.einsum('brwc,co->brwo', framed[:, row_tap:row_tap + rows_here, col_ta...  21.6 us
    gather x8, local copies, waits for them, and re-layouts, move_columns(): jnp.take(plane, picks, axis=1)  21.1 us
    dot_general x1, matrix products, on_device(): jnp.einsum('bnihd,bnjhd->bnhij', mixed_grad, values, preferred_element_ty...  17.7 us
    unnamed x169, local copies, waits for them, and re-layouts  17.2 us
  transfers between devices with their start and end apart: 9, of which 2 were waited for; matrix products, arithmetic and copies ran while one was open for 18% of the time, Pallas kernels for 0%

commit v1 on v0

v1 whole, which is shorter than its diff:
```python
import functools

import jax
import jax.numpy as jnp
import numpy as np
from jax import lax
from jax.experimental import pallas as pl
from jax.experimental.pallas import tpu as pltpu
from jax.sharding import PartitionSpec as P

HEADS = 6
HEAD_DIM = 30
WIN = 8
SHIFT = 4
C = 180
CP = 256
HID = 360
HP = 384
AREA = WIN * WIN
HI = HEADS * AREA
LOG2E = 1.4426950408889634
SCALE = HEAD_DIM ** (-0.5)

f32 = jnp.float32
bf16 = jnp.bfloat16


def dot(a, b, ca=1, cb=0):
    return lax.dot_general(a, b, (((ca,), (cb,)), ((), ())), preferred_element_type=f32)


def lanes(shape):
    return lax.broadcasted_iota(jnp.int32, shape, len(shape) - 1)


def rows_of(shape):
    return lax.broadcasted_iota(jnp.int32, shape, len(shape) - 2)


def ln_fwd(x, gain, bias):
    real = (lanes((1, CP)) < C).astype(f32)
    mean = jnp.sum(x, axis=-1, keepdims=True) * (1.0 / C)
    xc = (x - mean) * real
    var = jnp.sum(xc * xc, axis=-1, keepdims=True) * (1.0 / C)
    rstd = lax.rsqrt(var + 1e-05)
    xhat = xc * rstd
    return xhat, rstd, xhat * gain + bias


def ln_bwd(dy, xhat, rstd, gain):
    a = dy * gain
    m1 = jnp.sum(a, axis=-1, keepdims=True) * (1.0 / C)
    m2 = jnp.sum(a * xhat, axis=-1, keepdims=True) * (1.0 / C)
    return rstd * (a - m1 - xhat * m2)


def gelu_pair(h):
    z = jnp.abs(h) * 0.7071067811865476
    d = 1.0 + 0.3275911 * z
    t = pl.reciprocal(d, approx=True)
    t = t * (2.0 - d * t)
    e = jnp.exp2(h * h * (-0.5 * LOG2E))
    poly = t * (
        0.254829592 + t * (-0.284496736 + t * (1.421413741 + t * (-1.453152027 + t * 1.061405429)))
    )
    q = 0.5 * poly * e
    phi = jnp.where(h >= 0, 1.0 - q, q)
    return h * phi, phi + h * (e * 0.3989422804014327)


def fold8(v):
    return jnp.sum(v.reshape(v.shape[0] // 8, 8, v.shape[1]), axis=0)


def head_mask(h):
    ln = lanes((1, CP))
    return (ln >= h * HEAD_DIM) & (ln < (h + 1) * HEAD_DIM)


def spread_heads(v):
    return jnp.concatenate(
        [jnp.where(head_mask(h), v, jnp.zeros_like(v)) for h in range(HEADS)], axis=0
    )


def gather_heads(v):
    out = jnp.where(head_mask(0), v[:AREA], 0.0)
    for h in range(1, HEADS):
        out = jnp.where(head_mask(h), v[h * AREA : (h + 1) * AREA], out)
    return out


def main_kernel(
    scal,
    img,
    img_nxt,
    cot,
    cot_nxt,
    wqkv,
    wproj,
    wfc1,
    wfc2,
    wconv,
    vecs,
    extra,
    ll_out,
    gcat,
    ig_out,
    d_qkv,
    d_proj,
    d_fc1,
    d_fc2,
    d_norm,
    d_rel,
    xrow,
    xhat1,
    rstd,
    normed,
    qkv,
    probs,
    mixed,
    xhat2,
    normed2,
    act,
    dgelu,
    winf,
    fgrad,
    do_buf,
    tmp,
):
    nb = scal[0]
    last = scal[1]
    width = nb * WIN
    NW = 256 // WIN
    RM = 256

    def vec(i, n):
        return vecs[i : i + 1, 0:n]

    xrow[:, :, 128:256] = jnp.zeros((16, 256, 128), f32)

    @pl.loop(0, 12)
    def _(r):
        xrow[r, :, 0:C] = img[r + 4].astype(f32)

    @pl.loop(0, 4)
    def _(r):
        xrow[12 + r, :, 0:C] = img_nxt[r].astype(f32)

    tmp[...] = jnp.zeros_like(tmp)
    col_in = rows_of((256, C)) < width

    def put_g(pos, row, flag):
        g = jnp.where(col_in, row.astype(f32), 0.0) * flag
        tmp[8:264, 0:C] = g
        base = pl.multiple_of(pos * 256, 256)
        gcat[pl.ds(base, 256), 0:CP] = tmp[9:265, :].astype(bf16)
        gcat[pl.ds(base, 256), CP : 2 * CP] = tmp[8:264, :].astype(bf16)
        gcat[pl.ds(base, 256), 2 * CP : 3 * CP] = tmp[7:263, :].astype(bf16)

    joined = jnp.where(last == 1, 0.0, 1.0)

    @pl.loop(0, 13)
    def _(r):
        put_g(r, cot[r + 3], 1.0)

    put_g(13, cot_nxt[0], joined)
    put_g(14, cot[15], joined)

    @pl.loop(0, 5)
    def _(r):
        put_g(15 + r, cot_nxt[r], 1.0)

    d_qkv[...] = jnp.zeros_like(d_qkv)
    d_proj[...] = jnp.zeros_like(d_proj)
    d_fc1[...] = jnp.zeros_like(d_fc1)
    d_fc2[...] = jnp.zeros_like(d_fc2)
    d_norm[...] = jnp.zeros_like(d_norm)
    d_rel[...] = jnp.zeros_like(d_rel)

    pos_hi = rows_of((1, WIN, CP)) >= SHIFT

    def rolled(a, b):
        t = jnp.where(pos_hi, a, b)
        return pltpu.roll(t, SHIFT, 1)

    def to_win(ref, band, k):
        nxt = jnp.where(k == nb - 1, 0, jnp.minimum(k + 1, NW - 1))
        rs = pl.ds(pl.multiple_of(band * WIN, WIN), WIN)
        a = ref[rs, pl.ds(pl.multiple_of(k * WIN, WIN), WIN), :]
        b = ref[rs, pl.ds(pl.multiple_of(nxt * WIN, WIN), WIN), :]
        return rolled(a, b).reshape(AREA, CP)

    def from_win(ref, band, k):
        prv = jnp.where(k == 0, nb - 1, k - 1)
        a = ref[pl.ds(pl.multiple_of((band * NW + prv) * AREA, AREA), AREA), :]
        b = ref[pl.ds(pl.multiple_of((band * NW + k) * AREA, AREA), AREA), :]
        return rolled(a.reshape(WIN, WIN, CP), b.reshape(WIN, WIN, CP))

    def win_rows(w):
        return pl.ds(pl.multiple_of(w * AREA, AREA), AREA)

    @pl.loop(0, 8)
    def _(g):
        band = lax.div(g, 4)
        k0 = lax.rem(g, 4) * 8

        @pl.loop(0, 8)
        def _(i):
            x = to_win(xrow, band, k0 + i)
            rs = win_rows(g * 8 + i)
            xhat, rs_, out = ln_fwd(x, vec(0, CP), vec(1, CP))
            winf[rs, :] = x
            xhat1[rs, :] = xhat
            rstd[rs, 0:1] = rs_
            normed[rs, :] = out.astype(bf16)

        gs = pl.ds(pl.multiple_of(g * 512, 512), 512)
        for n in range(3):
            sl = slice(n * CP, (n + 1) * CP)
            qkv[gs, sl] = (dot(normed[gs, :], wqkv[:, sl]) + vecs[2:3, sl]).astype(bf16)

        @pl.loop(0, 8)
        def _(i):
            rs = win_rows(g * 8 + i)
            kk = k0 + i
            q = qkv[rs, 0:CP]
            k = qkv[rs, CP : 2 * CP]
            v = qkv[rs, 2 * CP : 3 * CP]
            which = jnp.where((band == 1) & (last == 1), 2, 0) + jnp.where(kk == nb - 1, 1, 0)
            s = dot(k, spread_heads(q), 1, 1) * (SCALE * LOG2E) + extra[which]
            top = jnp.max(s, axis=0, keepdims=True)
            e = jnp.exp2(s - top)
            total = jnp.sum(e, axis=0, keepdims=True)
            p = (e * (1.0 / total)).astype(bf16)
            probs[rs, :] = p
            o = gather_heads(dot(p, v, 0, 0))
            o = jnp.where(lanes((1, CP)) == C, 1.0, o)
            mixed[rs, :] = o.astype(bf16)

        @pl.loop(0, 512 // RM)
        def _(j):
            rs = pl.ds(pl.multiple_of(g * 512 + j * RM, RM), RM)
            fs = dot(mixed[rs, :], wproj[...]) + vec(3, CP) + winf[rs, :]
            xhat, rs_, out = ln_fwd(fs, vec(4, CP), vec(5, CP))
            xhat2[rs, :] = xhat
            rstd[rs, 1:2] = rs_
            n2 = out.astype(bf16)
            normed2[rs, :] = n2
            hid = dot(n2, wfc1[...]) + vec(6, HP)
            ac, dg = gelu_pair(hid)
            ac = jnp.where(lanes((1, HP)) == HID, 1.0, ac).astype(bf16)
            act[rs, :] = ac
            dgelu[rs, :] = dg.astype(bf16)
            winf[rs, :] = fs + dot(ac, wfc2[...]) + vec(7, CP)

    @pl.loop(0, 64)
    def _(w):
        band = lax.div(w, NW)
        k = lax.rem(w, NW)
        xrow[pl.ds(pl.multiple_of(band * 8, 8), 8), pl.ds(pl.multiple_of(k * 8, 8), 8), :] = from_win(
            winf, band, k
        )

    col_in_p = rows_of((256, CP)) < width

    @pl.loop(0, 16)
    def _(r):
        ll_out[pl.ds(pl.multiple_of(r * 256, 256), 256), :] = jnp.where(
            col_in_p, xrow[r], 0.0
        ).astype(bf16)

    @pl.loop(0, 16)
    def _(r):
        pos = r + 1 + jnp.where(r >= 12, 2, 0)
        acc = None
        for a in range(3):
            d = dot(
                gcat[pl.ds(pl.multiple_of((pos + 1 - a) * 256, 256), 256), :], wconv[a], 1, 1
            )
            acc = d if acc is None else acc + d
        xrow[r] = jnp.where(col_in_p, acc, 0.0)

    @pl.loop(0, 8)
    def _(g):
        band = lax.div(g, 4)
        k0 = lax.rem(g, 4) * 8
        gs = pl.ds(pl.multiple_of(g * 512, 512), 512)

        @pl.loop(0, 8)
        def _(i):
            fgrad[win_rows(i), :] = to_win(xrow, band, k0 + i)

        @pl.loop(0, 512 // RM)
        def _(j):
            ls = pl.ds(pl.multiple_of(j * RM, RM), RM)
            rs = pl.ds(pl.multiple_of(g * 512 + j * RM, RM), RM)
            lg = fgrad[ls, :]
            mg = lg.astype(bf16)
            d_fc2[...] += dot(act[rs, :], mg, 0, 0)
            ag = dot(mg, wfc2[...], 1, 1).astype(bf16).astype(f32)
            hg = (ag * dgelu[rs, :].astype(f32)).astype(bf16)
            d_fc1[...] += dot(normed2[rs, :], hg, 0, 0)
            dn2 = dot(hg, wfc1[...], 1, 1).astype(bf16).astype(f32)
            xhat = xhat2[rs, :]
            d_norm[0:8, :] += fold8(dn2 * xhat)
            d_norm[8:16, :] += fold8(dn2)
            fg = lg + ln_bwd(dn2, xhat, rstd[rs, 1:2], vec(4, CP))
            fgrad[ls, :] = fg
            at = fg.astype(bf16)
            d_proj[...] += dot(mixed[rs, :], at, 0, 0)
            do_buf[ls, :] = dot(at, wproj[...], 1, 1).astype(bf16)

        @pl.loop(0, 8)
        def _(i):
            rs = win_rows(g * 8 + i)
            q = qkv[rs, 0:CP]
            k = qkv[rs, CP : 2 * CP]
            v = qkv[rs, 2 * CP : 3 * CP]
            dobd = spread_heads(do_buf[win_rows(i), :])
            dp = dot(v, dobd, 1, 1)
            pb = probs[rs, :]
            p = pb.astype(f32)
            ds = p * (dp - jnp.sum(p * dp, axis=0, keepdims=True))
            dsb = ds.astype(bf16)
            d_rel[...] += dsb.astype(f32)
            dv = dot(pb, dobd)
            dk = dot(dsb, spread_heads(q)) * SCALE
            dq = gather_heads(dot(dsb, k, 0, 0)) * SCALE
            qkv[rs, 0:CP] = dq.astype(bf16)
            qkv[rs, CP : 2 * CP] = dk.astype(bf16)
            qkv[rs, 2 * CP : 3 * CP] = dv.astype(bf16)

        d_qkv[...] += dot(normed[gs, :], qkv[gs, :], 0, 0)

        @pl.loop(0, 512 // RM)
        def _(j):
            ls = pl.ds(pl.multiple_of(j * RM, RM), RM)
            rs = pl.ds(pl.multiple_of(g * 512 + j * RM, RM), RM)
            dn1 = dot(qkv[rs, :], wqkv[...], 1, 1).astype(bf16).astype(f32)
            xhat = xhat1[rs, :]
            d_norm[16:24, :] += fold8(dn1 * xhat)
            d_norm[24:32, :] += fold8(dn1)
            winf[rs, :] = fgrad[ls, :] + ln_bwd(dn1, xhat, rstd[rs, 0:1], vec(0, CP))

    @pl.loop(0, 64)
    def _(w):
        band = lax.div(w, NW)
        k = lax.rem(w, NW)
        xrow[pl.ds(pl.multiple_of(band * 8, 8), 8), pl.ds(pl.multiple_of(k * 8, 8), 8), :] = from_win(
            winf, band, k
        )

    @pl.loop(0, 16)
    def _(r):
        pos = r + 1 + jnp.where(r >= 12, 2, 0)
        g = gcat[pl.ds(pl.multiple_of(pos * 256, 256), 256), CP : 2 * CP]
        v = jnp.where(col_in_p, xrow[r] + g.astype(f32), 0.0)
        ig_out[r] = v[:, 0:C].astype(bf16)


def conv_kernel(
    scal, ll, ll_top, ll_bot, gcat, img, img_nxt, wconv, vecs, res_out, d_conv, buf, tmp
):
    nb = scal[0]
    last = scal[1]
    width = nb * WIN
    joined = jnp.where(last == 1, 0.0, 1.0).astype(bf16)
    buf[0:256] = ll_top[...]
    buf[256 : 13 * 256] = ll[0 : 12 * 256]
    buf[13 * 256 : 14 * 256] = ll[12 * 256 : 13 * 256] * joined
    buf[14 * 256 : 15 * 256] = ll[11 * 256 : 12 * 256] * joined
    buf[15 * 256 : 19 * 256] = ll[12 * 256 : 16 * 256]
    buf[19 * 256 :] = ll_bot[...]
    d_conv[...] = jnp.zeros_like(d_conv)
    tmp[...] = jnp.zeros_like(tmp)
    col_in = rows_of((256, C)) < width

    @pl.loop(0, 4)
    def _(n):
        start = 1 + 4 * n + jnp.where(n == 3, 2, 0)
        gs = gcat[pl.ds(pl.multiple_of(start * 256, 256), 1024), :]
        for a in range(3):
            xs = buf[pl.ds(pl.multiple_of((start + a - 1) * 256, 256), 1024), :]
            d_conv[a] += dot(xs, gs, 0, 0)

    def out_row(r, source):
        pos = r + 1 + jnp.where(r >= 12, 2, 0)
        acc = None
        for a in range(3):
            d = dot(buf[pl.ds(pl.multiple_of((pos + a - 1) * 256, 256), 256), :], wconv[a])
            acc = d if acc is None else acc + d
        tmp[8:264, :] = acc[:, 0:CP]
        tmp[280:536, :] = acc[:, 2 * CP : 3 * CP]
        out = acc[:, CP : 2 * CP] + tmp[7:263, :] + tmp[281:537, :] + vecs[8:9, 0:CP]
        out = out[:, 0:C] + source.astype(f32)
        res_out[r] = jnp.where(col_in, out, 0.0).astype(bf16)

    @pl.loop(0, 12)
    def _(r):
        out_row(r, img[r + 4])

    @pl.loop(0, 4)
    def _(r):
        out_row(r + 12, img_nxt[r])


def relative_index():
    coords = np.arange(AREA)
    row, col = coords // WIN, coords % WIN
    return (row[:, None] - row[None, :] + WIN - 1) * (2 * WIN - 1) + col[:, None] - col[None, :] + WIN - 1


def score_extra(bias_table):
    hot = jnp.asarray(
        (relative_index().T.reshape(-1)[:, None] == np.arange(225)[None, :]).astype(np.float32)
    )
    rel = jnp.dot(hot, bias_table, precision=lax.Precision.HIGHEST)
    rel = rel.reshape(AREA, AREA, HEADS).transpose(0, 2, 1).reshape(AREA, HI)
    coords = np.arange(AREA)
    yh = coords // WIN >= SHIFT
    xh = coords % WIN >= SHIFT
    ydiff = yh[:, None] != yh[None, :]
    xdiff = xh[:, None] != xh[None, :]
    masks = np.stack([np.zeros_like(ydiff), xdiff, ydiff, ydiff | xdiff])
    masks = np.where(np.tile(masks, (1, 1, HEADS)), -100.0, 0.0).astype(np.float32)
    return (rel[None] + jnp.asarray(masks)) * LOG2E


def rel_to_table(d_rel):
    hot = jnp.asarray(
        (relative_index().T.reshape(-1)[:, None] == np.arange(225)[None, :]).astype(np.float32)
    )
    per = d_rel.reshape(AREA, HEADS, AREA).transpose(0, 2, 1).reshape(AREA * AREA, HEADS)
    return jnp.dot(hot.T, per, precision=lax.Precision.HIGHEST)


def ring(value, axis, steps):
    count = lax.axis_size(axis)
    pairs = [(source, (source + steps) % count) for source in range(count)]
    return lax.ppermute(value, axis, pairs)


VM = pl.BlockSpec(memory_space=pltpu.VMEM)
SM = pl.BlockSpec(memory_space=pltpu.SMEM)


def run_main(scal, img, img_nxt, cot, cot_nxt, wqkv, wproj, wfc1, wfc2, wconv, vecs, extra):
    S = jax.ShapeDtypeStruct
    return pl.pallas_call(
        main_kernel,
        out_shape=(
            S((4096, CP), bf16),
            S((20 * 256, 3 * CP), bf16),
            S((16, 256, C), bf16),
            S((CP, 3 * CP), f32),
            S((CP, CP), f32),
            S((CP, HP), f32),
            S((HP, CP), f32),
            S((32, CP), f32),
            S((AREA, HI), f32),
        ),
        in_specs=[SM] + [VM] * 11,
        out_specs=[VM] * 9,
        scratch_shapes=[
            pltpu.VMEM((16, 256, CP), f32),
            pltpu.VMEM((4096, CP), f32),
            pltpu.VMEM((4096, 2), f32),
            pltpu.VMEM((4096, CP), bf16),
            pltpu.VMEM((4096, 3 * CP), bf16),
            pltpu.VMEM((4096, HI), bf16),
            pltpu.VMEM((4096, CP), bf16),
            pltpu.VMEM((4096, CP), f32),
            pltpu.VMEM((4096, CP), bf16),
            pltpu.VMEM((4096, HP), bf16),
            pltpu.VMEM((4096, HP), bf16),
            pltpu.VMEM((4096, CP), f32),
            pltpu.VMEM((512, CP), f32),
            pltpu.VMEM((512, CP), bf16),
            pltpu.VMEM((272, CP), f32),
        ],
        compiler_params=pltpu.CompilerParams(vmem_limit_bytes=63 * 1024 * 1024),
        name="layer",
    )(scal, img, img_nxt, cot, cot_nxt, wqkv, wproj, wfc1, wfc2, wconv, vecs, extra)


def run_conv(scal, ll, ll_top, ll_bot, gcat, img, img_nxt, wconv, vecs):
    S = jax.ShapeDtypeStruct
    return pl.pallas_call(
        conv_kernel,
        out_shape=(S((16, 256, C), bf16), S((3, CP, 3 * CP), f32)),
        in_specs=[SM] + [VM] * 8,
        out_specs=[VM] * 2,
        scratch_shapes=[pltpu.VMEM((20 * 256, CP), bf16), pltpu.VMEM((544, CP), f32)],
        compiler_params=pltpu.CompilerParams(vmem_limit_bytes=60 * 1024 * 1024),
        name="conv",
    )(scal, ll, ll_top, ll_bot, gcat, img, img_nxt, wconv, vecs)


def prepare(norm1_gain, norm1_bias, qkv_weight, qv_bias, bias_table, proj_weight, proj_bias,
            norm2_gain, norm2_bias, fc1_weight, fc1_bias, fc2_weight, fc2_bias, conv_weight, conv_bias):
    pc = CP - C
    wqkv = jnp.pad(qkv_weight.reshape(C, 3, C), ((0, pc), (0, 0), (0, pc))).reshape(CP, 3 * CP)
    wproj = jnp.pad(proj_weight, ((0, pc), (0, pc)))
    wfc1 = jnp.pad(fc1_weight, ((0, pc), (0, HP - HID)))
    wfc2 = jnp.pad(fc2_weight, ((0, HP - HID), (0, pc)))
    wconv = jnp.pad(conv_weight.transpose(0, 2, 1, 3), ((0, 0), (0, pc), (0, 0), (0, pc)))
    wconv = wconv.reshape(3, CP, 3 * CP)

    def row(v, one=False):
        v = jnp.concatenate([v, jnp.ones((1,), f32)]) if one else v
        return jnp.pad(v, (0, 3 * CP - v.shape[0]))

    zero = jnp.zeros((C,), f32)
    qkvb = jnp.pad(jnp.stack([qv_bias[:C], zero, qv_bias[C:]]), ((0, 0), (0, pc))).reshape(-1)
    vecs = jnp.stack(
        [row(norm1_gain), row(norm1_bias, True), qkvb, row(proj_bias), row(norm2_gain),
         row(norm2_bias, True), row(fc1_bias), row(fc2_bias, True), row(conv_bias)]
        + [jnp.zeros((3 * CP,), f32)] * 7
    )
    return wqkv, wproj, wfc1, wfc2, wconv, vecs, score_extra(bias_table)


def on_device(
    images, widths, norm1_gain, norm1_bias, qkv_weight, qv_bias, bias_table, proj_weight, proj_bias,
    norm2_gain, norm2_bias, fc1_weight, fc1_bias, fc2_weight, fc2_bias, conv_weight, conv_bias, cotangent,
):
    count, rows_here, width, chans = images.shape
    stripes = lax.axis_size("rows")
    img = images.reshape(rows_here, width, chans)
    cot = cotangent.reshape(rows_here, width, chans)
    is_last = (lax.axis_index("rows") == stripes - 1).astype(jnp.int32)
    scal = jnp.stack([lax.div(widths[0], WIN), is_last])
    img_nxt = ring(img[:SHIFT], "rows", -1)
    cot_nxt = ring(cot[: SHIFT + 1], "rows", -1)
    wqkv, wproj, wfc1, wfc2, wconv, vecs, extra = prepare(
        norm1_gain, norm1_bias, qkv_weight, qv_bias, bias_table, proj_weight, proj_bias,
        norm2_gain, norm2_bias, fc1_weight, fc1_bias, fc2_weight, fc2_bias, conv_weight, conv_bias,
    )
    ll, gcat, ig, d_qkv, d_proj, d_fc1, d_fc2, d_norm, d_rel = run_main(
        scal, img, img_nxt, cot, cot_nxt, wqkv, wproj, wfc1, wfc2, wconv, vecs, extra
    )
    ll_bot = ring(ll[:256], "rows", -1)
    ll_top = ring(ll[15 * 256 :], "rows", 1)
    res, d_conv = run_conv(scal, ll, ll_top, ll_bot, gcat, img, img_nxt, wconv, vecs)

    def moved(rows):
        head = ring(rows[rows_here - SHIFT :], "rows", 1)
        return jnp.concatenate([head, rows[: rows_here - SHIFT]], axis=0)[None]

    norms = jnp.sum(d_norm.reshape(4, 8, CP), axis=1)[:, :C]
    dq = d_qkv[: C + 1].reshape(C + 1, 3, CP)[:, :, :C]
    local = (
        norms[2],
        norms[3],
        dq[:C].reshape(C, 3 * C),
        jnp.concatenate([dq[C, 0], dq[C, 2]]),
        rel_to_table(d_rel),
        d_proj[:C, :C],
        d_proj[C, :C],
        norms[0],
        norms[1],
        d_fc1[:C, :HID],
        d_fc1[C, :HID],
        d_fc2[:HID, :C],
        d_fc2[HID, :C],
        d_conv.reshape(3, CP, 3, CP)[:, :C, :, :C].transpose(0, 2, 1, 3),
        d_conv[1, C, CP : CP + C],
    )
    summed = lax.psum(local, ("rows", "imgs"))
    return (moved(res), moved(ig)) + tuple(summed)


def solution(mesh):
    big = P("imgs", "rows", None, None)
    in_specs = (big, P("imgs")) + (P(),) * 15 + (big,)
    out_specs = (big, big) + (P(),) * 15
    return jax.shard_map(
        on_device, mesh=mesh, in_specs=in_specs, out_specs=out_specs, check_vma=False
    )
```

time: 581 us -> 378 us (0.65)
  Pallas kernels: 0 us -> 166 us
  matrix products: 170 us -> 10.2 us
  local copies, waits for them, and re-layouts: 165 us -> 51.4 us
  other arithmetic: 80.4 us -> 5.47 us
  starting transfers between devices: 15 us -> 5.93 us
  waiting for transfers between devices: 88.3 us -> 81 us
    pallas_call x0 -> x2, Pallas kernels: none -> 166 us  [the longest x1 145 us: run_main(): pl.pallas_call(main_kernel, out_shape=(S((4096, CP), bf16), S((20 * 256,...]
    dot_general x47 -> x2, matrix products: 170 us -> 10.2 us  [the longest x1 5.82 us: score_extra(): rel = jnp.dot(hot, bias_table, precision=lax.Precision.HIGHEST)]
    convert_element_type x5 -> x0, local copies, waits for them, and re-layouts: 51.9 us -> none  [the longest x2 26.5 us: on_device(): projected_grad = jnp.stack([query_grad, key_grad, value_grad], axis=3).re...]
    reduce_sum x12 -> x1, other arithmetic: 38.3 us -> 0.02 us  [on_device(): norms = jnp.sum(d_norm.reshape(4, 8, CP), axis=1)[:, :C]]
    transpose x4 -> x2, local copies, waits for them, and re-layouts: 28.7 us -> 1.39 us  [the longest x1 1.35 us: on_device(): d_conv.reshape(3, CP, 3, CP)[:, :C, :, :C].transpose(0, 2, 1, 3)]
    gather x8 -> x0, local copies, waits for them, and re-layouts: 21.1 us -> none  [move_columns(): jnp.take(plane, picks, axis=1)]
    convert_element_type x4 -> x0, other arithmetic: 20.2 us -> none  [the longest x1 15.4 us: on_device(): act_low = activated.astype(bf16)]
    another operation x2 -> x13, local copies, waits for them, and re-layouts: 16.1 us -> 1.39 us  [the longest x12 1.32 us: prepare(): jnp.stack([row(norm1_gain), row(norm1_bias, True), qkvb, row(proj_bias),...]
  transfers between devices with their start and end apart: 9 -> 7, of which waited for: 2 -> 1; matrix products, arithmetic and copies ran while one was open for 18% -> 14% of each run, Pallas kernels for 0% -> 6%
where the time goes in v1:
time: 378 us; the launch traced here: 377 us
  Pallas kernels  166 us (44%)
  waiting for transfers between devices  81 us (21%)
  local copies, waits for them, and re-layouts  51.4 us (14%)
  blocking collectives  42.3 us (11%)
  between operations  15.3 us (4%)
  matrix products  10.2 us (3%)
  starting transfers between devices  5.93 us (2%)
  other arithmetic  5.47 us (1%)
    pallas_call x1, Pallas kernels, run_main(): pl.pallas_call(main_kernel, out_shape=(S((4096, CP), bf16), S((20 * 256,...  145 us
    psum x1, waiting for transfers between devices, on_device(): summed = lax.psum(local, ('rows', 'imgs'))  80.9 us
    psum x1, blocking collectives, on_device(): summed = lax.psum(local, ('rows', 'imgs'))  42.3 us
    unnamed x75, local copies, waits for them, and re-layouts  24.2 us
    pallas_call x1, Pallas kernels, run_conv(): pl.pallas_call(conv_kernel, out_shape=(S((16, 256, C), bf16), S((3, CP, 3...  21.2 us
  transfers between devices with their start and end apart: 7, of which 1 were waited for; matrix products, arithmetic and copies ran while one was open for 14% of the time, Pallas kernels for 6%

profile of v1, /device:TPU:0, one launch (start us, length us, event | category | flops | bytes accessed | tf_op | source)
XLA Modules:
  0.0 377.4 jit_solution(4461309922473204005)
XLA Ops:
  7.2 1.2 slice.95
  9.3 3.3 collective-permute-start.1
  12.6 2.8 copy.68
  15.4 0.9 slice_bitcast_fusion.1
  17.3 5.8 %fusion.4 = f32[4096,6]{0,1:T(8,128)S(1)} fusion(f32[4096,225]{1,0:T(8,128)} %constant.31.clone, f32[225,6]{0,1:T(8,128)S(1)} %copy-done), kind=kOutput, calls=%fused_computation.20 | convolution fusion | flops 66355200 | bytes 3790104 | tf_op jit(solution)/shard_map/dot_general | solution.py:418
  23.4 4.2 %copy.70 = bf16[1,16,256,180]{3,2,1,0:T(8,128)(2,1)} copy(bf16[1,16,256,180]{2,1,3,0:T(8,128)(2,1)} %param.38) | data formatting | bytes 2949120 | tf_op args[17]
  31.4 0.9 copy.77.wqkv
  32.3 1.6 copy.74
  34.1 1.5 copy.78.wconv
  35.7 1.3 stack.71.vecs
  38.3 2.1 copy.76.cot_nxt
  41.2 144.7 %layer.1 = (bf16[4096,256]{1,0:T(8,128)(2,1)}, bf16[5120,768]{1,0:T(8,128)(2,1)}, bf16[16,256,180]{2,1,0:T(8,128)(2,1)}, f32[256,768]{1,0:T(8,128)}, f32[256,256...) custom-call(s32[2]{0:T(128)} %pad_add_fusion.scal, ...), custom_call_target="tpu_custom_call" | custom-call | tf_op jit(solution)/shard_map/layer/pallas_call | solution.py:450
  185.9 1.7 fusion
  188.1 1.1 slice.107
  192.7 1.1 slice.103
  193.8 1.3 collective-permute-start.5
  195.5 1.0 copy.88
  197.2 21.2 %conv.1 = (bf16[16,256,180]{2,1,0:T(8,128)(2,1)}, f32[3,256,768]{2,1,0:T(8,128)}) custom-call(s32[2]{0:T(128)} %pad_add_fusion.scal, bf16[4096,256]{1,0:T(8,128)(2,1)} %get-tuple-element.28.ll, bf16[256,256]{1,0:T(8,128)(2,1)} %copy-done.16, bf16[256,256]{1,0:T(8,128)(2,1)} %copy-done.15, bf16[5120,768]{1,0:T(8,128)(2,1)} %get-tuple-element.29.gcat, ...), custom_call_target="tpu_custom_call" | custom-call | tf_op jit(solution)/shard_map/conv/pallas_call | solution.py:489
  218.4 2.0 copy.82
  220.5 1.3 slice_bitcast_fusion
  221.9 4.4 %fusion.5 = f32[225,6]{0,1:T(8,128)S(1)} fusion(f32[4096,225]{1,0:T(8,128)} %constant.31.clone, f32[4096,6]{0,1:T(8,128)S(1)} %reshape.83), kind=kOutput, calls=%fused_computation.21 | convolution fusion | flops 66355200 | bytes 3790104 | tf_op jit(solution)/shard_map/dot_general | solution.py:435
  227.2 1.3 slice.104
  229.4 1.3 slice.102
  230.7 42.3 %all-reduce.14 = (f32[180]{0:T(256)}, f32[180]{0:T(256)}, f32[360]{0:T(512)}, f32[225,6]{0,1:T(8,128)}, f32[180]{0:T(256)}, /*index=5*/f32[180]{0:T(256)}, f32[1...) all-reduce(f32[180]{0:T(256)S(1)} %bitcast.73, ...), channel_id=1, replica_groups=mesh['rows'=8,'imgs'=4] {'rows','imgs'}, use_global_device_ids=true, to_apply=%region_1.2 | all-reduce | flops 3330 | bytes 26640 | tf_op jit(solution)/shard_map/psum | solution.py:570
  273.0 1.9 maximum_bitcast_fusion.1
  274.9 2.4 copy.84
  277.3 1.9 maximum_bitcast_fusion
  279.2 2.4 copy.83
  281.6 80.9 %all-reduce.18.cloned.1.call-done = (f32[180,540]{0,1:T(8,128)}, f32[180,180]{1,0:T(8,128)}, f32[180,360]{1,0:T(8,128)}, f32[360,180]{1,0:T(8,128)}, f32[3,3,180,180]{2,3,1,0:T(8,128)}) async-done(((f32[180,540]{0,1:T(8,128)}, f32[180,180]{1,0:T(8,128)}, f32[180,360]{1,0:T(8,128)}, f32[360,180]{1,0:T(8,128)}, f32[3,3,180,180]{2,3,1,0:T(8,128)}), (f32[180,540]{0,1:T(8,128)}, f32[180,180]{1,0:T(8,128)}, ...) | async-done | bytes 2203216 | tf_op jit(solution)/shard_map/psum | solution.py:570
  362.5 2.0 copy.85
  364.6 1.9 copy.86
  366.5 2.7 copy.87
  (132 shorter events, 15.4 us)
Async XLA Ops:
  7.2 10.1 %copy-start = (f32[225,6]{0,1:T(8,128)S(1)}, f32[225,6]{0,1:T(8,128)}, u32[]{:S(2)}) copy-start(f32[225,6]{0,1:T(8,128)} %param.27) | copy-start | bytes 16204
  7.2 355.3 %all-reduce.18.cloned.1.call-start = ((), (), s32[]{:S(2)}) async-start(), calls=%async_computation | async-start | bytes 6184960 | tf_op jit(solution)/shard_map/psum | solution.py:570
  9.3 7.8 %copy-start.21 = (f32[360]{0:T(512)S(1)}, f32[360]{0:T(512)}, u32[]{:S(2)}) copy-start(f32[360]{0:T(512)} %param.26) | copy-start | bytes 4324
  9.3 29.0 %collective-permute-start.1 = (bf16[5,256,180]{1,2,0:T(8,128)(2,1)}, bf16[5,256,180]{1,2,0:T(8,128)(2,1)}, u32[]{:S(2)}, u32[]{:S(2)}) collective-permute-start(bf16[5,256,180]{1,2,0:T(8,128)(2,1)} %bitcast.50), channel_id=1, source_target_pairs={{0,28},{4,0},{8,4},{12,8},{16,12},{20,16},{24,20},{28,24},{1,29},{... | collective-permute-start | bytes 1382408 | tf_op jit(solution)/shard_map/ppermute | solution.py:441
  15.4 7.7 %copy-start.2 = (bf16[1,16,256,180]{3,2,1,0:T(8,128)(2,1)}, bf16[1,16,256,180]{3,2,1,0:T(8,128)(2,1)S(1)}, u32[]{:S(2)}) copy-start(bf16[1,16,256,180]{3,2,1,0:T(8,128)(2,1)S(1)} %copy.68) | copy-start | bytes 4423684
  16.4 24.0 %collective-permute-start = (bf16[4,256,180]{2,1,0:T(8,128)(2,1)}, bf16[4,256,180]{2,1,0:T(8,128)(2,1)S(1)}, u32[]{:S(2)}, u32[]{:S(2)}) collective-permute-start(bf16[4,256,180]{2,1,0:T(8,128)(2,1)} %slice_bitcast_fusion.1), channel_id=1, source_target_pairs={{0,28},{4,0},{8,4},{12,8},{16,12},{20,16},{24,20},{28,24},{1,29},{... | collective-permute-start | bytes 1105928 | tf_op jit(solution)/shard_map/ppermute | solution.py:441
  17.3 5.9 %copy-start.24 = (f32[180]{0:T(256)S(1)}, f32[180]{0:T(256)}, u32[]{:S(2)}) copy-start(f32[180]{0:T(256)} %param.35) | copy-start | bytes 2164
  17.3 5.9 %copy-start.25 = (f32[180]{0:T(256)S(1)}, f32[180]{0:T(256)}, u32[]{:S(2)}) copy-start(f32[180]{0:T(256)} %param.31) | copy-start | bytes 2164
  17.3 6.0 %copy-start.23 = (f32[180]{0:T(256)S(1)}, f32[180]{0:T(256)}, u32[]{:S(2)}) copy-start(f32[180]{0:T(256)} %param.24) | copy-start | bytes 2164
  23.2 5.2 %copy-start.26 = (f32[180]{0:T(256)S(1)}, f32[180]{0:T(256)}, u32[]{:S(2)}) copy-start(f32[180]{0:T(256)} %param.23) | copy-start | bytes 2164
  23.2 5.2 %copy-start.27 = (f32[180]{0:T(256)S(1)}, f32[180]{0:T(256)}, u32[]{:S(2)}) copy-start(f32[180]{0:T(256)} %param.29) | copy-start | bytes 2164
  23.2 5.3 %copy-start.28 = (f32[180]{0:T(256)S(1)}, f32[180]{0:T(256)}, u32[]{:S(2)}) copy-start(f32[180]{0:T(256)} %param.30) | copy-start | bytes 2164
  23.2 5.3 %copy-start.22 = (f32[360]{0:T(512)S(1)}, f32[360]{0:T(512)}, u32[]{:S(2)}) copy-start(f32[360]{0:T(512)} %param.33) | copy-start | bytes 4324
  23.2 5.3 %copy-start.29 = (f32[180]{0:T(256)S(1)}, f32[180]{0:T(256)}, u32[]{:S(2)}) copy-start(f32[180]{0:T(256)} %param.37) | copy-start | bytes 2164
  23.4 5.5 %copy-start.12 = (bf16[360,180]{0,1:T(8,128)(2,1)S(1)}, bf16[360,180]{0,1:T(8,128)(2,1)}, u32[]{:S(2)}) copy-start(bf16[360,180]{0,1:T(8,128)(2,1)} %param.34) | copy-start | bytes 388804
  23.4 5.6 %copy-start.18 = (bf16[180,180]{1,0:T(8,128)(2,1)S(1)}, bf16[180,180]{1,0:T(8,128)(2,1)}, u32[]{:S(2)}) copy-start(bf16[180,180]{1,0:T(8,128)(2,1)} %param.28) | copy-start | bytes 194404
  23.4 7.0 %copy-start.13 = (bf16[180,360]{1,0:T(8,128)(2,1)S(1)}, bf16[180,360]{1,0:T(8,128)(2,1)}, u32[]{:S(2)}) copy-start(bf16[180,360]{1,0:T(8,128)(2,1)} %param.32) | copy-start | bytes 388804
  27.6 3.5 copy-start.9
  33.9 3.6 copy-start.6
  185.9 4.4 %copy-start.14 = (f32[256,256]{1,0:T(8,128)S(1)}, f32[256,256]{1,0:T(8,128)}, u32[]{:S(2)}) copy-start(f32[256,256]{1,0:T(8,128)} %get-tuple-element.35) | copy-start | bytes 786436
  187.6 8.9 %collective-permute-start.3 = (bf16[256,256]{1,0:T(8,128)(2,1)}, bf16[256,256]{1,0:T(8,128)(2,1)S(1)}, u32[]{:S(2)}, u32[]{:S(2)}) collective-permute-start(bf16[256,256]{1,0:T(8,128)(2,1)} %get-tuple-element.105), channel_id=1, source_target_pairs={{0,28},{4,0},{8,4},{12,8},{16,12},{20,16},{24,20},{28,24},{1,29},{... | collective-permute-start | bytes 393224 | tf_op jit(solution)/shard_map/ppermute | solution.py:441
  187.6 8.9 %collective-permute-start.2 = (bf16[256,256]{1,0:T(8,128)(2,1)}, bf16[256,256]{1,0:T(8,128)(2,1)S(1)}, u32[]{:S(2)}, u32[]{:S(2)}) collective-permute-start(bf16[256,256]{1,0:T(8,128)(2,1)} %get-tuple-element.106), channel_id=1, source_target_pairs={{0,4},{4,8},{8,12},{12,16},{16,20},{20,24},{24,28},{28,0},{1,5},{5... | collective-permute-start | bytes 393224 | tf_op jit(solution)/shard_map/ppermute | solution.py:441
  188.1 2.9 copy-start.7
  189.2 2.5 copy-start.10
  189.3 3.2 copy-start.17
  193.8 79.2 %collective-permute-start.5 = (bf16[4,256,180]{2,1,0:T(8,128)(2,1)S(1)}, bf16[4,256,180]{2,1,0:T(8,128)(2,1)}, u32[]{:S(2)}, u32[]{:S(2)}) collective-permute-start(bf16[4,256,180]{2,1,0:T(8,128)(2,1)S(1)} %slice.103), channel_id=1, source_target_pairs={{0,4},{4,8},{8,12},{12,16},{16,20},{20,24},{24,28},{28,0},{1,5},{5... | collective-permute-start | bytes 1105928 | tf_op jit(solution)/shard_map/ppermute | solution.py:441
  221.9 4.4 %copy-start.20 = (f32[1,1,180]{2,1,0:T(1,128)S(1)}, f32[1,1,180]{2,1,0:T(1,128)}, u32[]{:S(2)}) copy-start(f32[1,1,180]{2,1,0:T(1,128)} %get-tuple-element.108) | copy-start | bytes 2164
  221.9 5.3 %copy-start.4 = (bf16[16,256,180]{2,1,0:T(8,128)(2,1)S(1)}, bf16[16,256,180]{2,1,0:T(8,128)(2,1)}, u32[]{:S(2)}) copy-start(bf16[16,256,180]{2,1,0:T(8,128)(2,1)} %get-tuple-element.31) | copy-start | bytes 4423684
  228.6 48.7 %collective-permute-start.4 = (bf16[4,256,180]{2,1,0:T(8,128)(2,1)S(1)}, bf16[4,256,180]{2,1,0:T(8,128)(2,1)}, u32[]{:S(2)}, u32[]{:S(2)}) collective-permute-start(bf16[4,256,180]{2,1,0:T(8,128)(2,1)S(1)} %slice.101), channel_id=1, source_target_pairs={{0,4},{4,8},{8,12},{12,16},{16,20},{20,24},{24,28},{28,0},{1,5},{5... | collective-permute-start | bytes 1105928 | tf_op jit(solution)/shard_map/ppermute | solution.py:441
  364.6 4.6 %copy-start.11 = (f32[180,180]{1,0:T(8,128)S(1)}, f32[180,180]{1,0:T(8,128)}, u32[]{:S(2)}) copy-start(f32[180,180]{1,0:T(8,128)} %get-tuple-element.124) | copy-start | bytes 388804
  364.6 5.3 %copy-start.8 = (f32[180,360]{1,0:T(8,128)S(1)}, f32[180,360]{1,0:T(8,128)}, u32[]{:S(2)}) copy-start(f32[180,360]{1,0:T(8,128)} %get-tuple-element.128) | copy-start | bytes 777604
  366.5 4.1 %copy-start.1 = (f32[225,6]{0,1:T(8,128)S(1)}, f32[225,6]{0,1:T(8,128)}, u32[]{:S(2)}) copy-start(f32[225,6]{0,1:T(8,128)} %param.27) | copy-start | bytes 16204
  (5 other events, 6.7 us)
Sparse Core Ops, SparseCore 0:
  222.0 140.5 all-reduce.17

commit v2 on v1

v2 whole, which is shorter than its diff:
```python
import functools

import jax
import jax.numpy as jnp
import numpy as np
from jax import lax
from jax.experimental import pallas as pl
from jax.experimental.pallas import tpu as pltpu
from jax.sharding import PartitionSpec as P

HEADS = 6
HEAD_DIM = 30
WIN = 8
SHIFT = 4
C = 180
CP = 256
HID = 360
HP = 384
AREA = WIN * WIN
HI = HEADS * AREA
LOG2E = 1.4426950408889634
SCALE = HEAD_DIM ** (-0.5)

CR = 192
FC2_ROWS = 368
A1_FC1 = 9 * CR
A1_FC2 = A1_FC1 + 2 * CR
A1_PROJ = A1_FC2 + FC2_ROWS
A1_USED = A1_PROJ + CR
A2_SMALL = 3 * CR
A2_USED = A2_SMALL + 16

f32 = jnp.float32
bf16 = jnp.bfloat16


def dot(a, b, ca=1, cb=0):
    return lax.dot_general(a, b, (((ca,), (cb,)), ((), ())), preferred_element_type=f32)


def lanes(shape):
    return lax.broadcasted_iota(jnp.int32, shape, len(shape) - 1)


def rows_of(shape):
    return lax.broadcasted_iota(jnp.int32, shape, len(shape) - 2)


def ln_fwd(x, gain, bias):
    real = (lanes((1, CP)) < C).astype(f32)
    mean = jnp.sum(x, axis=-1, keepdims=True) * (1.0 / C)
    xc = (x - mean) * real
    var = jnp.sum(xc * xc, axis=-1, keepdims=True) * (1.0 / C)
    rstd = lax.rsqrt(var + 1e-05)
    xhat = xc * rstd
    return xhat, rstd, xhat * gain + bias


def with_rstd(xhat, rstd):
    high = rstd.astype(bf16).astype(f32)
    lane = lanes((1, CP))
    return jnp.where(lane == 200, high, jnp.where(lane == 201, rstd - high, xhat))


def ln_bwd(dy, xhat, rstd, gain):
    a = dy * gain
    m1 = jnp.sum(a, axis=-1, keepdims=True) * (1.0 / C)
    m2 = jnp.sum(a * xhat, axis=-1, keepdims=True) * (1.0 / C)
    return rstd * (a - m1 - xhat * m2)


def gelu_pair(h):
    z = jnp.abs(h) * 0.7071067811865476
    d = 1.0 + 0.3275911 * z
    t = pl.reciprocal(d, approx=True)
    t = t * (2.0 - d * t)
    e = jnp.exp2(h * h * (-0.5 * LOG2E))
    poly = t * (
        0.254829592 + t * (-0.284496736 + t * (1.421413741 + t * (-1.453152027 + t * 1.061405429)))
    )
    q = 0.5 * poly * e
    phi = jnp.where(h >= 0, 1.0 - q, q)
    return h * phi, phi + h * (e * 0.3989422804014327)


def fold8(v):
    return jnp.sum(v.reshape(v.shape[0] // 8, 8, v.shape[1]), axis=0)


def head_mask(h):
    ln = lanes((1, CP))
    return (ln >= h * HEAD_DIM) & (ln < (h + 1) * HEAD_DIM)


def spread_heads(v):
    return jnp.concatenate(
        [jnp.where(head_mask(h), v, jnp.zeros_like(v)) for h in range(HEADS)], axis=0
    )


def gather_heads(v):
    out = jnp.where(head_mask(0), v[:AREA], 0.0)
    for h in range(1, HEADS):
        out = jnp.where(head_mask(h), v[h * AREA : (h + 1) * AREA], out)
    return out


def column_masks(width):
    return rows_of((256, CP)) < width


class AllReduce:
    def __init__(self, buf, out, r1, r2, r3, ssem, rsem, pr, chips, imgs, zsplit):
        self.buf, self.out, self.r1, self.r2, self.r3 = buf, out, r1, r2, r3
        self.ssem, self.rsem, self.chips, self.imgs = ssem, rsem, chips, imgs
        self.zsplit = zsplit
        rows = lax.axis_index("rows")
        self.core = lax.rem(rows, 2)
        self.chip = lax.div(rows, 2)
        self.z = lax.axis_index("imgs")
        self.piece = pr
        self.group = pr * imgs if zsplit else pr
        self.half = self.group * chips
        self.used = 0

    def copy(self, src, dst, device, n):
        return pltpu.make_async_remote_copy(
            src_ref=src,
            dst_ref=dst,
            send_sem=self.ssem.at[n],
            recv_sem=self.rsem.at[n],
            device_id=device,
            device_id_type=pl.DeviceIdType.MESH,
        )

    def rows(self, ref, start, size):
        return ref.at[pl.ds(pl.multiple_of(start, 16), size)]

    def base_half(self, core):
        return core * self.half

    def base_group(self, chip):
        return self.core * self.half + chip * self.group

    def base_piece(self, z):
        return self.base_group(self.chip) + (z * self.piece if self.zsplit else 0)

    def core_copy(self, ref, dst, n, gather):
        side = self.core if gather else 1 - self.core
        src = self.rows(ref, self.base_half(side), self.half)
        dst = src if dst is None else dst
        return [self.copy(src, dst, {"rows": self.chip * 2 + 1 - self.core}, n)]

    def chip_copies(self, ref, dst, n, gather):
        out = []
        for d in range(1, self.chips):
            to = lax.rem(self.chip + d, self.chips)
            src = self.rows(ref, self.base_group(self.chip if gather else to), self.group)
            to_ref = src if gather else dst.at[pl.ds((d - 1) * self.group, self.group)]
            out.append(self.copy(src, to_ref, {"rows": to * 2 + self.core}, n + d - 1))
        return out

    def img_copies(self, ref, dst, n, gather):
        out = []
        for d in range(1, self.imgs):
            to = lax.rem(self.z + d, self.imgs)
            src = self.rows(ref, self.base_piece(self.z if gather else to), self.piece)
            to_ref = src if gather else dst.at[pl.ds((d - 1) * self.piece, self.piece)]
            out.append(self.copy(src, to_ref, {"imgs": to}, n + d - 1))
        return out

    def start(self, copies):
        for c in copies:
            c.start()
        return copies

    def wait(self, copies):
        for c in copies:
            c.wait()

    def add(self, base, size, extra, count, stride, target):
        step = min(size, 64)
        while size % step:
            step -= 16

        @pl.loop(0, size // step)
        def _(i):
            at = pl.ds(pl.multiple_of(base + i * step, 16), step)
            total = self.buf[at, :].astype(f32)
            for d in range(count):
                total += extra[pl.ds(pl.multiple_of(d * stride + i * step, 16), step), :].astype(f32)
            target[at, :] = total.astype(bf16)

    def step(self, k):
        n2 = 1
        n3 = n2 + self.chips - 1
        n4 = n3 + self.imgs - 1
        n5 = n4 + self.imgs - 1
        n6 = n5 + self.chips - 1
        first = lambda: self.core_copy(self.buf, self.r1, 0, False)
        second = lambda: self.chip_copies(self.buf, self.r2, n2, False)
        third = lambda: self.img_copies(self.buf, self.r3, n3, False)
        fourth = lambda: self.img_copies(self.out, None, n4, True) if self.zsplit else []
        fifth = lambda: self.chip_copies(self.out, None, n5, True)
        sixth = lambda: self.core_copy(self.out, None, n6, True)
        if k == 0:
            self.start(first())
        elif k == 1:
            self.wait(first())
            self.add(self.base_half(self.core), self.half, self.r1, 1, 0, self.buf)
            self.start(second())
        elif k == 2:
            self.wait(second())
            self.add(
                self.base_group(self.chip), self.group, self.r2, self.chips - 1, self.group, self.buf
            )
            self.start(third())
        elif k == 3:
            self.wait(third())
            self.add(
                self.base_piece(self.z), self.piece, self.r3, self.imgs - 1, self.piece, self.out
            )
            self.start(fourth() if self.zsplit else fifth())
        elif k == 4:
            if self.zsplit:
                self.wait(fourth())
                self.start(fifth())
        elif k == 5:
            self.wait(fifth())
            self.start(sixth())
        elif k == 6:
            self.wait(sixth())


def all_reduce_sems(chips, imgs):
    return 2 * (1 + chips - 1 + imgs - 1)


def layer_kernel(
    chips,
    imgs,
    piece1,
    piece2,
    scal,
    img,
    cot,
    wqkv,
    wproj,
    wfc1,
    wfc2,
    wconv,
    vecs,
    extra,
    res_out,
    ig_out,
    o_qkv,
    o_proj,
    o_fc1,
    o_fc2,
    o_conv,
    o_vec,
    d_qkv,
    d_proj,
    d_fc1,
    d_fc2,
    d_conv,
    d_norm,
    d_rel,
    io1,
    io2,
    xband,
    gband,
    gcat,
    llbuf,
    xhat1,
    normed,
    qkv,
    probs,
    mixed,
    xhat2,
    normed2,
    act,
    dgelu,
    winf,
    fgrad,
    do_buf,
    edge,
    tmp,
    a1_buf,
    a1_out,
    a1_r1,
    a1_r2,
    a1_r3,
    a2_buf,
    a2_out,
    a2_r1,
    a2_r2,
    a2_r3,
    lsem,
    hs,
    hr,
    a1_s,
    a1_r,
    a2_s,
    a2_r,
):
    stripes = 2 * chips
    rank = lax.axis_index("rows")
    core = lax.rem(rank, 2)
    up = lax.rem(rank + stripes - 1, stripes)
    down = lax.rem(rank + 1, stripes)
    ar1 = AllReduce(a1_buf, a1_out, a1_r1, a1_r2, a1_r3, a1_s, a1_r, piece1, chips, imgs, True)
    ar2 = AllReduce(a2_buf, a2_out, a2_r1, a2_r2, a2_r3, a2_s, a2_r, piece2, chips, imgs, False)

    barrier = pltpu.get_barrier_semaphore()
    peers = [{"rows": up}, {"rows": down}]
    peers += [{"rows": lax.rem(rank + 2 * d, stripes)} for d in range(1, chips)]
    peers += [{"imgs": lax.rem(ar1.z + d, imgs)} for d in range(1, imgs)]
    for peer in peers:
        pl.semaphore_signal(barrier, inc=1, device_id=peer, device_id_type=pl.DeviceIdType.MESH)
    pl.semaphore_wait(barrier, len(peers))

    def remote(src, dst, to, n):
        return pltpu.make_async_remote_copy(
            src_ref=src,
            dst_ref=dst,
            send_sem=hs.at[n],
            recv_sem=hr.at[n],
            device_id={"rows": to},
            device_id_type=pl.DeviceIdType.MESH,
        )

    send_img = remote(img.at[pl.ds(0, 4)], io2.at[pl.ds(16, 4)], up, 0)
    send_cot = remote(cot.at[pl.ds(0, 5)], io1.at[pl.ds(16, 5)], up, 1)
    send_cot.start()
    send_img.start()
    load_cot = pltpu.make_async_copy(cot, io1.at[pl.ds(0, 16)], lsem.at[0])
    load_img = pltpu.make_async_copy(img, io2.at[pl.ds(0, 16)], lsem.at[1])
    load_cot.start()
    load_img.start()

    nb = scal[0]
    width = nb * WIN
    is_last = rank == stripes - 1
    joined = jnp.where(is_last, 0.0, 1.0)
    NW = 256 // WIN
    RM = 256

    def vec(i, n):
        return vecs[i : i + 1, 0:n]

    def row_at(pos, count=1):
        return pl.ds(pl.multiple_of(pos * 256, 256), count * 256)

    xband[:, :, 128:256] = jnp.zeros((8, 256, 128), f32)
    tmp[...] = jnp.zeros_like(tmp)
    for ref in (d_qkv, d_proj, d_fc1, d_fc2, d_conv, d_norm, d_rel):
        ref[...] = jnp.zeros_like(ref)
    a1_buf[A1_USED:, :] = jnp.zeros((a1_buf.shape[0] - A1_USED, CP), bf16)
    a2_buf[A2_USED:, :] = jnp.zeros((a2_buf.shape[0] - A2_USED, CP), bf16)

    col_in = rows_of((256, C)) < width
    col_in_p = rows_of((256, CP)) < width

    def put_g(pos, row, flag):
        g = jnp.where(col_in, row.astype(f32), 0.0) * flag
        tmp[8:264, 0:C] = g
        at = row_at(pos)
        gcat[at, 0:CP] = tmp[9:265, :].astype(bf16)
        gcat[at, CP : 2 * CP] = tmp[8:264, :].astype(bf16)
        gcat[at, 2 * CP : 3 * CP] = tmp[7:263, :].astype(bf16)

    load_cot.wait()

    @pl.loop(0, 13)
    def _(r):
        put_g(r, io1[r + 3], 1.0)

    put_g(14, io1[15], joined)
    load_img.wait()

    pos_hi = rows_of((1, WIN, CP)) >= SHIFT

    def rolled(a, b):
        t = jnp.where(pos_hi, a, b)
        return pltpu.roll(t, SHIFT, 1)

    def to_win(ref, k):
        nxt = jnp.minimum(k + 1, NW - 1)
        a = ref[:, pl.ds(pl.multiple_of(k * WIN, WIN), WIN), :]
        b = ref[:, pl.ds(pl.multiple_of(nxt * WIN, WIN), WIN), :]
        b = jnp.where(k == nb - 1, ref[:, 0:WIN, :], b)
        return rolled(a, b).reshape(AREA, CP)

    def from_win(ref, band):
        def block(k):
            at = pl.multiple_of((band * NW + k) * AREA, AREA)
            return ref[pl.ds(at, AREA), :].reshape(WIN, WIN, CP)

        @pl.loop(0, NW, unroll=4)
        def _(k):
            b = block(k)
            edge[...] = jnp.where(k == nb - 1, b, edge[...])
            xband[:, pl.ds(pl.multiple_of(k * WIN, WIN), WIN), :] = rolled(
                block(jnp.maximum(k - 1, 0)), b
            )

        xband[:, 0:WIN, :] = rolled(edge[...], block(0))

    def win_rows(w):
        return pl.ds(pl.multiple_of(w * AREA, AREA), AREA)

    @pl.loop(0, 2)
    def _(band):
        @pl.when(band == 1)
        def _():
            send_cot.wait()
            send_img.wait()
            put_g(13, io1[16], joined)

            @pl.loop(0, 5)
            def _(r):
                put_g(15 + r, io1[16 + r], 1.0)

        @pl.loop(0, 8)
        def _(y):
            xband[y, :, 0:C] = io2[band * 8 + y + 4].astype(f32)

        @pl.loop(0, 8)
        def _(y):
            r = band * 8 + y
            pos = r + 1 + jnp.where(r >= 12, 2, 0)
            acc = None
            for a in range(3):
                d = dot(gcat[row_at(pos + 1 - a), :], wconv[a], 1, 1)
                acc = d if acc is None else acc + d
            gband[y] = jnp.where(col_in_p, acc, 0.0)

        @pl.loop(0, 4)
        def _(gg):
            g = band * 4 + gg
            k0 = gg * 8
            gs = pl.ds(pl.multiple_of(g * 512, 512), 512)

            @pl.loop(0, 8, unroll=4)
            def _(i):
                x = to_win(xband, k0 + i)
                rs = win_rows(g * 8 + i)
                xhat, rs_, out = ln_fwd(x, vec(0, CP), vec(1, CP))
                winf[rs, :] = x
                xhat1[rs, :] = with_rstd(xhat, rs_).astype(bf16)
                normed[rs, :] = out.astype(bf16)
                fgrad[rs, :] = to_win(gband, k0 + i)

            for n in range(3):
                sl = slice(n * CP, (n + 1) * CP)
                qkv[gs, sl] = (dot(normed[gs, :], wqkv[:, sl]) + vecs[2:3, sl]).astype(bf16)

            @pl.loop(0, 8, unroll=4)
            def _(i):
                rs = win_rows(g * 8 + i)
                kk = k0 + i
                q = qkv[rs, 0:CP]
                k = qkv[rs, CP : 2 * CP]
                v = qkv[rs, 2 * CP : 3 * CP]
                which = jnp.where((band == 1) & is_last, 2, 0)
                more = jnp.where(kk == nb - 1, extra[which + 1], extra[which])
                s = dot(k, spread_heads(q), 1, 1) * (SCALE * LOG2E) + more
                top = jnp.max(s, axis=0, keepdims=True)
                e = jnp.exp2(s - top)
                total = jnp.sum(e, axis=0, keepdims=True)
                p = (e * (1.0 / total)).astype(bf16)
                probs[rs, :] = p
                o = gather_heads(dot(p, v, 0, 0))
                o = jnp.where(lanes((1, CP)) == C, 1.0, o)
                mixed[win_rows(i), :] = o.astype(bf16)

            @pl.loop(0, 512 // RM)
            def _(j):
                ls = pl.ds(pl.multiple_of(j * RM, RM), RM)
                rs = pl.ds(pl.multiple_of(g * 512 + j * RM, RM), RM)
                fs = dot(mixed[ls, :], wproj[...]) + vec(3, CP) + winf[rs, :]
                xhat, rs_, out = ln_fwd(fs, vec(4, CP), vec(5, CP))
                xhat2[ls, :] = xhat
                n2 = out.astype(bf16)
                normed2[ls, :] = n2
                hid = dot(n2, wfc1[...]) + vec(6, HP)
                ac, dg = gelu_pair(hid)
                ac = jnp.where(lanes((1, HP)) == HID, 1.0, ac).astype(bf16)
                act[ls, :] = ac
                dgelu[ls, :] = dg.astype(bf16)
                winf[rs, :] = fs + dot(ac, wfc2[...]) + vec(7, CP)
                lg = fgrad[rs, :]
                mg = lg.astype(bf16)
                d_fc2[...] += dot(act[ls, 0:FC2_ROWS], mg, 0, 0)
                ag = dot(mg, wfc2[...], 1, 1).astype(bf16).astype(f32)
                hg = (ag * dgelu[ls, :].astype(f32)).astype(bf16)
                d_fc1[...] += dot(normed2[ls, 0:CR], hg, 0, 0)
                dn2 = dot(hg, wfc1[...], 1, 1).astype(bf16).astype(f32)
                xh = xhat2[ls, :]
                d_norm[0:8, :] += fold8(dn2 * xh)
                d_norm[8:16, :] += fold8(dn2)
                fg = lg + ln_bwd(dn2, xh, rs_, vec(4, CP))
                fgrad[rs, :] = fg
                at = fg.astype(bf16)
                d_proj[...] += dot(mixed[ls, 0:CR], at, 0, 0)
                do_buf[rs, :] = dot(at, wproj[...], 1, 1).astype(bf16)

    @pl.loop(0, 2)
    def _(band):
        from_win(winf, band)

        @pl.loop(0, 8)
        def _(y):
            r = band * 8 + y
            pos = r + 1 + jnp.where(r >= 12, 2, 0)
            llbuf[row_at(pos), :] = jnp.where(col_in_p, xband[y], 0.0).astype(bf16)

    send_up = remote(llbuf.at[pl.ds(256, 256)], llbuf.at[pl.ds(19 * 256, 256)], up, 2)
    send_down = remote(llbuf.at[pl.ds(18 * 256, 256)], llbuf.at[pl.ds(0, 256)], down, 3)
    send_up.start()
    send_down.start()
    joined_low = joined.astype(bf16)
    llbuf[13 * 256 : 14 * 256, :] = llbuf[15 * 256 : 16 * 256, :] * joined_low
    llbuf[14 * 256 : 15 * 256, :] = llbuf[12 * 256 : 13 * 256, :] * joined_low

    def wgrad_rows(n):
        start = 1 + 4 * n + jnp.where(n == 3, 2, 0)
        gs = gcat[row_at(start, 4), :]
        for a in range(3):
            d_conv[a] += dot(llbuf[row_at(start + a - 1, 4), 0:CR], gs, 0, 0)

    @pl.loop(1, 3)
    def _(n):
        wgrad_rows(n)

    send_up.wait()
    send_down.wait()

    @pl.loop(0, 2)
    def _(n):
        wgrad_rows(n * 3)

    for a in range(3):
        for b in range(3):
            at = (a * 3 + b) * CR
            a1_buf[at : at + CR, :] = d_conv[a, :, b * CP : (b + 1) * CP].astype(bf16)
    a1_buf[A1_FC1 : A1_FC1 + CR, :] = d_fc1[:, 0:CP].astype(bf16)
    a1_buf[A1_FC1 + CR : A1_FC1 + 2 * CR, 0:128] = d_fc1[:, CP:HP].astype(bf16)
    a1_buf[A1_FC1 + CR : A1_FC1 + 2 * CR, 128:256] = jnp.zeros((CR, 128), bf16)
    a1_buf[A1_FC2 : A1_FC2 + FC2_ROWS, :] = d_fc2[...].astype(bf16)
    a1_buf[A1_PROJ : A1_PROJ + CR, :] = d_proj[...].astype(bf16)
    ar1.step(0)

    def conv_rows(lo, hi):
        @pl.loop(lo, hi)
        def _(r):
            pos = r + 1 + jnp.where(r >= 12, 2, 0)
            acc = None
            for a in range(3):
                d = dot(llbuf[row_at(pos + a - 1), :], wconv[a])
                acc = d if acc is None else acc + d
            tmp[8:264, :] = acc[:, 0:CP]
            tmp[280:536, :] = acc[:, 2 * CP : 3 * CP]
            out = acc[:, CP : 2 * CP] + tmp[7:263, :] + tmp[281:537, :] + vec(8, CP)
            out = out[:, 0:C] + io2[r + 4].astype(f32)
            io1[r] = jnp.where(col_in, out, 0.0).astype(bf16)

    tmp[...] = jnp.zeros_like(tmp)
    conv_rows(12, 16)
    send_res = remote(io1.at[pl.ds(12, 4)], res_out.at[pl.ds(0, 4)], down, 4)
    send_res.start()
    conv_rows(0, 6)
    ar1.step(1)
    conv_rows(6, 12)
    ar1.step(2)
    store_res = pltpu.make_async_copy(io1.at[pl.ds(0, 12)], res_out.at[pl.ds(4, 12)], lsem.at[2])
    store_res.start()

    @pl.loop(0, 8)
    def _(g):
        gs = pl.ds(pl.multiple_of(g * 512, 512), 512)

        @pl.loop(0, 8, unroll=4)
        def _(i):
            rs = win_rows(g * 8 + i)
            q = qkv[rs, 0:CP]
            k = qkv[rs, CP : 2 * CP]
            v = qkv[rs, 2 * CP : 3 * CP]
            dobd = spread_heads(do_buf[rs, :])
            dp = dot(v, dobd, 1, 1)
            pb = probs[rs, :]
            p = pb.astype(f32)
            ds = p * (dp - jnp.sum(p * dp, axis=0, keepdims=True))
            dsb = ds.astype(bf16)
            d_rel[...] += dsb.astype(f32)
            dv = dot(pb, dobd)
            dk = dot(dsb, spread_heads(q)) * SCALE
            dq = gather_heads(dot(dsb, k, 0, 0)) * SCALE
            qkv[rs, 0:CP] = dq.astype(bf16)
            qkv[rs, CP : 2 * CP] = dk.astype(bf16)
            qkv[rs, 2 * CP : 3 * CP] = dv.astype(bf16)

        d_qkv[...] += dot(normed[gs, 0:CR], qkv[gs, :], 0, 0)

        @pl.loop(0, 512 // RM)
        def _(j):
            rs = pl.ds(pl.multiple_of(g * 512 + j * RM, RM), RM)
            dn1 = dot(qkv[rs, :], wqkv[...], 1, 1).astype(bf16).astype(f32)
            xhat = xhat1[rs, :].astype(f32)
            d_norm[16:24, :] += fold8(dn1 * xhat)
            d_norm[24:32, :] += fold8(dn1)
            fgrad[rs, :] = fgrad[rs, :] + ln_bwd(dn1, xhat, xhat[:, 200:201] + xhat[:, 201:202], vec(0, CP))

        @pl.when(g == 0)
        def _():
            ar1.step(3)

        @pl.when(g == 1)
        def _():
            ar1.step(4)

        @pl.when(g == 3)
        def _():
            ar1.step(5)

        @pl.when(g == 5)
        def _():
            ar1.step(6)

    for n in range(3):
        a2_buf[n * CR : (n + 1) * CR, :] = d_qkv[:, n * CP : (n + 1) * CP].astype(bf16)
    norms = jnp.sum(d_norm[...].reshape(4, 8, CP), axis=1)
    small = jnp.concatenate([norms, table_sum(d_rel[...]), jnp.zeros((4, CP), f32)], axis=0)
    a2_buf[A2_SMALL : A2_SMALL + 16, :] = small.astype(bf16)
    ar2.step(0)

    def grad_rows(band):
        from_win(fgrad, band)

        @pl.loop(0, 8)
        def _(y):
            r = band * 8 + y
            pos = r + 1 + jnp.where(r >= 12, 2, 0)
            v = xband[y] + gcat[row_at(pos), CP : 2 * CP].astype(f32)
            io2[r] = jnp.where(col_in_p, v, 0.0)[:, 0:C].astype(bf16)

    grad_rows(1)
    send_ig = remote(io2.at[pl.ds(12, 4)], ig_out.at[pl.ds(0, 4)], down, 5)
    send_ig.start()
    ar2.step(1)
    grad_rows(0)
    store_ig = pltpu.make_async_copy(io2.at[pl.ds(0, 12)], ig_out.at[pl.ds(4, 12)], lsem.at[3])
    store_ig.start()
    ar2.step(2)

    for a in range(3):
        for b in range(3):
            at = (a * 3 + b) * CR
            o_conv[a, b] = a1_out[at : at + CR, :].astype(f32)[0:C, 0:C]
    o_fc1[:, 0:CP] = a1_out[A1_FC1 : A1_FC1 + CR, :].astype(f32)[0:C, :]
    o_fc1[:, CP:HID] = a1_out[A1_FC1 + CR : A1_FC1 + 2 * CR, :].astype(f32)[0:C, 0 : HID - CP]
    o_fc2[...] = a1_out[A1_FC2 : A1_FC2 + FC2_ROWS, :].astype(f32)[0:HID, 0:C]
    o_proj[...] = a1_out[A1_PROJ : A1_PROJ + CR, :].astype(f32)[0:C, 0:C]
    o_vec[0:8, :] = a1_out[A1_FC1 + 176 : A1_FC1 + 192, :].astype(f32)[0:8]
    o_vec[8:16, :] = a1_out[A1_FC1 + CR + 176 : A1_FC1 + CR + 192, :].astype(f32)[0:8]
    o_vec[16:24, :] = a1_out[A1_FC2 + 352 : A1_FC2 + 368, :].astype(f32)[8:16]
    o_vec[24:32, :] = a1_out[A1_PROJ + 176 : A1_PROJ + 192, :].astype(f32)[0:8]
    o_vec[32:40, :] = a1_out[4 * CR + 176 : 4 * CR + 192, :].astype(f32)[0:8]
    ar2.step(3)
    ar2.step(5)
    ar2.step(6)
    for n in range(3):
        o_qkv[:, n * C : (n + 1) * C] = a2_out[n * CR : (n + 1) * CR, :].astype(f32)[0:C, 0:C]
    o_vec[40:48, :] = a2_out[176:192, :].astype(f32)[0:8]
    o_vec[48:56, :] = a2_out[2 * CR + 176 : 2 * CR + 192, :].astype(f32)[0:8]
    o_vec[56:72, :] = a2_out[A2_SMALL : A2_SMALL + 16, :].astype(f32)
    send_res.wait()
    send_ig.wait()
    store_res.wait()
    store_ig.wait()


def table_sum(d_rel):
    row = lax.broadcasted_iota(jnp.int32, (AREA, CP), 0)
    lane = lax.broadcasted_iota(jnp.int32, (AREA, CP), 1)
    put = (lane == row + lax.div(row, WIN) * (WIN - 1)).astype(bf16)
    heads = []
    for h in range(HEADS):
        v = d_rel[:, h * AREA : (h + 1) * AREA]
        v1 = v.astype(bf16)
        v2 = (v - v1.astype(f32)).astype(bf16)
        wide = dot(v1, put) + dot(v2, put)
        total = None
        for y in range(WIN):
            part = pltpu.roll(wide[y * WIN : (y + 1) * WIN, :], 112 - 15 * y, 1)
            total = part if total is None else total + part
        heads.append(total)
    out = None
    for x in range(WIN):
        rows = jnp.concatenate([t[x : x + 1] for t in heads] + [jnp.zeros((2, CP), f32)], axis=0)
        rows = pltpu.roll(rows, CP - x, 1) if x else rows
        out = rows if out is None else out + rows
    return out


def relative_index():
    coords = np.arange(AREA)
    row, col = coords // WIN, coords % WIN
    return (row[:, None] - row[None, :] + WIN - 1) * (2 * WIN - 1) + col[:, None] - col[None, :] + WIN - 1


def score_extra(bias_table):
    hot = jnp.asarray(
        (relative_index().T.reshape(-1)[:, None] == np.arange(225)[None, :]).astype(np.float32)
    )
    rel = jnp.dot(hot, bias_table, precision=lax.Precision.HIGHEST)
    rel = rel.reshape(AREA, AREA, HEADS).transpose(0, 2, 1).reshape(AREA, HI)
    coords = np.arange(AREA)
    yh = coords // WIN >= SHIFT
    xh = coords % WIN >= SHIFT
    ydiff = yh[:, None] != yh[None, :]
    xdiff = xh[:, None] != xh[None, :]
    masks = np.stack([np.zeros_like(ydiff), xdiff, ydiff, ydiff | xdiff])
    masks = np.where(np.tile(masks, (1, 1, HEADS)), -100.0, 0.0).astype(np.float32)
    return (rel[None] + jnp.asarray(masks)) * LOG2E


VM = pl.BlockSpec(memory_space=pltpu.VMEM)
SM = pl.BlockSpec(memory_space=pltpu.SMEM)
HB = pl.BlockSpec(memory_space=pl.ANY)


def up_to(n, m):
    return (n + m - 1) // m * m


def run_layer(stripes, imgs, scal, img, cot, wqkv, wproj, wfc1, wfc2, wconv, vecs, extra):
    S = jax.ShapeDtypeStruct
    V = pltpu.VMEM
    chips = stripes // 2
    piece1 = up_to(-(-A1_USED // (stripes * imgs)), 16)
    piece2 = up_to(-(-A2_USED // stripes), 16)
    half1 = piece1 * imgs * chips
    half2 = piece2 * chips
    sems = 2 * (chips + imgs - 1)
    dma = pltpu.SemaphoreType.DMA
    return pl.pallas_call(
        functools.partial(layer_kernel, chips, imgs, piece1, piece2),
        out_shape=(
            S((16, 256, C), bf16),
            S((16, 256, C), bf16),
            S((C, 3 * C), f32),
            S((C, C), f32),
            S((C, HID), f32),
            S((HID, C), f32),
            S((3, 3, C, C), f32),
            S((72, CP), f32),
        ),
        in_specs=[SM, HB, HB] + [VM] * 7,
        out_specs=[HB] * 2 + [VM] * 6,
        scratch_shapes=[
            V((CR, 3 * CP), f32),
            V((CR, CP), f32),
            V((CR, HP), f32),
            V((FC2_ROWS, CP), f32),
            V((3, CR, 3 * CP), f32),
            V((32, CP), f32),
            V((AREA, HI), f32),
            V((21, 256, C), bf16),
            V((20, 256, C), bf16),
            V((8, 256, CP), f32),
            V((8, 256, CP), f32),
            V((20 * 256, 3 * CP), bf16),
            V((20 * 256, CP), bf16),
            V((4096, CP), bf16),
            V((4096, CP), bf16),
            V((4096, 3 * CP), bf16),
            V((4096, HI), bf16),
            V((512, CP), bf16),
            V((512, CP), f32),
            V((512, CP), bf16),
            V((512, HP), bf16),
            V((512, HP), bf16),
            V((4096, CP), f32),
            V((4096, CP), f32),
            V((4096, CP), bf16),
            V((WIN, WIN, CP), f32),
            V((544, CP), f32),
            V((2 * half1, CP), bf16),
            V((2 * half1, CP), bf16),
            V((half1, CP), bf16),
            V(((chips - 1) * piece1 * imgs, CP), bf16),
            V(((imgs - 1) * piece1, CP), bf16),
            V((2 * half2, CP), bf16),
            V((2 * half2, CP), bf16),
            V((half2, CP), bf16),
            V(((chips - 1) * piece2, CP), bf16),
            V(((imgs - 1) * piece2, CP), bf16),
            dma((4,)),
            dma((6,)),
            dma((6,)),
            dma((sems,)),
            dma((sems,)),
            dma((sems,)),
            dma((sems,)),
        ],
        compiler_params=pltpu.CompilerParams(
            vmem_limit_bytes=63 * 1024 * 1024, collective_id=0, has_side_effects=True
        ),
        name="layer",
    )(scal, img, cot, wqkv, wproj, wfc1, wfc2, wconv, vecs, extra)


def prepare(norm1_gain, norm1_bias, qkv_weight, qv_bias, bias_table, proj_weight, proj_bias,
            norm2_gain, norm2_bias, fc1_weight, fc1_bias, fc2_weight, fc2_bias, conv_weight, conv_bias):
    pc = CP - C
    wqkv = jnp.pad(qkv_weight.reshape(C, 3, C), ((0, pc), (0, 0), (0, pc))).reshape(CP, 3 * CP)
    wproj = jnp.pad(proj_weight, ((0, pc), (0, pc)))
    wfc1 = jnp.pad(fc1_weight, ((0, pc), (0, HP - HID)))
    wfc2 = jnp.pad(fc2_weight, ((0, HP - HID), (0, pc)))
    wconv = jnp.pad(conv_weight.transpose(0, 2, 1, 3), ((0, 0), (0, pc), (0, 0), (0, pc)))
    wconv = wconv.reshape(3, CP, 3 * CP)

    def row(v, one=False):
        v = jnp.concatenate([v, jnp.ones((1,), f32)]) if one else v
        return jnp.pad(v, (0, 3 * CP - v.shape[0]))

    zero = jnp.zeros((C,), f32)
    qkvb = jnp.pad(jnp.stack([qv_bias[:C], zero, qv_bias[C:]]), ((0, 0), (0, pc))).reshape(-1)
    vecs = jnp.stack(
        [row(norm1_gain), row(norm1_bias, True), qkvb, row(proj_bias), row(norm2_gain),
         row(norm2_bias, True), row(fc1_bias), row(fc2_bias, True), row(conv_bias)]
        + [jnp.zeros((3 * CP,), f32)] * 7
    )
    return wqkv, wproj, wfc1, wfc2, wconv, vecs, score_extra(bias_table)


def on_device(
    images, widths, norm1_gain, norm1_bias, qkv_weight, qv_bias, bias_table, proj_weight, proj_bias,
    norm2_gain, norm2_bias, fc1_weight, fc1_bias, fc2_weight, fc2_bias, conv_weight, conv_bias, cotangent,
):
    count, rows_here, width, chans = images.shape
    img = images.reshape(rows_here, width, chans)
    cot = cotangent.reshape(rows_here, width, chans)
    scal = lax.div(widths, WIN)
    wqkv, wproj, wfc1, wfc2, wconv, vecs, extra = prepare(
        norm1_gain, norm1_bias, qkv_weight, qv_bias, bias_table, proj_weight, proj_bias,
        norm2_gain, norm2_bias, fc1_weight, fc1_bias, fc2_weight, fc2_bias, conv_weight, conv_bias,
    )
    res, ig, g_qkv, g_proj, g_fc1, g_fc2, g_conv, v = run_layer(
        lax.axis_size("rows"), lax.axis_size("imgs"),
        scal, img, cot, wqkv, wproj, wfc1, wfc2, wconv, vecs, extra,
    )
    return (
        res[None],
        ig[None],
        v[58, :C],
        v[59, :C],
        g_qkv,
        jnp.concatenate([v[44, :C], v[52, :C]]),
        v[60 : 60 + HEADS, :225].T,
        g_proj,
        v[28, :C],
        v[56, :C],
        v[57, :C],
        g_fc1,
        jnp.concatenate([v[4], v[12, : HID - CP]]),
        g_fc2,
        v[16, :C],
        g_conv,
        v[36, :C],
    )


def solution(mesh):
    big = P("imgs", "rows", None, None)
    in_specs = (big, P("imgs")) + (P(),) * 15 + (big,)
    out_specs = (big, big) + (P(),) * 15
    return jax.shard_map(
        on_device, mesh=mesh, in_specs=in_specs, out_specs=out_specs, check_vma=False
    )
```

time: 378 us -> 211 us (0.56)
  waiting for transfers between devices: 81 us -> 0 us
  blocking collectives: 42.3 us -> 0 us
  local copies, waits for them, and re-layouts: 51.4 us -> 32.4 us
  between operations: 15.3 us -> 1.52 us
  starting transfers between devices: 5.93 us -> 0 us
  matrix products: 10.2 us -> 5.84 us
    psum x1 -> x0, waiting for transfers between devices: 80.9 us -> none  [on_device(): summed = lax.psum(local, ('rows', 'imgs'))]
    psum x1 -> x0, blocking collectives: 42.3 us -> none  [on_device(): summed = lax.psum(local, ('rows', 'imgs'))]
    slice x18 -> x2, local copies, waits for them, and re-layouts: 13.1 us -> 2.17 us  [the longest x1 1.48 us: on_device(): v[36, :C]]
    unnamed x75 -> x44, local copies, waits for them, and re-layouts: 24.2 us -> 17.3 us
    ppermute x6 -> x0, starting transfers between devices: 5.89 us -> none  [ring(): return lax.ppermute(value, axis, pairs)]
    dot_general x1 -> x0, matrix products: 4.37 us -> none  [rel_to_table(): return jnp.dot(hot.T, per, precision=lax.Precision.HIGHEST)]
    broadcast_in_dim x2 -> x0, other arithmetic: 3.79 us -> none  [moved(): return jnp.concatenate([head, rows[:rows_here - SHIFT]], axis=0)[None]]
    pallas_call x2 -> x1, Pallas kernels: 166 us -> 167 us  [run_layer(): pl.pallas_call(functools.partial(layer_kernel, chips, imgs, piece1, piece...]
  transfers between devices with their start and end apart: 7 -> 0, of which waited for: 1 -> 0; matrix products, arithmetic and copies ran while one was open for 14% -> 0% of each run, Pallas kernels for 6% -> 0%
where the time goes in v2:
time: 211 us; the launch traced here: 210 us
  Pallas kernels  167 us (79%)
  local copies, waits for them, and re-layouts  32.4 us (15%)
  matrix products  5.84 us (3%)
  other arithmetic  3.62 us (2%)
    pallas_call x1, Pallas kernels, run_layer(): pl.pallas_call(functools.partial(layer_kernel, chips, imgs, piece1, piece...  167 us
    unnamed x44, local copies, waits for them, and re-layouts  17.3 us
    dot_general x1, matrix products, score_extra(): rel = jnp.dot(hot, bias_table, precision=lax.Precision.HIGHEST)  5.84 us

profile of v2, /device:TPU:0, one launch (start us, length us, event | category | flops | bytes accessed | tf_op | source)
XLA Modules:
  0.0 210.4 jit_solution(3354701639441941023)
XLA Ops:
  1.4 0.8 pad_maximum_fusion.5
  2.2 0.8 fusion.1
  3.1 0.8 pad_maximum_fusion.3
  3.9 0.7 pad.56
  4.6 0.7 pad.59
  5.3 0.7 pad.60
  6.0 0.7 pad.62
  6.7 0.7 pad.64
  7.4 1.3 stack.55.vecs
  8.7 5.8 %fusion.2 = f32[4096,6]{0,1:T(8,128)S(1)} fusion(f32[4096,225]{1,0:T(8,128)} %constant.24.clone, f32[225,6]{0,1:T(8,128)S(1)} %copy-done), kind=kOutput, calls=%fused_computation.13 | convolution fusion | flops 66355200 | bytes 3790104 | tf_op jit(solution)/shard_map/dot_general | solution.py:717
  14.9 0.7 pad.52.wproj
  15.7 0.7 pad.54.wfc2
  16.4 0.7 pad.53.wfc1
  17.4 0.9 copy.51.wqkv
  18.3 0.8 add_multiply_fusion.extra
  19.1 0.8 copy.49
  20.1 1.5 copy.52.wconv
  21.6 2.6 %copy.45 = bf16[1,16,256,180]{3,2,1,0:T(8,128)(2,1)} copy(bf16[1,16,256,180]{2,1,3,0:T(8,128)(2,1)S(1)} %copy-done.3) | data formatting | bytes 2949120 | tf_op args[0]
  24.3 2.6 %copy.46 = bf16[1,16,256,180]{3,2,1,0:T(8,128)(2,1)} copy(bf16[1,16,256,180]{2,1,3,0:T(8,128)(2,1)S(1)} %copy-done.4) | data formatting | bytes 2949120 | tf_op args[17]
  26.9 167.0 %layer.1 = (bf16[16,256,180]{2,1,0:T(8,128)(2,1)}, bf16[16,256,180]{2,1,0:T(8,128)(2,1)}, f32[180,540]{1,0:T(8,128)}, f32[180,180]{1,0:T(8,128)}, f32[180,360]{1...) custom-call(s32[1]{0:T(128)S(6)} %div.18.scal, bf16[16,256,180]{2,1,0:T(8,128)(2,1)} %bitcast.37, ...), custom_call_target="tpu_custom_call" | custom-call | tf_op jit(solution)/shard_map/layer/pallas_call | solution.py:748
  193.9 4.3 %copy.53 = bf16[1,16,256,180]{2,1,3,0:T(8,128)(2,1)} copy(bf16[1,16,256,180]{3,2,1,0:T(8,128)(2,1)} %bitcast.42) | data formatting | bytes 2949120
  198.2 2.4 %copy.54 = bf16[1,16,256,180]{2,1,3,0:T(8,128)(2,1)} copy(bf16[1,16,256,180]{3,2,1,0:T(8,128)(2,1)S(1)} %bitcast.41) | data formatting | bytes 2949120
  200.6 0.8 slice_bitcast_fusion.1
  201.4 0.7 slice.52
  202.7 1.3 slice_bitcast_fusion
  204.0 1.5 fusion
  205.5 0.7 pad_maximum_fusion.1
  206.1 0.9 copy.55
  207.0 0.8 copy.64
  207.8 0.7 copy.65
  208.5 0.7 copy.66
  209.2 1.2 copy.67
  (57 shorter events, 1.8 us)
Async XLA Ops:
  0.7 8.0 %copy-start = (f32[225,6]{0,1:T(8,128)S(1)}, f32[225,6]{0,1:T(8,128)}, u32[]{:S(2)}) copy-start(f32[225,6]{0,1:T(8,128)} %param.26) | copy-start | bytes 16204
  8.7 6.2 %copy-start.14 = (bf16[180,180]{1,0:T(8,128)(2,1)S(1)}, bf16[180,180]{1,0:T(8,128)(2,1)}, u32[]{:S(2)}) copy-start(bf16[180,180]{1,0:T(8,128)(2,1)} %param.27) | copy-start | bytes 194404
  8.7 6.9 %copy-start.12 = (bf16[360,180]{0,1:T(8,128)(2,1)S(1)}, bf16[360,180]{0,1:T(8,128)(2,1)}, u32[]{:S(2)}) copy-start(bf16[360,180]{0,1:T(8,128)(2,1)} %param.33) | copy-start | bytes 388804
  14.5 1.9 copy-start.13
  14.5 2.6 %copy-start.10 = (bf16[180,540]{1,0:T(8,128)(2,1)S(1)}, bf16[180,540]{1,0:T(8,128)(2,1)}, u32[]{:S(2)}) copy-start(bf16[180,540]{1,0:T(8,128)(2,1)} %param.24) | copy-start | bytes 583204
  14.8 3.6 %copy-start.7 = (f32[4,64,384]{2,1,0:T(8,128)S(1)}, f32[4,64,384]{2,1,0:T(8,128)}, u32[]{:S(2)}) copy-start(f32[4,64,384]{2,1,0:T(8,128)} %constant.25.clone) | copy-start | bytes 1179652
  15.7 3.4 %copy-start.5 = (bf16[3,3,180,180]{3,2,1,0:T(8,128)(2,1)S(1)}, bf16[3,3,180,180]{3,2,1,0:T(8,128)(2,1)}, u32[]{:S(2)}) copy-start(bf16[3,3,180,180]{3,2,1,0:T(8,128)(2,1)} %param.35) | copy-start | bytes 1749604
  19.9 1.7 copy-start.3
  21.6 2.6 %copy-start.4 = (bf16[1,16,256,180]{2,1,3,0:T(8,128)(2,1)S(1)}, bf16[1,16,256,180]{2,1,3,0:T(8,128)(2,1)}, u32[]{:S(2)}) copy-start(bf16[1,16,256,180]{2,1,3,0:T(8,128)(2,1)} %param.37) | copy-start | bytes 4423684
  193.9 4.3 %copy-start.1 = (bf16[16,256,180]{2,1,0:T(8,128)(2,1)S(1)}, bf16[16,256,180]{2,1,0:T(8,128)(2,1)}, u32[]{:S(2)}) copy-start(bf16[16,256,180]{2,1,0:T(8,128)(2,1)} %get-tuple-element.26) | copy-start | bytes 4423684
  198.2 8.0 %copy-start.8 = (f32[360,180]{1,0:T(8,128)S(1)}, f32[360,180]{1,0:T(8,128)}, u32[]{:S(2)}) copy-start(f32[360,180]{1,0:T(8,128)} %get-tuple-element.63) | copy-start | bytes 777604
  198.2 8.8 %copy-start.6 = (f32[180,540]{1,0:T(8,128)S(1)}, f32[180,540]{1,0:T(8,128)}, u32[]{:S(2)}) copy-start(f32[180,540]{1,0:T(8,128)} %get-tuple-element.101) | copy-start | bytes 1166404
  198.2 9.6 %copy-start.11 = (f32[180,180]{1,0:T(8,128)S(1)}, f32[180,180]{1,0:T(8,128)}, u32[]{:S(2)}) copy-start(f32[180,180]{1,0:T(8,128)} %get-tuple-element.104) | copy-start | bytes 388804
  198.2 10.3 %copy-start.9 = (f32[180,360]{1,0:T(8,128)S(1)}, f32[180,360]{1,0:T(8,128)}, u32[]{:S(2)}) copy-start(f32[180,360]{1,0:T(8,128)} %get-tuple-element.108) | copy-start | bytes 777604
  200.6 8.6 %copy-start.2 = (f32[3,3,180,180]{3,2,1,0:T(8,128)S(1)}, f32[3,3,180,180]{3,2,1,0:T(8,128)}, u32[]{:S(2)}) copy-start(f32[3,3,180,180]{3,2,1,0:T(8,128)} %get-tuple-element.112) | copy-start | bytes 3499204

commit v3 on v2

--- a/solution.py
+++ b/solution.py
@@ -87,22 +87,40 @@
     return jnp.sum(v.reshape(v.shape[0] // 8, 8, v.shape[1]), axis=0)
 
 
+HP_DIM = 32
+
+
+def by_rows(f, step, *arrays):
+    rows = arrays[0].shape[0]
+    parts = [f(*[a[i : i + step] for a in arrays]) for i in range(0, rows, step)]
+    if not isinstance(parts[0], tuple):
+        return jnp.concatenate(parts, axis=0)
+    return tuple(jnp.concatenate(p, axis=0) for p in zip(*parts))
+
+
+def added(values):
+    return functools.reduce(jnp.add, values)
+
+
 def head_mask(h):
-    ln = lanes((1, CP))
-    return (ln >= h * HEAD_DIM) & (ln < (h + 1) * HEAD_DIM)
-
-
-def spread_heads(v):
+    ln = lanes((1, 128))
+    return (ln >= h * HP_DIM) & (ln < (h + 1) * HP_DIM)
+
+
+def spread_heads(v, count):
     return jnp.concatenate(
-        [jnp.where(head_mask(h), v, jnp.zeros_like(v)) for h in range(HEADS)], axis=0
+        [jnp.where(head_mask(h), v, jnp.zeros_like(v)) for h in range(count)], axis=0
     )
 
 
-def gather_heads(v):
+def gather_heads(v, count):
     out = jnp.where(head_mask(0), v[:AREA], 0.0)
-    for h in range(1, HEADS):
+    for h in range(1, count):
         out = jnp.where(head_mask(h), v[h * AREA : (h + 1) * AREA], out)
     return out
+
+
+GROUPS = ((0, 4), (4, 2))
 
 
 def column_masks(width):
@@ -277,10 +295,6 @@
     qkv,
     probs,
     mixed,
-    xhat2,
-    normed2,
-    act,
-    dgelu,
     winf,
     fgrad,
     do_buf,
@@ -442,69 +456,91 @@
             k0 = gg * 8
             gs = pl.ds(pl.multiple_of(g * 512, 512), 512)
 
-            @pl.loop(0, 8, unroll=4)
-            def _(i):
-                x = to_win(xband, k0 + i)
-                rs = win_rows(g * 8 + i)
-                xhat, rs_, out = ln_fwd(x, vec(0, CP), vec(1, CP))
-                winf[rs, :] = x
-                xhat1[rs, :] = with_rstd(xhat, rs_).astype(bf16)
-                normed[rs, :] = out.astype(bf16)
-                fgrad[rs, :] = to_win(gband, k0 + i)
+            xs = [to_win(xband, k0 + w) for w in range(8)]
+            for w in range(8):
+                winf[win_rows(g * 8 + w), :] = xs[w]
+                fgrad[win_rows(g * 8 + w), :] = to_win(gband, k0 + w)
+                xhat, rs_, ln_out = ln_fwd(xs[w], vec(0, CP), vec(1, CP))
+                xhat1[win_rows(g * 8 + w), :] = with_rstd(xhat, rs_).astype(bf16)
+                normed[win_rows(g * 8 + w), :] = ln_out.astype(bf16)
 
             for n in range(3):
                 sl = slice(n * CP, (n + 1) * CP)
                 qkv[gs, sl] = (dot(normed[gs, :], wqkv[:, sl]) + vecs[2:3, sl]).astype(bf16)
 
-            @pl.loop(0, 8, unroll=4)
-            def _(i):
-                rs = win_rows(g * 8 + i)
-                kk = k0 + i
-                q = qkv[rs, 0:CP]
-                k = qkv[rs, CP : 2 * CP]
-                v = qkv[rs, 2 * CP : 3 * CP]
+            i = 0
+            if True:
                 which = jnp.where((band == 1) & is_last, 2, 0)
-                more = jnp.where(kk == nb - 1, extra[which + 1], extra[which])
-                s = dot(k, spread_heads(q), 1, 1) * (SCALE * LOG2E) + more
-                top = jnp.max(s, axis=0, keepdims=True)
-                e = jnp.exp2(s - top)
-                total = jnp.sum(e, axis=0, keepdims=True)
-                p = (e * (1.0 / total)).astype(bf16)
-                probs[rs, :] = p
-                o = gather_heads(dot(p, v, 0, 0))
-                o = jnp.where(lanes((1, CP)) == C, 1.0, o)
-                mixed[win_rows(i), :] = o.astype(bf16)
-
-            @pl.loop(0, 512 // RM)
-            def _(j):
-                ls = pl.ds(pl.multiple_of(j * RM, RM), RM)
-                rs = pl.ds(pl.multiple_of(g * 512 + j * RM, RM), RM)
-                fs = dot(mixed[ls, :], wproj[...]) + vec(3, CP) + winf[rs, :]
-                xhat, rs_, out = ln_fwd(fs, vec(4, CP), vec(5, CP))
-                xhat2[ls, :] = xhat
-                n2 = out.astype(bf16)
-                normed2[ls, :] = n2
-                hid = dot(n2, wfc1[...]) + vec(6, HP)
-                ac, dg = gelu_pair(hid)
-                ac = jnp.where(lanes((1, HP)) == HID, 1.0, ac).astype(bf16)
-                act[ls, :] = ac
-                dgelu[ls, :] = dg.astype(bf16)
+                jobs = []
+                for w in range(8):
+                    rs = win_rows(g * 8 + i * 8 + w)
+                    edge_win = k0 + i * 8 + w == nb - 1
+                    for n, (h0, count) in enumerate(GROUPS):
+                        jobs.append((rs, w, edge_win, n, count, slice(h0 * AREA, (h0 + count) * AREA)))
+                qs = [qkv[rs, n * 128 : (n + 1) * 128] for rs, w, ew, n, count, hl in jobs]
+                ks = [qkv[rs, CP + n * 128 : CP + (n + 1) * 128] for rs, w, ew, n, count, hl in jobs]
+                vs = [qkv[rs, 2 * CP + n * 128 : 2 * CP + (n + 1) * 128] for rs, w, ew, n, count, hl in jobs]
+                ss = [dot(k, spread_heads(q, job[4]), 1, 1) for q, k, job in zip(qs, ks, jobs)]
+                ps = []
+                for s, (rs, w, ew, n, count, hl) in zip(ss, jobs):
+                    more = jnp.where(ew, extra[which + 1, :, hl], extra[which, :, hl])
+                    s = s * (SCALE * LOG2E) + more
+                    top = jnp.max(s, axis=0, keepdims=True)
+                    e = jnp.exp2(s - top)
+                    total = jnp.sum(e, axis=0, keepdims=True)
+                    ps.append((e * (1.0 / total)).astype(bf16))
+                os = [gather_heads(dot(p, v, 0, 0), job[4]) for p, v, job in zip(ps, vs, jobs)]
+                for p, o, (rs, w, ew, n, count, hl) in zip(ps, os, jobs):
+                    probs[rs, hl] = p
+                    if n == 0:
+                        o = jnp.where(lanes((1, 128)) == HEAD_DIM, 1.0, o)
+                    mixed[win_rows(i * 8 + w), n * 128 : (n + 1) * 128] = o.astype(bf16)
+
+            parts = range(0, 512, 256)
+            at_rows = [pl.ds(pl.multiple_of(g * 512 + r, 256), 256) for r in parts]
+            mixes = [mixed[r : r + 256, :] for r in parts]
+            firsts = [dot(m, wproj[...]) + vec(3, CP) + winf[rs, :] for m, rs in zip(mixes, at_rows)]
+
+            def norm2(v):
+                xhat, rs_, ln_out = ln_fwd(v, vec(4, CP), vec(5, CP))
+                return xhat, rs_, ln_out.astype(bf16)
+
+            def activate(v):
+                ac, dg = gelu_pair(v + vec(6, HP))
+                return jnp.where(lanes((1, HP)) == HID, 1.0, ac).astype(bf16), dg.astype(bf16)
+
+            norms = [by_rows(norm2, 64, v) for v in firsts]
+            n2s = [n[2] for n in norms]
+            acts = [by_rows(activate, 64, dot(n2, wfc1[...])) for n2 in n2s]
+            for fs, (ac, dg), rs in zip(firsts, acts, at_rows):
                 winf[rs, :] = fs + dot(ac, wfc2[...]) + vec(7, CP)
-                lg = fgrad[rs, :]
-                mg = lg.astype(bf16)
-                d_fc2[...] += dot(act[ls, 0:FC2_ROWS], mg, 0, 0)
-                ag = dot(mg, wfc2[...], 1, 1).astype(bf16).astype(f32)
-                hg = (ag * dgelu[ls, :].astype(f32)).astype(bf16)
-                d_fc1[...] += dot(normed2[ls, 0:CR], hg, 0, 0)
-                dn2 = dot(hg, wfc1[...], 1, 1).astype(bf16).astype(f32)
-                xh = xhat2[ls, :]
-                d_norm[0:8, :] += fold8(dn2 * xh)
-                d_norm[8:16, :] += fold8(dn2)
+            lgs = [fgrad[rs, :] for rs in at_rows]
+            mgs = [lg.astype(bf16) for lg in lgs]
+            hgs = [
+                (dot(mg, wfc2[...], 1, 1).astype(bf16).astype(f32) * dg.astype(f32)).astype(bf16)
+                for mg, (ac, dg) in zip(mgs, acts)
+            ]
+            dns = [dot(hg, wfc1[...], 1, 1).astype(bf16) for hg in hgs]
+
+            def back2(dn2, xh, rs_, lg):
+                dn2 = dn2.astype(f32)
                 fg = lg + ln_bwd(dn2, xh, rs_, vec(4, CP))
-                fgrad[rs, :] = fg
-                at = fg.astype(bf16)
-                d_proj[...] += dot(mixed[ls, 0:CR], at, 0, 0)
-                do_buf[rs, :] = dot(at, wproj[...], 1, 1).astype(bf16)
+                return fg, fg.astype(bf16), fold8(dn2 * xh), fold8(dn2)
+
+            backs = [
+                by_rows(back2, 64, dn, n[0], n[1], lg) for dn, n, lg in zip(dns, norms, lgs)
+            ]
+            ats = [b[1] for b in backs]
+            for b, rs in zip(backs, at_rows):
+                fgrad[rs, :] = b[0]
+                do_buf[rs, :] = dot(b[1], wproj[...], 1, 1).astype(bf16)
+            d_norm[0:8, :] += added([fold8(b[2]) for b in backs])
+            d_norm[8:16, :] += added([fold8(b[3]) for b in backs])
+            join = lambda vs: jnp.concatenate(vs, axis=0)
+            mg = join(mgs)
+            d_fc2[...] += dot(join([ac for ac, dg in acts])[:, 0:FC2_ROWS], mg, 0, 0)
+            d_fc1[...] += dot(join(n2s)[:, 0:CR], join(hgs), 0, 0)
+            d_proj[...] += dot(mixed[:, 0:CR], join(ats), 0, 0)
 
     @pl.loop(0, 2)
     def _(band):
@@ -551,6 +587,75 @@
     a1_buf[A1_FC2 : A1_FC2 + FC2_ROWS, :] = d_fc2[...].astype(bf16)
     a1_buf[A1_PROJ : A1_PROJ + CR, :] = d_proj[...].astype(bf16)
     ar1.step(0)
+
+    @pl.loop(0, 8)
+    def _(g):
+        gs = pl.ds(pl.multiple_of(g * 512, 512), 512)
+
+        i = 0
+        if True:
+            jobs = []
+            for w in range(8):
+                rs = win_rows(g * 8 + i * 8 + w)
+                for n, (h0, count) in enumerate(GROUPS):
+                    jobs.append((rs, n, count, slice(h0 * AREA, (h0 + count) * AREA)))
+            qs = [qkv[rs, n * 128 : (n + 1) * 128] for rs, n, count, hl in jobs]
+            ks = [qkv[rs, CP + n * 128 : CP + (n + 1) * 128] for rs, n, count, hl in jobs]
+            vs = [qkv[rs, 2 * CP + n * 128 : 2 * CP + (n + 1) * 128] for rs, n, count, hl in jobs]
+            dos = [spread_heads(do_buf[rs, n * 128 : (n + 1) * 128], count) for rs, n, count, hl in jobs]
+            pbs = [probs[rs, hl] for rs, n, count, hl in jobs]
+            dps = [dot(v, d, 1, 1) for v, d in zip(vs, dos)]
+            dvs = [dot(p, d) for p, d in zip(pbs, dos)]
+            dss = []
+            for dp, pb in zip(dps, pbs):
+                p = pb.astype(f32)
+                dss.append((p * (dp - jnp.sum(p * dp, axis=0, keepdims=True))).astype(bf16))
+            dks = [dot(ds, spread_heads(q, job[2])) * SCALE for ds, q, job in zip(dss, qs, jobs)]
+            dqs = [gather_heads(dot(ds, k, 0, 0), job[2]) * SCALE for ds, k, job in zip(dss, ks, jobs)]
+            for n, (h0, count) in enumerate(GROUPS):
+                hl = slice(h0 * AREA, (h0 + count) * AREA)
+                d_rel[:, hl] += functools.reduce(jnp.add, [d.astype(f32) for d in dss[n::2]])
+            for dq, dk, dv, (rs, n, count, hl) in zip(dqs, dks, dvs, jobs):
+                qkv[rs, n * 128 : (n + 1) * 128] = dq.astype(bf16)
+                qkv[rs, CP + n * 128 : CP + (n + 1) * 128] = dk.astype(bf16)
+                qkv[rs, 2 * CP + n * 128 : 2 * CP + (n + 1) * 128] = dv.astype(bf16)
+
+        d_qkv[...] += dot(normed[gs, 0:CR], qkv[gs, :], 0, 0)
+
+        dn1 = dot(qkv[gs, :], wqkv[...], 1, 1).astype(bf16)
+
+        def back1(dn, xhat, fg):
+            dn, xhat = dn.astype(f32), xhat.astype(f32)
+            out = fg + ln_bwd(dn, xhat, xhat[:, 200:201] + xhat[:, 201:202], vec(0, CP))
+            return out, fold8(dn * xhat), fold8(dn)
+
+        back = by_rows(back1, 64, dn1, xhat1[gs, :], fgrad[gs, :])
+        fgrad[gs, :] = back[0]
+        d_norm[16:24, :] += fold8(back[1])
+        d_norm[24:32, :] += fold8(back[2])
+
+        for k, at in enumerate((0, 2, 4, 6)):
+
+            @pl.when(g == at)
+            def _(k=k):
+                ar1.step(k + 1)
+
+    for n in range(3):
+        a2_buf[n * CR : (n + 1) * CR, :] = d_qkv[:, n * CP : (n + 1) * CP].astype(bf16)
+    norms = jnp.sum(d_norm[...].reshape(4, 8, CP), axis=1)
+    small = jnp.concatenate([norms, table_sum(d_rel[...]), jnp.zeros((4, CP), f32)], axis=0)
+    a2_buf[A2_SMALL : A2_SMALL + 16, :] = small.astype(bf16)
+    ar2.step(0)
+
+    def grad_rows(band):
+        from_win(fgrad, band)
+
+        @pl.loop(0, 8)
+        def _(y):
+            r = band * 8 + y
+            pos = r + 1 + jnp.where(r >= 12, 2, 0)
+            v = xband[y] + gcat[row_at(pos), CP : 2 * CP].astype(f32)
+            io2[r] = jnp.where(col_in_p, v, 0.0)[:, 0:C].astype(bf16)
 
     def conv_rows(lo, hi):
         @pl.loop(lo, hi)
@@ -566,93 +671,25 @@
             out = out[:, 0:C] + io2[r + 4].astype(f32)
             io1[r] = jnp.where(col_in, out, 0.0).astype(bf16)
 
-    tmp[...] = jnp.zeros_like(tmp)
     conv_rows(12, 16)
     send_res = remote(io1.at[pl.ds(12, 4)], res_out.at[pl.ds(0, 4)], down, 4)
     send_res.start()
-    conv_rows(0, 6)
-    ar1.step(1)
-    conv_rows(6, 12)
-    ar1.step(2)
+    ar1.step(5)
+    ar2.step(1)
+    conv_rows(0, 8)
+    ar2.step(2)
+    ar1.step(6)
+    conv_rows(8, 12)
     store_res = pltpu.make_async_copy(io1.at[pl.ds(0, 12)], res_out.at[pl.ds(4, 12)], lsem.at[2])
     store_res.start()
-
-    @pl.loop(0, 8)
-    def _(g):
-        gs = pl.ds(pl.multiple_of(g * 512, 512), 512)
-
-        @pl.loop(0, 8, unroll=4)
-        def _(i):
-            rs = win_rows(g * 8 + i)
-            q = qkv[rs, 0:CP]
-            k = qkv[rs, CP : 2 * CP]
-            v = qkv[rs, 2 * CP : 3 * CP]
-            dobd = spread_heads(do_buf[rs, :])
-            dp = dot(v, dobd, 1, 1)
-            pb = probs[rs, :]
-            p = pb.astype(f32)
-            ds = p * (dp - jnp.sum(p * dp, axis=0, keepdims=True))
-            dsb = ds.astype(bf16)
-            d_rel[...] += dsb.astype(f32)
-            dv = dot(pb, dobd)
-            dk = dot(dsb, spread_heads(q)) * SCALE
-            dq = gather_heads(dot(dsb, k, 0, 0)) * SCALE
-            qkv[rs, 0:CP] = dq.astype(bf16)
-            qkv[rs, CP : 2 * CP] = dk.astype(bf16)
-            qkv[rs, 2 * CP : 3 * CP] = dv.astype(bf16)
-
-        d_qkv[...] += dot(normed[gs, 0:CR], qkv[gs, :], 0, 0)
-
-        @pl.loop(0, 512 // RM)
-        def _(j):
-            rs = pl.ds(pl.multiple_of(g * 512 + j * RM, RM), RM)
-            dn1 = dot(qkv[rs, :], wqkv[...], 1, 1).astype(bf16).astype(f32)
-            xhat = xhat1[rs, :].astype(f32)
-            d_norm[16:24, :] += fold8(dn1 * xhat)
-            d_norm[24:32, :] += fold8(dn1)
-            fgrad[rs, :] = fgrad[rs, :] + ln_bwd(dn1, xhat, xhat[:, 200:201] + xhat[:, 201:202], vec(0, CP))
-
-        @pl.when(g == 0)
-        def _():
-            ar1.step(3)
-
-        @pl.when(g == 1)
-        def _():
-            ar1.step(4)
-
-        @pl.when(g == 3)
-        def _():
-            ar1.step(5)
-
-        @pl.when(g == 5)
-        def _():
-            ar1.step(6)
-
-    for n in range(3):
-        a2_buf[n * CR : (n + 1) * CR, :] = d_qkv[:, n * CP : (n + 1) * CP].astype(bf16)
-    norms = jnp.sum(d_norm[...].reshape(4, 8, CP), axis=1)
-    small = jnp.concatenate([norms, table_sum(d_rel[...]), jnp.zeros((4, CP), f32)], axis=0)
-    a2_buf[A2_SMALL : A2_SMALL + 16, :] = small.astype(bf16)
-    ar2.step(0)
-
-    def grad_rows(band):
-        from_win(fgrad, band)
-
-        @pl.loop(0, 8)
-        def _(y):
-            r = band * 8 + y
-            pos = r + 1 + jnp.where(r >= 12, 2, 0)
-            v = xband[y] + gcat[row_at(pos), CP : 2 * CP].astype(f32)
-            io2[r] = jnp.where(col_in_p, v, 0.0)[:, 0:C].astype(bf16)
-
     grad_rows(1)
     send_ig = remote(io2.at[pl.ds(12, 4)], ig_out.at[pl.ds(0, 4)], down, 5)
     send_ig.start()
-    ar2.step(1)
+    ar2.step(3)
     grad_rows(0)
     store_ig = pltpu.make_async_copy(io2.at[pl.ds(0, 12)], ig_out.at[pl.ds(4, 12)], lsem.at[3])
     store_ig.start()
-    ar2.step(2)
+    ar2.step(5)
 
     for a in range(3):
         for b in range(3):
@@ -661,19 +698,25 @@
     o_fc1[:, 0:CP] = a1_out[A1_FC1 : A1_FC1 + CR, :].astype(f32)[0:C, :]
     o_fc1[:, CP:HID] = a1_out[A1_FC1 + CR : A1_FC1 + 2 * CR, :].astype(f32)[0:C, 0 : HID - CP]
     o_fc2[...] = a1_out[A1_FC2 : A1_FC2 + FC2_ROWS, :].astype(f32)[0:HID, 0:C]
-    o_proj[...] = a1_out[A1_PROJ : A1_PROJ + CR, :].astype(f32)[0:C, 0:C]
+    for h in range(HEADS):
+        at = A1_PROJ + h * HP_DIM
+        o_proj[h * HEAD_DIM : (h + 1) * HEAD_DIM, :] = a1_out[at : at + HP_DIM, :].astype(f32)[
+            0:HEAD_DIM, 0:C
+        ]
     o_vec[0:8, :] = a1_out[A1_FC1 + 176 : A1_FC1 + 192, :].astype(f32)[0:8]
     o_vec[8:16, :] = a1_out[A1_FC1 + CR + 176 : A1_FC1 + CR + 192, :].astype(f32)[0:8]
     o_vec[16:24, :] = a1_out[A1_FC2 + 352 : A1_FC2 + 368, :].astype(f32)[8:16]
-    o_vec[24:32, :] = a1_out[A1_PROJ + 176 : A1_PROJ + 192, :].astype(f32)[0:8]
+    o_vec[24:32, :] = a1_out[A1_PROJ + 16 : A1_PROJ + 32, :].astype(f32)[8:16]
     o_vec[32:40, :] = a1_out[4 * CR + 176 : 4 * CR + 192, :].astype(f32)[0:8]
-    ar2.step(3)
-    ar2.step(5)
     ar2.step(6)
+    wide = lax.broadcasted_iota(jnp.int32, (CP, CP), 0)
+    dense = lax.broadcasted_iota(jnp.int32, (CP, CP), 1)
+    heads_out = (wide == dense + lax.div(dense, HEAD_DIM) * (HP_DIM - HEAD_DIM)) & (dense < C)
+    heads_out = heads_out.astype(bf16)
     for n in range(3):
-        o_qkv[:, n * C : (n + 1) * C] = a2_out[n * CR : (n + 1) * CR, :].astype(f32)[0:C, 0:C]
-    o_vec[40:48, :] = a2_out[176:192, :].astype(f32)[0:8]
-    o_vec[48:56, :] = a2_out[2 * CR + 176 : 2 * CR + 192, :].astype(f32)[0:8]
+        o_qkv[:, n * C : (n + 1) * C] = dot(a2_out[n * CR : (n + 1) * CR, :], heads_out)[0:C, 0:C]
+    o_vec[40:48, :] = dot(a2_out[176:192, :], heads_out)[0:8]
+    o_vec[48:56, :] = dot(a2_out[2 * CR + 176 : 2 * CR + 192, :], heads_out)[0:8]
     o_vec[56:72, :] = a2_out[A2_SMALL : A2_SMALL + 16, :].astype(f32)
     send_res.wait()
     send_ig.wait()
@@ -778,10 +821,6 @@
             V((4096, 3 * CP), bf16),
             V((4096, HI), bf16),
             V((512, CP), bf16),
-            V((512, CP), f32),
-            V((512, CP), bf16),
-            V((512, HP), bf16),
-            V((512, HP), bf16),
             V((4096, CP), f32),
             V((4096, CP), f32),
             V((4096, CP), bf16),
@@ -815,8 +854,10 @@
 def prepare(norm1_gain, norm1_bias, qkv_weight, qv_bias, bias_table, proj_weight, proj_bias,
             norm2_gain, norm2_bias, fc1_weight, fc1_bias, fc2_weight, fc2_bias, conv_weight, conv_bias):
     pc = CP - C
-    wqkv = jnp.pad(qkv_weight.reshape(C, 3, C), ((0, pc), (0, 0), (0, pc))).reshape(CP, 3 * CP)
-    wproj = jnp.pad(proj_weight, ((0, pc), (0, pc)))
+    hp = HP_DIM - HEAD_DIM
+    wqkv = jnp.pad(qkv_weight.reshape(C, 3, HEADS, HEAD_DIM), ((0, pc), (0, 0), (0, 2), (0, hp)))
+    wqkv = wqkv.reshape(CP, 3 * CP)
+    wproj = jnp.pad(proj_weight.reshape(HEADS, HEAD_DIM, C), ((0, 2), (0, hp), (0, pc))).reshape(CP, CP)
     wfc1 = jnp.pad(fc1_weight, ((0, pc), (0, HP - HID)))
     wfc2 = jnp.pad(fc2_weight, ((0, HP - HID), (0, pc)))
     wconv = jnp.pad(conv_weight.transpose(0, 2, 1, 3), ((0, 0), (0, pc), (0, 0), (0, pc)))
@@ -827,7 +868,8 @@
         return jnp.pad(v, (0, 3 * CP - v.shape[0]))
 
     zero = jnp.zeros((C,), f32)
-    qkvb = jnp.pad(jnp.stack([qv_bias[:C], zero, qv_bias[C:]]), ((0, 0), (0, pc))).reshape(-1)
+    qkvb = jnp.stack([qv_bias[:C], zero, qv_bias[C:]]).reshape(3, HEADS, HEAD_DIM)
+    qkvb = jnp.pad(qkvb, ((0, 0), (0, 2), (0, hp))).reshape(-1)
     vecs = jnp.stack(
         [row(norm1_gain), row(norm1_bias, True), qkvb, row(proj_bias), row(norm2_gain),
          row(norm2_bias, True), row(fc1_bias), row(fc2_bias, True), row(conv_bias)]
@@ -861,7 +903,7 @@
         jnp.concatenate([v[44, :C], v[52, :C]]),
         v[60 : 60 + HEADS, :225].T,
         g_proj,
-        v[28, :C],
+        v[30, :C],
         v[56, :C],
         v[57, :C],
         g_fc1,

time: 211 us -> 159 us (0.75)
  Pallas kernels: 167 us -> 114 us
    pallas_call x1, Pallas kernels: 167 us -> 114 us  [run_layer(): pl.pallas_call(functools.partial(layer_kernel, chips, imgs, piece1, piece...]
    unnamed x44 -> x40, local copies, waits for them, and re-layouts: 17.3 us -> 17.2 us
where the time goes in v3:
time: 159 us; the launch traced here: 158 us
  Pallas kernels  114 us (72%)
  local copies, waits for them, and re-layouts  33.5 us (21%)
  matrix products  5.84 us (4%)
  other arithmetic  3.62 us (2%)
    pallas_call x1, Pallas kernels, run_layer(): pl.pallas_call(functools.partial(layer_kernel, chips, imgs, piece1, piece...  114 us
    unnamed x40, local copies, waits for them, and re-layouts  17.2 us
    dot_general x1, matrix products, score_extra(): rel = jnp.dot(hot, bias_table, precision=lax.Precision.HIGHEST)  5.84 us
    pad x8, local copies, waits for them, and re-layouts, row(): return jnp.pad(v, (0, 3 * CP - v.shape[0]))  3.43 us

profile of v3, /device:TPU:0, one launch (start us, length us, event | category | flops | bytes accessed | tf_op | source)
XLA Modules:
  0.0 158.5 jit_solution(6284084083529910125)
XLA Ops:
  1.4 0.8 pad_maximum_fusion.5
  2.2 0.8 fusion.1
  3.0 0.8 pad_maximum_fusion.3
  4.1 0.7 pad.56
  4.8 0.7 pad.59
  5.5 0.7 pad.60
  6.2 0.7 pad.62
  6.9 0.7 pad.64
  7.6 1.3 stack.55.vecs
  8.9 0.9 reshape.83
  9.8 0.7 pad.52
  10.5 5.8 %fusion.2 = f32[4096,6]{0,1:T(8,128)S(1)} fusion(f32[4096,225]{1,0:T(8,128)} %constant.24.clone, f32[225,6]{0,1:T(8,128)S(1)} %copy-done), kind=kOutput, calls=%fused_computation.12 | convolution fusion | flops 66355200 | bytes 3790104 | tf_op jit(solution)/shard_map/dot_general | solution.py:760
  16.9 0.7 pad.54.wfc2
  17.6 0.7 pad.53.wfc1
  18.6 0.9 copy.51.wqkv
  19.5 0.8 add_multiply_fusion.extra
  20.3 0.8 copy.49
  21.3 1.5 copy.52.wconv
  22.8 2.6 %copy.45 = bf16[1,16,256,180]{3,2,1,0:T(8,128)(2,1)} copy(bf16[1,16,256,180]{2,1,3,0:T(8,128)(2,1)S(1)} %copy-done.3) | data formatting | bytes 2949120 | tf_op args[0]
  25.4 2.6 %copy.46 = bf16[1,16,256,180]{3,2,1,0:T(8,128)(2,1)} copy(bf16[1,16,256,180]{2,1,3,0:T(8,128)(2,1)S(1)} %copy-done.4) | data formatting | bytes 2949120 | tf_op args[17]
  28.0 114.0 %layer.1 = (bf16[16,256,180]{2,1,0:T(8,128)(2,1)}, bf16[16,256,180]{2,1,0:T(8,128)(2,1)}, f32[180,540]{1,0:T(8,128)}, f32[180,180]{1,0:T(8,128)}, f32[180,360]{1...) custom-call(s32[1]{0:T(128)S(6)} %div.18.scal, bf16[16,256,180]{2,1,0:T(8,128)(2,1)} %bitcast.32, ...), custom_call_target="tpu_custom_call" | custom-call | tf_op jit(solution)/shard_map/layer/pallas_call | solution.py:791
  142.0 4.3 %copy.53 = bf16[1,16,256,180]{2,1,3,0:T(8,128)(2,1)} copy(bf16[1,16,256,180]{3,2,1,0:T(8,128)(2,1)} %bitcast.37) | data formatting | bytes 2949120
  146.3 2.4 %copy.54 = bf16[1,16,256,180]{2,1,3,0:T(8,128)(2,1)} copy(bf16[1,16,256,180]{3,2,1,0:T(8,128)(2,1)S(1)} %bitcast.36) | data formatting | bytes 2949120
  148.7 0.8 slice_bitcast_fusion.1
  149.5 0.7 slice.64
  150.8 1.3 slice_bitcast_fusion
  152.1 1.5 fusion
  154.2 0.9 copy.55
  155.1 0.8 copy.63
  155.9 0.7 copy.64
  156.6 0.7 copy.65
  157.3 1.2 copy.66
  (58 shorter events, 2.7 us)
Async XLA Ops:
  0.7 9.8 %copy-start = (f32[225,6]{0,1:T(8,128)S(1)}, f32[225,6]{0,1:T(8,128)}, u32[]{:S(2)}) copy-start(f32[225,6]{0,1:T(8,128)} %param.26) | copy-start | bytes 16204
  10.5 6.2 %copy-start.12 = (bf16[360,180]{0,1:T(8,128)(2,1)S(1)}, bf16[360,180]{0,1:T(8,128)(2,1)}, u32[]{:S(2)}) copy-start(bf16[360,180]{0,1:T(8,128)(2,1)} %param.33) | copy-start | bytes 388804
  10.5 7.1 %copy-start.13 = (bf16[180,360]{1,0:T(8,128)(2,1)S(1)}, bf16[180,360]{1,0:T(8,128)(2,1)}, u32[]{:S(2)}) copy-start(bf16[180,360]{1,0:T(8,128)(2,1)} %param.31) | copy-start | bytes 388804
  16.3 1.9 %copy-start.10 = (bf16[180,540]{1,0:T(8,128)(2,1)S(1)}, bf16[180,540]{1,0:T(8,128)(2,1)}, u32[]{:S(2)}) copy-start(bf16[180,540]{1,0:T(8,128)(2,1)} %param.24) | copy-start | bytes 583204
  16.6 2.9 %copy-start.7 = (f32[4,64,384]{2,1,0:T(8,128)S(1)}, f32[4,64,384]{2,1,0:T(8,128)}, u32[]{:S(2)}) copy-start(f32[4,64,384]{2,1,0:T(8,128)} %constant.25.clone) | copy-start | bytes 1179652
  16.8 3.5 %copy-start.5 = (bf16[3,3,180,180]{3,2,1,0:T(8,128)(2,1)S(1)}, bf16[3,3,180,180]{3,2,1,0:T(8,128)(2,1)}, u32[]{:S(2)}) copy-start(bf16[3,3,180,180]{3,2,1,0:T(8,128)(2,1)} %param.35) | copy-start | bytes 1749604
  21.1 1.7 %copy-start.3 = (bf16[1,16,256,180]{2,1,3,0:T(8,128)(2,1)S(1)}, bf16[1,16,256,180]{2,1,3,0:T(8,128)(2,1)}, u32[]{:S(2)}) copy-start(bf16[1,16,256,180]{2,1,3,0:T(8,128)(2,1)} %param.20) | copy-start | bytes 4423684
  22.8 2.6 %copy-start.4 = (bf16[1,16,256,180]{2,1,3,0:T(8,128)(2,1)S(1)}, bf16[1,16,256,180]{2,1,3,0:T(8,128)(2,1)}, u32[]{:S(2)}) copy-start(bf16[1,16,256,180]{2,1,3,0:T(8,128)(2,1)} %param.37) | copy-start | bytes 4423684
  142.0 4.3 %copy-start.1 = (bf16[16,256,180]{2,1,0:T(8,128)(2,1)S(1)}, bf16[16,256,180]{2,1,0:T(8,128)(2,1)}, u32[]{:S(2)}) copy-start(bf16[16,256,180]{2,1,0:T(8,128)(2,1)} %get-tuple-element.26) | copy-start | bytes 4423684
  146.3 8.0 %copy-start.8 = (f32[360,180]{1,0:T(8,128)S(1)}, f32[360,180]{1,0:T(8,128)}, u32[]{:S(2)}) copy-start(f32[360,180]{1,0:T(8,128)} %get-tuple-element.63) | copy-start | bytes 777604
  146.3 8.8 %copy-start.6 = (f32[180,540]{1,0:T(8,128)S(1)}, f32[180,540]{1,0:T(8,128)}, u32[]{:S(2)}) copy-start(f32[180,540]{1,0:T(8,128)} %get-tuple-element.101) | copy-start | bytes 1166404
  146.3 9.6 %copy-start.11 = (f32[180,180]{1,0:T(8,128)S(1)}, f32[180,180]{1,0:T(8,128)}, u32[]{:S(2)}) copy-start(f32[180,180]{1,0:T(8,128)} %get-tuple-element.104) | copy-start | bytes 388804
  146.3 10.3 %copy-start.9 = (f32[180,360]{1,0:T(8,128)S(1)}, f32[180,360]{1,0:T(8,128)}, u32[]{:S(2)}) copy-start(f32[180,360]{1,0:T(8,128)} %get-tuple-element.108) | copy-start | bytes 777604
  148.7 8.6 %copy-start.2 = (f32[3,3,180,180]{3,2,1,0:T(8,128)S(1)}, f32[3,3,180,180]{3,2,1,0:T(8,128)}, u32[]{:S(2)}) copy-start(f32[3,3,180,180]{3,2,1,0:T(8,128)} %get-tuple-element.112) | copy-start | bytes 3499204

commit v4 on v3

--- a/solution.py
+++ b/solution.py
@@ -22,13 +22,12 @@
 SCALE = HEAD_DIM ** (-0.5)
 
 CR = 192
-FC2_ROWS = 368
-A1_FC1 = 9 * CR
-A1_FC2 = A1_FC1 + 2 * CR
-A1_PROJ = A1_FC2 + FC2_ROWS
-A1_USED = A1_PROJ + CR
-A2_SMALL = 3 * CR
-A2_USED = A2_SMALL + 16
+A_USED = 5 * CR
+B_SMALL = 5 * CR
+B_USED = B_SMALL + 32
+C_MIX = 9 * CR
+C_FC1 = C_MIX + 5 * CR
+C_USED = C_FC1 + 2 * CR
 
 f32 = jnp.float32
 bf16 = jnp.bfloat16
@@ -125,6 +124,9 @@
 
 def column_masks(width):
     return rows_of((256, CP)) < width
+
+
+TURNS = ((1, (("a", 2), ("c", 1))), (2, (("a", 3),)), (5, (("c", 2), ("a", 4))))
 
 
 class AllReduce:
@@ -257,26 +259,37 @@
 def layer_kernel(
     chips,
     imgs,
-    piece1,
-    piece2,
+    pieces,
     scal,
     img,
     cot,
+    r_qkv,
+    r_proj,
+    r_fc1,
+    r_fc2t,
+    r_conv,
+    r_table,
+    r_n1g,
+    r_n1b,
+    r_qvb,
+    r_pb,
+    r_n2g,
+    r_n2b,
+    r_f1b,
+    r_f2b,
+    r_cb,
+    res_out,
+    ig_out,
+    a_out,
+    b_out,
+    c_out,
     wqkv,
     wproj,
     wfc1,
-    wfc2,
+    wfc2t,
     wconv,
     vecs,
     extra,
-    res_out,
-    ig_out,
-    o_qkv,
-    o_proj,
-    o_fc1,
-    o_fc2,
-    o_conv,
-    o_vec,
     d_qkv,
     d_proj,
     d_fc1,
@@ -298,38 +311,45 @@
     winf,
     fgrad,
     do_buf,
+    ig_rows,
     edge,
     tmp,
-    a1_buf,
-    a1_out,
-    a1_r1,
-    a1_r2,
-    a1_r3,
-    a2_buf,
-    a2_out,
-    a2_r1,
-    a2_r2,
-    a2_r3,
+    a_buf,
+    a_r1,
+    a_r2,
+    a_r3,
+    b_buf,
+    b_r1,
+    b_r2,
+    b_r3,
+    c_buf,
+    c_r1,
+    c_r2,
+    c_r3,
     lsem,
     hs,
     hr,
-    a1_s,
-    a1_r,
-    a2_s,
-    a2_r,
+    a_s,
+    a_r,
+    b_s,
+    b_r,
+    c_s,
+    c_r,
 ):
     stripes = 2 * chips
     rank = lax.axis_index("rows")
     core = lax.rem(rank, 2)
     up = lax.rem(rank + stripes - 1, stripes)
     down = lax.rem(rank + 1, stripes)
-    ar1 = AllReduce(a1_buf, a1_out, a1_r1, a1_r2, a1_r3, a1_s, a1_r, piece1, chips, imgs, True)
-    ar2 = AllReduce(a2_buf, a2_out, a2_r1, a2_r2, a2_r3, a2_s, a2_r, piece2, chips, imgs, False)
+    pa, pb, pc = pieces
+    ara = AllReduce(a_buf, a_out, a_r1, a_r2, a_r3, a_s, a_r, pa, chips, imgs, True)
+    arb = AllReduce(b_buf, b_out, b_r1, b_r2, b_r3, b_s, b_r, pb, chips, imgs, False)
+    arc = AllReduce(c_buf, c_out, c_r1, c_r2, c_r3, c_s, c_r, pc, chips, imgs, True)
 
     barrier = pltpu.get_barrier_semaphore()
     peers = [{"rows": up}, {"rows": down}]
     peers += [{"rows": lax.rem(rank + 2 * d, stripes)} for d in range(1, chips)]
-    peers += [{"imgs": lax.rem(ar1.z + d, imgs)} for d in range(1, imgs)]
+    peers += [{"imgs": lax.rem(ara.z + d, imgs)} for d in range(1, imgs)]
     for peer in peers:
         pl.semaphore_signal(barrier, inc=1, device_id=peer, device_id_type=pl.DeviceIdType.MESH)
     pl.semaphore_wait(barrier, len(peers))
@@ -366,12 +386,12 @@
     def row_at(pos, count=1):
         return pl.ds(pl.multiple_of(pos * 256, 256), count * 256)
 
-    xband[:, :, 128:256] = jnp.zeros((8, 256, 128), f32)
     tmp[...] = jnp.zeros_like(tmp)
     for ref in (d_qkv, d_proj, d_fc1, d_fc2, d_conv, d_norm, d_rel):
         ref[...] = jnp.zeros_like(ref)
-    a1_buf[A1_USED:, :] = jnp.zeros((a1_buf.shape[0] - A1_USED, CP), bf16)
-    a2_buf[A2_USED:, :] = jnp.zeros((a2_buf.shape[0] - A2_USED, CP), bf16)
+    for ref, size in ((a_buf, A_USED), (b_buf, B_USED), (c_buf, C_USED)):
+        if ref.shape[0] > size:
+            ref[size:, :] = jnp.zeros((ref.shape[0] - size, 128), bf16)
 
     col_in = rows_of((256, C)) < width
     col_in_p = rows_of((256, CP)) < width
@@ -384,6 +404,42 @@
         gcat[at, CP : 2 * CP] = tmp[8:264, :].astype(bf16)
         gcat[at, 2 * CP : 3 * CP] = tmp[7:263, :].astype(bf16)
 
+    def iota(shape, dim):
+        return lax.broadcasted_iota(jnp.int32, shape, dim)
+
+    def padded(v):
+        return jnp.concatenate([v.astype(f32), jnp.zeros((CR - C, v.shape[1]), f32)], axis=0).astype(bf16)
+
+    for ref in (wqkv, wproj, wfc1, wfc2t, wconv, vecs):
+        ref[...] = jnp.zeros_like(ref)
+    part = iota((3 * C, 3 * CP), 1)
+    lane = part & (CP - 1)
+    place = (part >> 8) * C + (lane >> 5) * HEAD_DIM + (lane & 31)
+    used = ((lane & 31) < HEAD_DIM) & (lane < HEADS * HP_DIM)
+    spread = (used & (iota((3 * C, 3 * CP), 0) == place)).astype(bf16)
+    wqkv[0:CR, :] = padded(dot(r_qkv[...], spread))
+    lane = iota((CP, C), 0)
+    place = (lane >> 5) * HEAD_DIM + (lane & 31)
+    used = ((lane & 31) < HEAD_DIM) & (lane < HEADS * HP_DIM)
+    wproj[:, 0:C] = dot((used & (iota((CP, C), 1) == place)).astype(bf16), r_proj[...]).astype(bf16)
+    wfc1[0:CR, 0:HID] = padded(r_fc1[...])
+    wfc2t[0:CR, 0:HID] = padded(r_fc2t[...])
+    for a in range(3):
+        for b in range(3):
+            wconv[a, 0:CR, b * CP : b * CP + C] = padded(r_conv[a, b])
+    for n, ref in ((0, r_n1g), (1, r_n1b), (3, r_pb), (4, r_n2g), (5, r_n2b), (6, r_f1b), (7, r_f2b), (8, r_cb)):
+        vecs[n : n + 1, 0 : ref.shape[0]] = ref[...].reshape(1, ref.shape[0])
+    for n in (1, 5, 7):
+        vecs[n : n + 1, C : C + 1] = jnp.ones((1, 1), f32)
+    qvb = r_qvb[...].reshape(1, 2 * C)
+    for h in range(HEADS):
+        at = h * HP_DIM
+        vecs[2:3, at : at + HEAD_DIM] = qvb[:, h * HEAD_DIM : (h + 1) * HEAD_DIM]
+        vecs[2:3, 2 * CP + at : 2 * CP + at + HEAD_DIM] = qvb[
+            :, C + h * HEAD_DIM : C + (h + 1) * HEAD_DIM
+        ]
+    score_terms(r_table[...], extra)
+
     load_cot.wait()
 
     @pl.loop(0, 13)
@@ -435,6 +491,8 @@
             @pl.loop(0, 5)
             def _(r):
                 put_g(15 + r, io1[16 + r], 1.0)
+
+        xband[:, :, 128:256] = jnp.zeros((8, 256, 128), f32)
 
         @pl.loop(0, 8)
         def _(y):
@@ -458,7 +516,7 @@
 
             xs = [to_win(xband, k0 + w) for w in range(8)]
             for w in range(8):
-                winf[win_rows(g * 8 + w), :] = xs[w]
+                winf[win_rows(gg * 8 + w), :] = xs[w]
                 fgrad[win_rows(g * 8 + w), :] = to_win(gband, k0 + w)
                 xhat, rs_, ln_out = ln_fwd(xs[w], vec(0, CP), vec(1, CP))
                 xhat1[win_rows(g * 8 + w), :] = with_rstd(xhat, rs_).astype(bf16)
@@ -498,8 +556,9 @@
 
             parts = range(0, 512, 256)
             at_rows = [pl.ds(pl.multiple_of(g * 512 + r, 256), 256) for r in parts]
+            in_band = [pl.ds(pl.multiple_of(gg * 512 + r, 256), 256) for r in parts]
             mixes = [mixed[r : r + 256, :] for r in parts]
-            firsts = [dot(m, wproj[...]) + vec(3, CP) + winf[rs, :] for m, rs in zip(mixes, at_rows)]
+            firsts = [dot(m, wproj[...]) + vec(3, CP) + winf[rs, :] for m, rs in zip(mixes, in_band)]
 
             def norm2(v):
                 xhat, rs_, ln_out = ln_fwd(v, vec(4, CP), vec(5, CP))
@@ -512,12 +571,12 @@
             norms = [by_rows(norm2, 64, v) for v in firsts]
             n2s = [n[2] for n in norms]
             acts = [by_rows(activate, 64, dot(n2, wfc1[...])) for n2 in n2s]
-            for fs, (ac, dg), rs in zip(firsts, acts, at_rows):
-                winf[rs, :] = fs + dot(ac, wfc2[...]) + vec(7, CP)
+            for fs, (ac, dg), rs in zip(firsts, acts, in_band):
+                winf[rs, :] = fs + dot(ac, wfc2t[...], 1, 1) + vec(7, CP)
             lgs = [fgrad[rs, :] for rs in at_rows]
             mgs = [lg.astype(bf16) for lg in lgs]
             hgs = [
-                (dot(mg, wfc2[...], 1, 1).astype(bf16).astype(f32) * dg.astype(f32)).astype(bf16)
+                (dot(mg, wfc2t[...]).astype(bf16).astype(f32) * dg.astype(f32)).astype(bf16)
                 for mg, (ac, dg) in zip(mgs, acts)
             ]
             dns = [dot(hg, wfc1[...], 1, 1).astype(bf16) for hg in hgs]
@@ -538,13 +597,12 @@
             d_norm[8:16, :] += added([fold8(b[3]) for b in backs])
             join = lambda vs: jnp.concatenate(vs, axis=0)
             mg = join(mgs)
-            d_fc2[...] += dot(join([ac for ac, dg in acts])[:, 0:FC2_ROWS], mg, 0, 0)
+            d_fc2[...] += dot(mg[:, 0:CR], join([ac for ac, dg in acts]), 0, 0)
+            d_norm[32:40, :] += fold8(mg.astype(f32))
             d_fc1[...] += dot(join(n2s)[:, 0:CR], join(hgs), 0, 0)
             d_proj[...] += dot(mixed[:, 0:CR], join(ats), 0, 0)
 
-    @pl.loop(0, 2)
-    def _(band):
-        from_win(winf, band)
+        from_win(winf, 0)
 
         @pl.loop(0, 8)
         def _(y):
@@ -566,30 +624,76 @@
         for a in range(3):
             d_conv[a] += dot(llbuf[row_at(start + a - 1, 4), 0:CR], gs, 0, 0)
 
+    low_lanes = lanes((1, 128)) < 64
+
+    def mix(p, q):
+        return jnp.where(low_lanes, p, pltpu.roll(q, 64, 1)).astype(bf16)
+
+    a_buf[0:CR, :] = d_fc1[:, CP:HP].astype(bf16)
+    for n in range(3):
+        a_buf[(n + 1) * CR : (n + 2) * CR, :] = d_fc2[:, n * 128 : (n + 1) * 128].astype(bf16)
+    a_buf[4 * CR : 5 * CR, :] = d_proj[:, 0:128].astype(bf16)
+    ara.step(0)
+
     @pl.loop(1, 3)
     def _(n):
         wgrad_rows(n)
 
     send_up.wait()
     send_down.wait()
+    ara.step(1)
 
     @pl.loop(0, 2)
     def _(n):
         wgrad_rows(n * 3)
 
+    tails = []
     for a in range(3):
         for b in range(3):
             at = (a * 3 + b) * CR
-            a1_buf[at : at + CR, :] = d_conv[a, :, b * CP : (b + 1) * CP].astype(bf16)
-    a1_buf[A1_FC1 : A1_FC1 + CR, :] = d_fc1[:, 0:CP].astype(bf16)
-    a1_buf[A1_FC1 + CR : A1_FC1 + 2 * CR, 0:128] = d_fc1[:, CP:HP].astype(bf16)
-    a1_buf[A1_FC1 + CR : A1_FC1 + 2 * CR, 128:256] = jnp.zeros((CR, 128), bf16)
-    a1_buf[A1_FC2 : A1_FC2 + FC2_ROWS, :] = d_fc2[...].astype(bf16)
-    a1_buf[A1_PROJ : A1_PROJ + CR, :] = d_proj[...].astype(bf16)
-    ar1.step(0)
+            c_buf[at : at + CR, :] = d_conv[a, :, b * CP : b * CP + 128].astype(bf16)
+            tails.append((d_conv, a, slice(b * CP + 128, (b + 1) * CP)))
+    tails = [ref[a, :, ln] for ref, a, ln in tails] + [d_proj[:, 128:256]]
+    for n in range(5):
+        at = C_MIX + n * CR
+        c_buf[at : at + CR, :] = mix(tails[2 * n], tails[2 * n + 1])
+    for n in range(2):
+        at = C_FC1 + n * CR
+        c_buf[at : at + CR, :] = d_fc1[:, n * 128 : (n + 1) * 128].astype(bf16)
+    arc.step(0)
+
+    def conv_rows(lo, hi):
+        @pl.loop(lo, hi)
+        def _(r):
+            pos = r + 1 + jnp.where(r >= 12, 2, 0)
+            acc = None
+            for a in range(3):
+                d = dot(llbuf[row_at(pos + a - 1), :], wconv[a])
+                acc = d if acc is None else acc + d
+            tmp[8:264, :] = acc[:, 0:CP]
+            tmp[280:536, :] = acc[:, 2 * CP : 3 * CP]
+            out = acc[:, CP : 2 * CP] + tmp[7:263, :] + tmp[281:537, :] + vec(8, CP)
+            out = out[:, 0:C] + io2[r + 4].astype(f32)
+            io1[r] = jnp.where(col_in, out, 0.0).astype(bf16)
+
+    def grad_rows(band):
+        from_win(fgrad, band)
+
+        @pl.loop(0, 8)
+        def _(y):
+            r = band * 8 + y
+            pos = r + 1 + jnp.where(r >= 12, 2, 0)
+            v = xband[y] + gcat[row_at(pos), CP : 2 * CP].astype(f32)
+            ig_rows[r] = jnp.where(col_in_p, v, 0.0)[:, 0:C].astype(bf16)
+
+    conv_rows(12, 16)
+    send_res = remote(io1.at[pl.ds(12, 4)], res_out.at[pl.ds(0, 4)], down, 4)
+    send_res.start()
+    send_ig = remote(ig_rows.at[pl.ds(12, 4)], ig_out.at[pl.ds(0, 4)], down, 5)
 
     @pl.loop(0, 8)
-    def _(g):
+    def _(turn):
+        g = lax.rem(turn + 4, 8)
         gs = pl.ds(pl.multiple_of(g * 512, 512), 512)
 
         i = 0
@@ -634,94 +738,125 @@
         d_norm[16:24, :] += fold8(back[1])
         d_norm[24:32, :] += fold8(back[2])
 
-        for k, at in enumerate((0, 2, 4, 6)):
-
-            @pl.when(g == at)
-            def _(k=k):
-                ar1.step(k + 1)
+        for at, steps in TURNS:
+
+            @pl.when(turn == at)
+            def _(steps=steps):
+                for which, k in steps:
+                    {"a": ara, "c": arc}[which].step(k)
+
+        @pl.when(turn == 3)
+        def _():
+            grad_rows(1)
+            send_ig.start()
 
     for n in range(3):
-        a2_buf[n * CR : (n + 1) * CR, :] = d_qkv[:, n * CP : (n + 1) * CP].astype(bf16)
-    norms = jnp.sum(d_norm[...].reshape(4, 8, CP), axis=1)
-    small = jnp.concatenate([norms, table_sum(d_rel[...]), jnp.zeros((4, CP), f32)], axis=0)
-    a2_buf[A2_SMALL : A2_SMALL + 16, :] = small.astype(bf16)
-    ar2.step(0)
-
-    def grad_rows(band):
-        from_win(fgrad, band)
-
-        @pl.loop(0, 8)
-        def _(y):
-            r = band * 8 + y
-            pos = r + 1 + jnp.where(r >= 12, 2, 0)
-            v = xband[y] + gcat[row_at(pos), CP : 2 * CP].astype(f32)
-            io2[r] = jnp.where(col_in_p, v, 0.0)[:, 0:C].astype(bf16)
-
-    def conv_rows(lo, hi):
-        @pl.loop(lo, hi)
-        def _(r):
-            pos = r + 1 + jnp.where(r >= 12, 2, 0)
-            acc = None
-            for a in range(3):
-                d = dot(llbuf[row_at(pos + a - 1), :], wconv[a])
-                acc = d if acc is None else acc + d
-            tmp[8:264, :] = acc[:, 0:CP]
-            tmp[280:536, :] = acc[:, 2 * CP : 3 * CP]
-            out = acc[:, CP : 2 * CP] + tmp[7:263, :] + tmp[281:537, :] + vec(8, CP)
-            out = out[:, 0:C] + io2[r + 4].astype(f32)
-            io1[r] = jnp.where(col_in, out, 0.0).astype(bf16)
-
-    conv_rows(12, 16)
-    send_res = remote(io1.at[pl.ds(12, 4)], res_out.at[pl.ds(0, 4)], down, 4)
-    send_res.start()
-    ar1.step(5)
-    ar2.step(1)
-    conv_rows(0, 8)
-    ar2.step(2)
-    ar1.step(6)
+        b_buf[n * CR : (n + 1) * CR, :] = d_qkv[:, n * CP : n * CP + 128].astype(bf16)
+    b_buf[3 * CR : 4 * CR, :] = mix(d_qkv[:, 128:256], d_qkv[:, CP + 128 : 2 * CP])
+    b_buf[4 * CR : 5 * CR, :] = mix(d_qkv[:, 2 * CP + 128 : 3 * CP], d_qkv[:, 2 * CP + 128 : 3 * CP])
+    sums = jnp.sum(d_norm[...].reshape(5, 8, CP), axis=1)
+    small = jnp.concatenate([table_sum(d_rel[...]), sums, jnp.zeros((3, CP), f32)], axis=0)
+    b_buf[B_SMALL : B_SMALL + 16, :] = small[:, 0:128].astype(bf16)
+    b_buf[B_SMALL + 16 : B_SMALL + 32, :] = small[:, 128:256].astype(bf16)
+    arb.step(0)
+    ara.step(5)
+    arc.step(3)
+    conv_rows(0, 4)
+    arb.step(1)
+    ara.step(6)
+    conv_rows(4, 8)
+    arc.step(4)
     conv_rows(8, 12)
     store_res = pltpu.make_async_copy(io1.at[pl.ds(0, 12)], res_out.at[pl.ds(4, 12)], lsem.at[2])
     store_res.start()
-    grad_rows(1)
-    send_ig = remote(io2.at[pl.ds(12, 4)], ig_out.at[pl.ds(0, 4)], down, 5)
-    send_ig.start()
-    ar2.step(3)
+    arb.step(2)
     grad_rows(0)
-    store_ig = pltpu.make_async_copy(io2.at[pl.ds(0, 12)], ig_out.at[pl.ds(4, 12)], lsem.at[3])
+    store_ig = pltpu.make_async_copy(ig_rows.at[pl.ds(0, 12)], ig_out.at[pl.ds(4, 12)], lsem.at[3])
     store_ig.start()
-    ar2.step(5)
-
+    arb.step(3)
+    arc.step(5)
+    arb.step(5)
+    arc.step(6)
+    arb.step(6)
+    send_res.wait()
+    send_ig.wait()
+    store_res.wait()
+    store_ig.wait()
+
+
+def finish_kernel(
+    a_ref, b_ref, c_ref, o_n1g, o_n1b, o_qkv, o_qvb, o_table, o_proj, o_pb, o_n2g, o_n2b, o_fc1, o_f1b, o_fc2t,
+    o_f2b, o_conv, o_cb,
+):
+    def block(ref, at, rows=CR):
+        return ref[at : at + rows, :].astype(f32)
+
+    def halves(v):
+        return v, pltpu.roll(v, 64, 1)
+
+    tails = []
+    for n in range(5):
+        tails += halves(block(c_ref, C_MIX + n * CR))
     for a in range(3):
         for b in range(3):
-            at = (a * 3 + b) * CR
-            o_conv[a, b] = a1_out[at : at + CR, :].astype(f32)[0:C, 0:C]
-    o_fc1[:, 0:CP] = a1_out[A1_FC1 : A1_FC1 + CR, :].astype(f32)[0:C, :]
-    o_fc1[:, CP:HID] = a1_out[A1_FC1 + CR : A1_FC1 + 2 * CR, :].astype(f32)[0:C, 0 : HID - CP]
-    o_fc2[...] = a1_out[A1_FC2 : A1_FC2 + FC2_ROWS, :].astype(f32)[0:HID, 0:C]
+            v = jnp.concatenate([block(c_ref, (a * 3 + b) * CR), tails[a * 3 + b]], axis=1)
+            o_conv[a, b] = v[0:C, 0:C]
+            if a == 1 and b == 1:
+                o_cb[...] = v[C : C + 1, 0:C].reshape(C)
+    fc1 = [block(c_ref, C_FC1), block(c_ref, C_FC1 + CR), block(a_ref, 0)]
+    fc1 = jnp.concatenate(fc1, axis=1)
+    o_fc1[...] = fc1[0:C, 0:HID]
+    o_f1b[...] = fc1[C : C + 1, 0:HID].reshape(HID)
+    fc2 = jnp.concatenate([block(a_ref, (n + 1) * CR) for n in range(3)], axis=1)
+    o_fc2t[...] = fc2[0:C, 0:HID]
+    proj = jnp.concatenate([block(a_ref, 4 * CR), tails[9]], axis=1)
     for h in range(HEADS):
-        at = A1_PROJ + h * HP_DIM
-        o_proj[h * HEAD_DIM : (h + 1) * HEAD_DIM, :] = a1_out[at : at + HP_DIM, :].astype(f32)[
-            0:HEAD_DIM, 0:C
-        ]
-    o_vec[0:8, :] = a1_out[A1_FC1 + 176 : A1_FC1 + 192, :].astype(f32)[0:8]
-    o_vec[8:16, :] = a1_out[A1_FC1 + CR + 176 : A1_FC1 + CR + 192, :].astype(f32)[0:8]
-    o_vec[16:24, :] = a1_out[A1_FC2 + 352 : A1_FC2 + 368, :].astype(f32)[8:16]
-    o_vec[24:32, :] = a1_out[A1_PROJ + 16 : A1_PROJ + 32, :].astype(f32)[8:16]
-    o_vec[32:40, :] = a1_out[4 * CR + 176 : 4 * CR + 192, :].astype(f32)[0:8]
-    ar2.step(6)
+        at = h * HP_DIM
+        o_proj[h * HEAD_DIM : (h + 1) * HEAD_DIM, :] = proj[at : at + HEAD_DIM, 0:C]
+    o_pb[...] = proj[HEAD_DIM : HEAD_DIM + 1, 0:C].reshape(C)
     wide = lax.broadcasted_iota(jnp.int32, (CP, CP), 0)
     dense = lax.broadcasted_iota(jnp.int32, (CP, CP), 1)
     heads_out = (wide == dense + lax.div(dense, HEAD_DIM) * (HP_DIM - HEAD_DIM)) & (dense < C)
     heads_out = heads_out.astype(bf16)
+    rest = halves(block(b_ref, 3 * CR)) + halves(block(b_ref, 4 * CR))
     for n in range(3):
-        o_qkv[:, n * C : (n + 1) * C] = dot(a2_out[n * CR : (n + 1) * CR, :], heads_out)[0:C, 0:C]
-    o_vec[40:48, :] = dot(a2_out[176:192, :], heads_out)[0:8]
-    o_vec[48:56, :] = dot(a2_out[2 * CR + 176 : 2 * CR + 192, :], heads_out)[0:8]
-    o_vec[56:72, :] = a2_out[A2_SMALL : A2_SMALL + 16, :].astype(f32)
-    send_res.wait()
-    send_ig.wait()
-    store_res.wait()
-    store_ig.wait()
+        v = jnp.concatenate([block(b_ref, n * CR), rest[n]], axis=1).astype(bf16)
+        v = dot(v, heads_out)
+        o_qkv[:, n * C : (n + 1) * C] = v[0:C, 0:C]
+        if n != 1:
+            o_qvb[n // 2 * C : (n // 2 + 1) * C] = v[C : C + 1, 0:C].reshape(C)
+    small = jnp.concatenate([block(b_ref, B_SMALL, 16), block(b_ref, B_SMALL + 16, 16)], axis=1)
+    o_table[...] = small[0:HEADS, 0 : o_table.shape[1]]
+    for n, ref in ((8, o_n2g), (9, o_n2b), (10, o_n1g), (11, o_n1b), (12, o_f2b)):
+        ref[...] = small[n : n + 1, 0:C].reshape(C)
+
+
+def score_terms(table, extra):
+    table = jnp.concatenate([table * LOG2E, jnp.zeros((2, table.shape[1]), f32)], axis=0)
+    table = jnp.concatenate([table, jnp.zeros((8, CP - table.shape[1]), f32)], axis=1)
+    shifted = [pltpu.roll(table, x, 1) if x else table for x in range(WIN)]
+    row = lax.broadcasted_iota(jnp.int32, (AREA, CP), 0)
+    lane = lax.broadcasted_iota(jnp.int32, (AREA, CP), 1)
+    put = (lane == row + (row >> 3) * (WIN - 1)).astype(bf16)
+    shape = (AREA, AREA)
+    j = lax.broadcasted_iota(jnp.int32, shape, 0)
+    i = lax.broadcasted_iota(jnp.int32, shape, 1)
+    rows_differ = ((j >> 5) & 1) != ((i >> 5) & 1)
+    cols_differ = ((j >> 2) & 1) != ((i >> 2) & 1)
+    masks = [None, cols_differ, rows_differ, rows_differ | cols_differ]
+    for h in range(HEADS):
+        base = jnp.concatenate([t[h : h + 1] for t in shifted], axis=0)
+        wide = jnp.concatenate(
+            [pltpu.roll(base, CP - (112 - 15 * y), 1) for y in range(WIN)], axis=0
+        )
+        high = wide.astype(bf16)
+        rest = wide - high.astype(f32)
+        mid = rest.astype(bf16)
+        low = (rest - mid.astype(f32)).astype(bf16)
+        term = dot(high, put, 1, 1) + dot(mid, put, 1, 1) + dot(low, put, 1, 1)
+        for n, mask in enumerate(masks):
+            value = term if mask is None else term + jnp.where(mask, -100.0 * LOG2E, 0.0)
+            extra[n, :, h * AREA : (h + 1) * AREA] = value
 
 
 def table_sum(d_rel):
@@ -747,28 +882,6 @@
     return out
 
 
-def relative_index():
-    coords = np.arange(AREA)
-    row, col = coords // WIN, coords % WIN
-    return (row[:, None] - row[None, :] + WIN - 1) * (2 * WIN - 1) + col[:, None] - col[None, :] + WIN - 1
-
-
-def score_extra(bias_table):
-    hot = jnp.asarray(
-        (relative_index().T.reshape(-1)[:, None] == np.arange(225)[None, :]).astype(np.float32)
-    )
-    rel = jnp.dot(hot, bias_table, precision=lax.Precision.HIGHEST)
-    rel = rel.reshape(AREA, AREA, HEADS).transpose(0, 2, 1).reshape(AREA, HI)
-    coords = np.arange(AREA)
-    yh = coords // WIN >= SHIFT
-    xh = coords % WIN >= SHIFT
-    ydiff = yh[:, None] != yh[None, :]
-    xdiff = xh[:, None] != xh[None, :]
-    masks = np.stack([np.zeros_like(ydiff), xdiff, ydiff, ydiff | xdiff])
-    masks = np.where(np.tile(masks, (1, 1, HEADS)), -100.0, 0.0).astype(np.float32)
-    return (rel[None] + jnp.asarray(masks)) * LOG2E
-
-
 VM = pl.BlockSpec(memory_space=pltpu.VMEM)
 SM = pl.BlockSpec(memory_space=pltpu.SMEM)
 HB = pl.BlockSpec(memory_space=pl.ANY)
@@ -778,37 +891,44 @@
     return (n + m - 1) // m * m
 
 
-def run_layer(stripes, imgs, scal, img, cot, wqkv, wproj, wfc1, wfc2, wconv, vecs, extra):
+def run_layer(stripes, imgs, *operands):
     S = jax.ShapeDtypeStruct
     V = pltpu.VMEM
     chips = stripes // 2
-    piece1 = up_to(-(-A1_USED // (stripes * imgs)), 16)
-    piece2 = up_to(-(-A2_USED // stripes), 16)
-    half1 = piece1 * imgs * chips
-    half2 = piece2 * chips
+    dma = pltpu.SemaphoreType.DMA
     sems = 2 * (chips + imgs - 1)
-    dma = pltpu.SemaphoreType.DMA
+    pieces, buffers, outs = [], [], []
+    for used, zsplit in ((A_USED, True), (B_USED, False), (C_USED, True)):
+        parts = stripes * imgs if zsplit else stripes
+        piece = up_to(-(-used // parts), 16)
+        group = piece * imgs if zsplit else piece
+        pieces.append(piece)
+        outs.append(S((stripes * group, 128), bf16))
+        buffers += [
+            V((stripes * group, 128), bf16),
+            V((chips * group, 128), bf16),
+            V(((chips - 1) * group, 128), bf16),
+            V(((imgs - 1) * piece, 128), bf16),
+        ]
     return pl.pallas_call(
-        functools.partial(layer_kernel, chips, imgs, piece1, piece2),
-        out_shape=(
-            S((16, 256, C), bf16),
-            S((16, 256, C), bf16),
-            S((C, 3 * C), f32),
-            S((C, C), f32),
-            S((C, HID), f32),
-            S((HID, C), f32),
-            S((3, 3, C, C), f32),
-            S((72, CP), f32),
-        ),
-        in_specs=[SM, HB, HB] + [VM] * 7,
-        out_specs=[HB] * 2 + [VM] * 6,
+        functools.partial(layer_kernel, chips, imgs, tuple(pieces)),
+        out_shape=(S((16, 256, C), bf16), S((16, 256, C), bf16), *outs),
+        in_specs=[SM, HB, HB] + [VM] * 15,
+        out_specs=[HB] * 2 + [VM] * 3,
         scratch_shapes=[
+            V((CP, 3 * CP), bf16),
+            V((CP, CP), bf16),
+            V((CP, HP), bf16),
+            V((CP, HP), bf16),
+            V((3, CP, 3 * CP), bf16),
+            V((16, 3 * CP), f32),
+            V((4, AREA, HI), f32),
             V((CR, 3 * CP), f32),
             V((CR, CP), f32),
             V((CR, HP), f32),
-            V((FC2_ROWS, CP), f32),
+            V((CR, HP), f32),
             V((3, CR, 3 * CP), f32),
-            V((32, CP), f32),
+            V((40, CP), f32),
             V((AREA, HI), f32),
             V((21, 256, C), bf16),
             V((20, 256, C), bf16),
@@ -821,61 +941,49 @@
             V((4096, 3 * CP), bf16),
             V((4096, HI), bf16),
             V((512, CP), bf16),
-            V((4096, CP), f32),
+            V((2048, CP), f32),
             V((4096, CP), f32),
             V((4096, CP), bf16),
+            V((16, 256, C), bf16),
             V((WIN, WIN, CP), f32),
             V((544, CP), f32),
-            V((2 * half1, CP), bf16),
-            V((2 * half1, CP), bf16),
-            V((half1, CP), bf16),
-            V(((chips - 1) * piece1 * imgs, CP), bf16),
-            V(((imgs - 1) * piece1, CP), bf16),
-            V((2 * half2, CP), bf16),
-            V((2 * half2, CP), bf16),
-            V((half2, CP), bf16),
-            V(((chips - 1) * piece2, CP), bf16),
-            V(((imgs - 1) * piece2, CP), bf16),
+            *buffers,
             dma((4,)),
             dma((6,)),
             dma((6,)),
-            dma((sems,)),
-            dma((sems,)),
-            dma((sems,)),
-            dma((sems,)),
-        ],
+        ]
+        + [dma((sems,))] * 6,
         compiler_params=pltpu.CompilerParams(
             vmem_limit_bytes=63 * 1024 * 1024, collective_id=0, has_side_effects=True
         ),
         name="layer",
-    )(scal, img, cot, wqkv, wproj, wfc1, wfc2, wconv, vecs, extra)
-
-
-def prepare(norm1_gain, norm1_bias, qkv_weight, qv_bias, bias_table, proj_weight, proj_bias,
-            norm2_gain, norm2_bias, fc1_weight, fc1_bias, fc2_weight, fc2_bias, conv_weight, conv_bias):
-    pc = CP - C
-    hp = HP_DIM - HEAD_DIM
-    wqkv = jnp.pad(qkv_weight.reshape(C, 3, HEADS, HEAD_DIM), ((0, pc), (0, 0), (0, 2), (0, hp)))
-    wqkv = wqkv.reshape(CP, 3 * CP)
-    wproj = jnp.pad(proj_weight.reshape(HEADS, HEAD_DIM, C), ((0, 2), (0, hp), (0, pc))).reshape(CP, CP)
-    wfc1 = jnp.pad(fc1_weight, ((0, pc), (0, HP - HID)))
-    wfc2 = jnp.pad(fc2_weight, ((0, HP - HID), (0, pc)))
-    wconv = jnp.pad(conv_weight.transpose(0, 2, 1, 3), ((0, 0), (0, pc), (0, 0), (0, pc)))
-    wconv = wconv.reshape(3, CP, 3 * CP)
-
-    def row(v, one=False):
-        v = jnp.concatenate([v, jnp.ones((1,), f32)]) if one else v
-        return jnp.pad(v, (0, 3 * CP - v.shape[0]))
-
-    zero = jnp.zeros((C,), f32)
-    qkvb = jnp.stack([qv_bias[:C], zero, qv_bias[C:]]).reshape(3, HEADS, HEAD_DIM)
-    qkvb = jnp.pad(qkvb, ((0, 0), (0, 2), (0, hp))).reshape(-1)
-    vecs = jnp.stack(
-        [row(norm1_gain), row(norm1_bias, True), qkvb, row(proj_bias), row(norm2_gain),
-         row(norm2_bias, True), row(fc1_bias), row(fc2_bias, True), row(conv_bias)]
-        + [jnp.zeros((3 * CP,), f32)] * 7
-    )
-    return wqkv, wproj, wfc1, wfc2, wconv, vecs, score_extra(bias_table)
+    )(*operands)
+
+
+def run_finish(a, b, c, table):
+    S = jax.ShapeDtypeStruct
+    return pl.pallas_call(
+        finish_kernel,
+        out_shape=(
+            S((C,), f32),
+            S((C,), f32),
+            S((C, 3 * C), f32),
+            S((2 * C,), f32),
+            S((HEADS, table), f32),
+            S((C, C), f32),
+            S((C,), f32),
+            S((C,), f32),
+            S((C,), f32),
+            S((C, HID), f32),
+            S((HID,), f32),
+            S((C, HID), f32),
+            S((C,), f32),
+            S((3, 3, C, C), f32),
+            S((C,), f32),
+        ),
+        compiler_params=pltpu.CompilerParams(vmem_limit_bytes=32 * 1024 * 1024),
+        name="finish",
+    )(a, b, c)
 
 
 def on_device(
@@ -886,33 +994,15 @@
     img = images.reshape(rows_here, width, chans)
     cot = cotangent.reshape(rows_here, width, chans)
     scal = lax.div(widths, WIN)
-    wqkv, wproj, wfc1, wfc2, wconv, vecs, extra = prepare(
-        norm1_gain, norm1_bias, qkv_weight, qv_bias, bias_table, proj_weight, proj_bias,
-        norm2_gain, norm2_bias, fc1_weight, fc1_bias, fc2_weight, fc2_bias, conv_weight, conv_bias,
+    res, ig, a, b, c = run_layer(
+        lax.axis_size("rows"), lax.axis_size("imgs"),
+        scal, img, cot, qkv_weight, proj_weight, fc1_weight, fc2_weight.T, conv_weight, bias_table.T,
+        norm1_gain, norm1_bias, qv_bias, proj_bias, norm2_gain, norm2_bias, fc1_bias, fc2_bias, conv_bias,
     )
-    res, ig, g_qkv, g_proj, g_fc1, g_fc2, g_conv, v = run_layer(
-        lax.axis_size("rows"), lax.axis_size("imgs"),
-        scal, img, cot, wqkv, wproj, wfc1, wfc2, wconv, vecs, extra,
-    )
-    return (
-        res[None],
-        ig[None],
-        v[58, :C],
-        v[59, :C],
-        g_qkv,
-        jnp.concatenate([v[44, :C], v[52, :C]]),
-        v[60 : 60 + HEADS, :225].T,
-        g_proj,
-        v[30, :C],
-        v[56, :C],
-        v[57, :C],
-        g_fc1,
-        jnp.concatenate([v[4], v[12, : HID - CP]]),
-        g_fc2,
-        v[16, :C],
-        g_conv,
-        v[36, :C],
-    )
+    grads = list(run_finish(a, b, c, bias_table.shape[0]))
+    grads[4] = grads[4].T
+    grads[11] = grads[11].T
+    return (res[None], ig[None], *grads)
 
 
 def solution(mesh):

time: 159 us -> 114 us (0.72)
  local copies, waits for them, and re-layouts: 33.5 us -> 13.6 us
  Pallas kernels: 114 us -> 99 us
  matrix products: 5.84 us -> 0 us
  other arithmetic: 3.62 us -> 0 us
    pallas_call x1 -> x2, Pallas kernels: 114 us -> 99 us  [the longest x1 97.1 us: run_layer(): pl.pallas_call(functools.partial(layer_kernel, chips, imgs, tuple(pieces)...]
    dot_general x1 -> x0, matrix products: 5.84 us -> none  [score_extra(): rel = jnp.dot(hot, bias_table, precision=lax.Precision.HIGHEST)]
    pad x14 -> x0, local copies, waits for them, and re-layouts: 5.75 us -> none  [the longest x8 3.43 us: row(): return jnp.pad(v, (0, 3 * CP - v.shape[0]))]
    reshape x6 -> x0, local copies, waits for them, and re-layouts: 3.71 us -> none  [the longest x1 1.53 us: prepare(): wconv = wconv.reshape(3, CP, 3 * CP)]
    unnamed x40 -> x14, local copies, waits for them, and re-layouts: 17.2 us -> 13.6 us
    slice x3 -> x0, local copies, waits for them, and re-layouts: 3 us -> none  [the longest x1 1.48 us: on_device(): v[36, :C]]
    concatenate x4 -> x0, other arithmetic: 2.76 us -> none  [the longest x2 1.52 us: row(): v = jnp.concatenate([v, jnp.ones((1,), f32)]) if one else v]
    another operation x16 -> x0, local copies, waits for them, and re-layouts: 1.65 us -> none  [the longest x13 1.42 us: prepare(): jnp.stack([row(norm1_gain), row(norm1_bias, True), qkvb, row(proj_bias),...]
where the time goes in v4:
time: 114 us
  Pallas kernels  99 us (87%)
  local copies, waits for them, and re-layouts  13.6 us (12%)
  between operations  1.35 us (1%)
    pallas_call x1, Pallas kernels, run_layer(): pl.pallas_call(functools.partial(layer_kernel, chips, imgs, tuple(pieces)...  97.1 us
    unnamed x14, local copies, waits for them, and re-layouts  13.6 us

profile of v4, /device:TPU:0, one launch (start us, length us, event | category | flops | bytes accessed | tf_op | source)
XLA Modules:
  0.0 114.0 jit_solution(18110745928505131629)
XLA Ops:
  1.3 0.0 copy-start.4
  1.3 4.3 %copy.35 = bf16[1,16,256,180]{3,2,1,0:T(8,128)(2,1)} copy(bf16[1,16,256,180]{2,1,3,0:T(8,128)(2,1)} %param.18) | data formatting | bytes 2949120 | tf_op args[0]
  5.6 0.0 copy-done.4
  5.6 2.6 %copy.36 = bf16[1,16,256,180]{3,2,1,0:T(8,128)(2,1)} copy(bf16[1,16,256,180]{2,1,3,0:T(8,128)(2,1)S(1)} %copy-done.4) | data formatting | bytes 2949120 | tf_op args[17]
  8.3 97.1 %layer.1 = (bf16[16,256,180]{2,1,0:T(8,128)(2,1)}, bf16[16,256,180]{2,1,0:T(8,128)(2,1)}, bf16[1024,128]{1,0:T(8,128)(2,1)}, bf16[1024,128]{1,0:T(8,128)(2,1)}, bf16[3072,128]{1,0:T(8,128)(2,1)}) custom-call(s32[1]{0:T(128)S(6)} %div.18.scal, bf16[16,256,180]{2,1,0:T(8,128)(2,1)} %bitcast.8, bf16[16,256,180]{2,1,0:T(8,128)(2,1)} %bitcast.9, ...), custom_call_target="tpu_custom_call" | custom-call | tf_op jit(solution)/shard_map/layer/pallas_call | solution.py:913
  105.4 0.0 copy-start.3
  105.4 4.3 %copy.37 = bf16[1,16,256,180]{2,1,3,0:T(8,128)(2,1)} copy(bf16[1,16,256,180]{3,2,1,0:T(8,128)(2,1)} %bitcast.11) | data formatting | bytes 2949120
  109.7 0.0 copy-done.3
  109.7 0.0 copy-start
  109.7 0.0 copy-start.1
  109.7 0.0 copy-start.2
  109.7 2.4 %copy.38 = bf16[1,16,256,180]{2,1,3,0:T(8,128)(2,1)} copy(bf16[1,16,256,180]{3,2,1,0:T(8,128)(2,1)S(1)} %bitcast.10) | data formatting | bytes 2949120
  112.1 0.0 copy-done
  112.1 0.0 copy-done.1
  112.1 0.0 copy-done.2
  112.1 1.9 %finish.1 = (f32[180]{0:T(256)}, f32[180]{0:T(256)}, f32[180,540]{1,0:T(8,128)}, f32[360]{0:T(512)}, f32[6,225]{1,0:T(8,128)}, /*index=5*/f32[180,180]{1,0:T(8,1...) custom-call(bf16[1024,128]{1,0:T(8,128)(2,1)S(1)} %copy-done.1, ...), custom_call_target="tpu_custom_call" | custom-call | tf_op jit(solution)/shard_map/finish/pallas_call | solution.py:965
Async XLA Ops:
  1.3 4.3 %copy-start.4 = (bf16[1,16,256,180]{2,1,3,0:T(8,128)(2,1)S(1)}, bf16[1,16,256,180]{2,1,3,0:T(8,128)(2,1)}, u32[]{:S(2)}) copy-start(bf16[1,16,256,180]{2,1,3,0:T(8,128)(2,1)} %param.35) | copy-start | bytes 4423684
  105.4 4.3 %copy-start.3 = (bf16[16,256,180]{2,1,0:T(8,128)(2,1)S(1)}, bf16[16,256,180]{2,1,0:T(8,128)(2,1)}, u32[]{:S(2)}) copy-start(bf16[16,256,180]{2,1,0:T(8,128)(2,1)} %get-tuple-element.38) | copy-start | bytes 4423684
  109.7 2.4 %copy-start = (bf16[3072,128]{1,0:T(8,128)(2,1)S(1)}, bf16[3072,128]{1,0:T(8,128)(2,1)}, u32[]{:S(2)}) copy-start(bf16[3072,128]{1,0:T(8,128)(2,1)} %get-tuple-element.41.c_ref) | copy-start | bytes 2359300
  109.7 2.4 %copy-start.1 = (bf16[1024,128]{1,0:T(8,128)(2,1)S(1)}, bf16[1024,128]{1,0:T(8,128)(2,1)}, u32[]{:S(2)}) copy-start(bf16[1024,128]{1,0:T(8,128)(2,1)} %get-tuple-element.39.a_ref) | copy-start | bytes 786436
  109.7 2.4 %copy-start.2 = (bf16[1024,128]{1,0:T(8,128)(2,1)S(1)}, bf16[1024,128]{1,0:T(8,128)(2,1)}, u32[]{:S(2)}) copy-start(bf16[1024,128]{1,0:T(8,128)(2,1)} %get-tuple-element.40.b_ref) | copy-start | bytes 786436

commit v5 on v4

--- a/solution.py
+++ b/solution.py
@@ -126,7 +126,49 @@
     return rows_of((256, CP)) < width
 
 
-TURNS = ((1, (("a", 2), ("c", 1))), (2, (("a", 3),)), (5, (("c", 2), ("a", 4))))
+class SmallAllReduce:
+    def __init__(self, sums, slots, ssem, rsem, chips, imgs):
+        self.sums, self.ssem, self.rsem = [sums.at[n] for n in range(4)], ssem, rsem
+        rows, z = lax.axis_index("rows"), lax.axis_index("imgs")
+        core, chip = lax.rem(rows, 2), lax.div(rows, 2)
+        self.stages = [
+            [{"rows": chip * 2 + 1 - core}],
+            [{"rows": lax.rem(chip + d, chips) * 2 + core} for d in range(1, chips)],
+            [{"imgs": lax.rem(z + d, imgs)} for d in range(1, imgs)],
+        ]
+        self.first = [0, 1, chips]
+        self.slots = slots
+
+    def copies(self, n):
+        return [
+            pltpu.make_async_remote_copy(
+                src_ref=self.sums[n],
+                dst_ref=self.slots.at[self.first[n] + d],
+                send_sem=self.ssem.at[self.first[n] + d],
+                recv_sem=self.rsem.at[self.first[n] + d],
+                device_id=to,
+                device_id_type=pl.DeviceIdType.MESH,
+            )
+            for d, to in enumerate(self.stages[n])
+        ]
+
+    def begin(self, value):
+        self.sums[0][...] = value
+        for c in self.copies(0):
+            c.start()
+
+    def step(self, n):
+        value = self.sums[n][...]
+        for d, c in enumerate(self.copies(n)):
+            c.wait()
+            value += self.slots[self.first[n] + d]
+        self.sums[n + 1][...] = value
+        if n < 2:
+            for c in self.copies(n + 1):
+                c.start()
+
+
+TURNS = ((1, (("a", 2), ("c", 1))), (5, (("a", 3),)), (7, (("c", 2),)))
 
 
 class AllReduce:
@@ -283,6 +325,7 @@
     a_out,
     b_out,
     c_out,
+    d_out,
     wqkv,
     wproj,
     wfc1,
@@ -326,6 +369,8 @@
     c_r1,
     c_r2,
     c_r3,
+    dd_sums,
+    dd_slots,
     lsem,
     hs,
     hr,
@@ -335,6 +380,8 @@
     b_r,
     c_s,
     c_r,
+    dd_s,
+    dd_r,
 ):
     stripes = 2 * chips
     rank = lax.axis_index("rows")
@@ -346,13 +393,19 @@
     arb = AllReduce(b_buf, b_out, b_r1, b_r2, b_r3, b_s, b_r, pb, chips, imgs, False)
     arc = AllReduce(c_buf, c_out, c_r1, c_r2, c_r3, c_s, c_r, pc, chips, imgs, True)
 
+    ard = SmallAllReduce(dd_sums, dd_slots, dd_s, dd_r, chips, imgs)
+
+    load_cot = pltpu.make_async_copy(cot, io1.at[pl.ds(0, 16)], lsem.at[0])
+    load_img = pltpu.make_async_copy(img, io2.at[pl.ds(0, 16)], lsem.at[1])
+    load_cot.start()
+    load_img.start()
+
     barrier = pltpu.get_barrier_semaphore()
     peers = [{"rows": up}, {"rows": down}]
     peers += [{"rows": lax.rem(rank + 2 * d, stripes)} for d in range(1, chips)]
     peers += [{"imgs": lax.rem(ara.z + d, imgs)} for d in range(1, imgs)]
     for peer in peers:
         pl.semaphore_signal(barrier, inc=1, device_id=peer, device_id_type=pl.DeviceIdType.MESH)
-    pl.semaphore_wait(barrier, len(peers))
 
     def remote(src, dst, to, n):
         return pltpu.make_async_remote_copy(
@@ -366,13 +419,6 @@
 
     send_img = remote(img.at[pl.ds(0, 4)], io2.at[pl.ds(16, 4)], up, 0)
     send_cot = remote(cot.at[pl.ds(0, 5)], io1.at[pl.ds(16, 5)], up, 1)
-    send_cot.start()
-    send_img.start()
-    load_cot = pltpu.make_async_copy(cot, io1.at[pl.ds(0, 16)], lsem.at[0])
-    load_img = pltpu.make_async_copy(img, io2.at[pl.ds(0, 16)], lsem.at[1])
-    load_cot.start()
-    load_img.start()
-
     nb = scal[0]
     width = nb * WIN
     is_last = rank == stripes - 1
@@ -447,6 +493,9 @@
         put_g(r, io1[r + 3], 1.0)
 
     put_g(14, io1[15], joined)
+    pl.semaphore_wait(barrier, len(peers))
+    send_cot.start()
+    send_img.start()
     load_img.wait()
 
     pos_hi = rows_of((1, WIN, CP)) >= SHIFT
@@ -498,15 +547,16 @@
         def _(y):
             xband[y, :, 0:C] = io2[band * 8 + y + 4].astype(f32)
 
-        @pl.loop(0, 8)
+        @pl.loop(0, 4)
         def _(y):
-            r = band * 8 + y
+            r = band * 8 + 2 * y
             pos = r + 1 + jnp.where(r >= 12, 2, 0)
             acc = None
             for a in range(3):
-                d = dot(gcat[row_at(pos + 1 - a), :], wconv[a], 1, 1)
+                d = dot(gcat[row_at(pos + 1 - a, 2), :], wconv[a], 1, 1)
                 acc = d if acc is None else acc + d
-            gband[y] = jnp.where(col_in_p, acc, 0.0)
+            for n in range(2):
+                gband[2 * y + n] = jnp.where(col_in_p, acc[n * 256 : (n + 1) * 256], 0.0)
 
         @pl.loop(0, 4)
         def _(gg):
@@ -607,22 +657,23 @@
         @pl.loop(0, 8)
         def _(y):
             r = band * 8 + y
-            pos = r + 1 + jnp.where(r >= 12, 2, 0)
+            pos = r + 5 + jnp.where(r >= 12, 2, 0)
             llbuf[row_at(pos), :] = jnp.where(col_in_p, xband[y], 0.0).astype(bf16)
 
-    send_up = remote(llbuf.at[pl.ds(256, 256)], llbuf.at[pl.ds(19 * 256, 256)], up, 2)
-    send_down = remote(llbuf.at[pl.ds(18 * 256, 256)], llbuf.at[pl.ds(0, 256)], down, 3)
+    joined_low = joined.astype(bf16)
+    llbuf[17 * 256 : 18 * 256, :] = llbuf[19 * 256 : 20 * 256, :] * joined_low
+    llbuf[18 * 256 : 19 * 256, :] = llbuf[16 * 256 : 17 * 256, :] * joined_low
+    send_up = remote(llbuf.at[pl.ds(5 * 256, 256)], llbuf.at[pl.ds(23 * 256, 256)], up, 2)
+    send_down = remote(llbuf.at[pl.ds(22 * 256, 256)], llbuf.at[pl.ds(4 * 256, 256)], down, 3)
+    send_more = remote(llbuf.at[pl.ds(18 * 256, 1024)], llbuf.at[pl.ds(0, 1024)], down, 4)
     send_up.start()
     send_down.start()
-    joined_low = joined.astype(bf16)
-    llbuf[13 * 256 : 14 * 256, :] = llbuf[15 * 256 : 16 * 256, :] * joined_low
-    llbuf[14 * 256 : 15 * 256, :] = llbuf[12 * 256 : 13 * 256, :] * joined_low
 
     def wgrad_rows(n):
         start = 1 + 4 * n + jnp.where(n == 3, 2, 0)
         gs = gcat[row_at(start, 4), :]
         for a in range(3):
-            d_conv[a] += dot(llbuf[row_at(start + a - 1, 4), 0:CR], gs, 0, 0)
+            d_conv[a] += dot(llbuf[row_at(start + a + 3, 4), 0:CR], gs, 0, 0)
 
     low_lanes = lanes((1, 128)) < 64
 
@@ -663,18 +714,20 @@
     arc.step(0)
 
     def conv_rows(lo, hi):
-        @pl.loop(lo, hi)
-        def _(r):
-            pos = r + 1 + jnp.where(r >= 12, 2, 0)
+        @pl.loop(lo // 2, hi // 2)
+        def _(half):
+            r = 2 * half
             acc = None
             for a in range(3):
-                d = dot(llbuf[row_at(pos + a - 1), :], wconv[a])
+                d = dot(llbuf[row_at(r + a, 2), :], wconv[a])
                 acc = d if acc is None else acc + d
-            tmp[8:264, :] = acc[:, 0:CP]
-            tmp[280:536, :] = acc[:, 2 * CP : 3 * CP]
-            out = acc[:, CP : 2 * CP] + tmp[7:263, :] + tmp[281:537, :] + vec(8, CP)
-            out = out[:, 0:C] + io2[r + 4].astype(f32)
-            io1[r] = jnp.where(col_in, out, 0.0).astype(bf16)
+            for n in range(2):
+                px = slice(n * 256, (n + 1) * 256)
+                tmp[8:264, :] = acc[px, 0:CP]
+                tmp[280:536, :] = acc[px, 2 * CP : 3 * CP]
+                out = acc[px, CP : 2 * CP] + tmp[7:263, :] + tmp[281:537, :] + vec(8, CP)
+                out = out[:, 0:C] + io2[r + n].astype(f32)
+                io1[r + n] = jnp.where(col_in, out, 0.0).astype(bf16)
 
     def grad_rows(band):
         from_win(fgrad, band)
@@ -686,9 +739,6 @@
             v = xband[y] + gcat[row_at(pos), CP : 2 * CP].astype(f32)
             ig_rows[r] = jnp.where(col_in_p, v, 0.0)[:, 0:C].astype(bf16)
 
-    conv_rows(12, 16)
-    send_res = remote(io1.at[pl.ds(12, 4)], res_out.at[pl.ds(0, 4)], down, 4)
-    send_res.start()
     send_ig = remote(ig_rows.at[pl.ds(12, 4)], ig_out.at[pl.ds(0, 4)], down, 5)
 
     @pl.loop(0, 8)
@@ -726,17 +776,9 @@
 
         d_qkv[...] += dot(normed[gs, 0:CR], qkv[gs, :], 0, 0)
 
-        dn1 = dot(qkv[gs, :], wqkv[...], 1, 1).astype(bf16)
-
-        def back1(dn, xhat, fg):
-            dn, xhat = dn.astype(f32), xhat.astype(f32)
-            out = fg + ln_bwd(dn, xhat, xhat[:, 200:201] + xhat[:, 201:202], vec(0, CP))
-            return out, fold8(dn * xhat), fold8(dn)
-
-        back = by_rows(back1, 64, dn1, xhat1[gs, :], fgrad[gs, :])
-        fgrad[gs, :] = back[0]
-        d_norm[16:24, :] += fold8(back[1])
-        d_norm[24:32, :] += fold8(back[2])
+        @pl.when(turn == 5)
+        def _():
+            send_more.start()
 
         for at, steps in TURNS:
 
@@ -744,11 +786,6 @@
             def _(steps=steps):
                 for which, k in steps:
                     {"a": ara, "c": arc}[which].step(k)
-
-        @pl.when(turn == 3)
-        def _():
-            grad_rows(1)
-            send_ig.start()
 
     for n in range(3):
         b_buf[n * CR : (n + 1) * CR, :] = d_qkv[:, n * CP : n * CP + 128].astype(bf16)
@@ -759,33 +796,62 @@
     b_buf[B_SMALL : B_SMALL + 16, :] = small[:, 0:128].astype(bf16)
     b_buf[B_SMALL + 16 : B_SMALL + 32, :] = small[:, 128:256].astype(bf16)
     arb.step(0)
+    ara.step(4)
+
+    def norm1_back(lo, hi):
+        @pl.loop(lo, hi)
+        def _(g):
+            gs = pl.ds(pl.multiple_of(g * 512, 512), 512)
+            dn1 = dot(qkv[gs, :], wqkv[...], 1, 1).astype(bf16)
+
+            def back1(dn, xhat, fg):
+                dn, xhat = dn.astype(f32), xhat.astype(f32)
+                out = fg + ln_bwd(dn, xhat, xhat[:, 200:201] + xhat[:, 201:202], vec(0, CP))
+                return out, fold8(dn * xhat), fold8(dn)
+
+            back = by_rows(back1, 64, dn1, xhat1[gs, :], fgrad[gs, :])
+            fgrad[gs, :] = back[0]
+            d_norm[16:24, :] += fold8(back[1])
+            d_norm[24:32, :] += fold8(back[2])
+
+    norm1_back(4, 8)
+    arb.step(1)
+    grad_rows(1)
+    send_ig.start()
+    norm1_back(0, 4)
+    sums = jnp.sum(d_norm[16:32, :].reshape(2, 8, CP), axis=1)
+    sums = jnp.concatenate([sums[:, 0:128], sums[:, 128:256], jnp.zeros((4, 128), f32)], axis=0)
+    ard.begin(sums)
     ara.step(5)
     arc.step(3)
+    conv_rows(4, 8)
+    arb.step(2)
+    ara.step(6)
+    ard.step(0)
+    conv_rows(8, 16)
+    arc.step(4)
+    ard.step(1)
+    send_more.wait()
     conv_rows(0, 4)
-    arb.step(1)
-    ara.step(6)
-    conv_rows(4, 8)
-    arc.step(4)
-    conv_rows(8, 12)
-    store_res = pltpu.make_async_copy(io1.at[pl.ds(0, 12)], res_out.at[pl.ds(4, 12)], lsem.at[2])
+    store_res = pltpu.make_async_copy(io1.at[pl.ds(0, 16)], res_out, lsem.at[2])
     store_res.start()
-    arb.step(2)
     grad_rows(0)
     store_ig = pltpu.make_async_copy(ig_rows.at[pl.ds(0, 12)], ig_out.at[pl.ds(4, 12)], lsem.at[3])
     store_ig.start()
     arb.step(3)
+    ard.step(2)
+    d_out[...] = dd_sums[3]
     arc.step(5)
     arb.step(5)
     arc.step(6)
     arb.step(6)
-    send_res.wait()
     send_ig.wait()
     store_res.wait()
     store_ig.wait()
 
 
 def finish_kernel(
-    a_ref, b_ref, c_ref, o_n1g, o_n1b, o_qkv, o_qvb, o_table, o_proj, o_pb, o_n2g, o_n2b, o_fc1, o_f1b, o_fc2t,
+    a_ref, b_ref, c_ref, d_ref, o_n1g, o_n1b, o_qkv, o_qvb, o_table, o_proj, o_pb, o_n2g, o_n2b, o_fc1, o_f1b, o_fc2t,
     o_f2b, o_conv, o_cb,
 ):
     def block(ref, at, rows=CR):
@@ -827,7 +893,10 @@
             o_qvb[n // 2 * C : (n // 2 + 1) * C] = v[C : C + 1, 0:C].reshape(C)
     small = jnp.concatenate([block(b_ref, B_SMALL, 16), block(b_ref, B_SMALL + 16, 16)], axis=1)
     o_table[...] = small[0:HEADS, 0 : o_table.shape[1]]
-    for n, ref in ((8, o_n2g), (9, o_n2b), (10, o_n1g), (11, o_n1b), (12, o_f2b)):
+    for n, ref in ((0, o_n1g), (1, o_n1b)):
+        v = jnp.concatenate([d_ref[n : n + 1, :], d_ref[n + 2 : n + 3, :]], axis=1)
+        ref[...] = v[:, 0:C].reshape(C)
+    for n, ref in ((8, o_n2g), (9, o_n2b), (12, o_f2b)):
         ref[...] = small[n : n + 1, 0:C].reshape(C)
 
 
@@ -912,9 +981,9 @@
         ]
     return pl.pallas_call(
         functools.partial(layer_kernel, chips, imgs, tuple(pieces)),
-        out_shape=(S((16, 256, C), bf16), S((16, 256, C), bf16), *outs),
+        out_shape=(S((16, 256, C), bf16), S((16, 256, C), bf16), *outs, S((8, 128), f32)),
         in_specs=[SM, HB, HB] + [VM] * 15,
-        out_specs=[HB] * 2 + [VM] * 3,
+        out_specs=[HB] * 2 + [VM] * 4,
         scratch_shapes=[
             V((CP, 3 * CP), bf16),
             V((CP, CP), bf16),
@@ -935,7 +1004,7 @@
             V((8, 256, CP), f32),
             V((8, 256, CP), f32),
             V((20 * 256, 3 * CP), bf16),
-            V((20 * 256, CP), bf16),
+            V((24 * 256, CP), bf16),
             V((4096, CP), bf16),
             V((4096, CP), bf16),
             V((4096, 3 * CP), bf16),
@@ -948,11 +1017,14 @@
             V((WIN, WIN, CP), f32),
             V((544, CP), f32),
             *buffers,
+            V((4, 8, 128), f32),
+            V((chips + imgs - 1, 8, 128), f32),
             dma((4,)),
             dma((6,)),
             dma((6,)),
         ]
-        + [dma((sems,))] * 6,
+        + [dma((sems,))] * 6
+        + [dma((chips + imgs - 1,))] * 2,
         compiler_params=pltpu.CompilerParams(
             vmem_limit_bytes=63 * 1024 * 1024, collective_id=0, has_side_effects=True
         ),
@@ -960,7 +1032,7 @@
     )(*operands)
 
 
-def run_finish(a, b, c, table):
+def run_finish(a, b, c, d, table):
     S = jax.ShapeDtypeStruct
     return pl.pallas_call(
         finish_kernel,
@@ -983,7 +1055,7 @@
         ),
         compiler_params=pltpu.CompilerParams(vmem_limit_bytes=32 * 1024 * 1024),
         name="finish",
-    )(a, b, c)
+    )(a, b, c, d)
 
 
 def on_device(
@@ -994,12 +1066,12 @@
     img = images.reshape(rows_here, width, chans)
     cot = cotangent.reshape(rows_here, width, chans)
     scal = lax.div(widths, WIN)
-    res, ig, a, b, c = run_layer(
+    res, ig, a, b, c, d = run_layer(
         lax.axis_size("rows"), lax.axis_size("imgs"),
         scal, img, cot, qkv_weight, proj_weight, fc1_weight, fc2_weight.T, conv_weight, bias_table.T,
         norm1_gain, norm1_bias, qv_bias, proj_bias, norm2_gain, norm2_bias, fc1_bias, fc2_bias, conv_bias,
     )
-    grads = list(run_finish(a, b, c, bias_table.shape[0]))
+    grads = list(run_finish(a, b, c, d, bias_table.shape[0]))
     grads[4] = grads[4].T
     grads[11] = grads[11].T
     return (res[None], ig[None], *grads)

time: 114 us -> 106 us (0.930)
  Pallas kernels: 99 us -> 91.1 us
    pallas_call x1, Pallas kernels: 97.1 us -> 89.2 us  [run_layer(): pl.pallas_call(functools.partial(layer_kernel, chips, imgs, tuple(pieces)...]
    unnamed x14 -> x16, local copies, waits for them, and re-layouts: 13.6 us -> 13.5 us
where the time goes in v5:
time: 106 us
  Pallas kernels  91.1 us (86%)
  local copies, waits for them, and re-layouts  13.5 us (13%)
  between operations  1.52 us (1%)
    pallas_call x1, Pallas kernels, run_layer(): pl.pallas_call(functools.partial(layer_kernel, chips, imgs, tuple(pieces)...  89.2 us
    unnamed x16, local copies, waits for them, and re-layouts  13.5 us

profile of v5, /device:TPU:0, one launch (start us, length us, event | category | flops | bytes accessed | tf_op | source)
XLA Modules:
  0.0 106.2 jit_solution(15669872095384416580)
XLA Ops:
  1.3 0.0 copy-start.5
  1.3 4.3 %copy.35 = bf16[1,16,256,180]{3,2,1,0:T(8,128)(2,1)} copy(bf16[1,16,256,180]{2,1,3,0:T(8,128)(2,1)} %param.18) | data formatting | bytes 2949120 | tf_op args[0]
  5.6 0.0 copy-done.5
  5.6 2.6 %copy.36 = bf16[1,16,256,180]{3,2,1,0:T(8,128)(2,1)} copy(bf16[1,16,256,180]{2,1,3,0:T(8,128)(2,1)S(1)} %copy-done.5) | data formatting | bytes 2949120 | tf_op args[17]
  8.2 89.2 %layer.1 = (bf16[16,256,180]{2,1,0:T(8,128)(2,1)}, bf16[16,256,180]{2,1,0:T(8,128)(2,1)}, bf16[1024,128]{1,0:T(8,128)(2,1)}, bf16[1024,128]{1,0:T(8,128)(2,1)}, ...) custom-call(s32[1]{0:T(128)S(6)} %div.18.scal, bf16[16,256,180]{2,1,0:T(8,128)(2,1)} %bitcast.8, ...), custom_call_target="tpu_custom_call" | custom-call | tf_op jit(solution)/shard_map/layer/pallas_call | solution.py:982
  97.4 0.0 copy-start.4
  97.4 4.3 %copy.37 = bf16[1,16,256,180]{2,1,3,0:T(8,128)(2,1)} copy(bf16[1,16,256,180]{3,2,1,0:T(8,128)(2,1)} %bitcast.11) | data formatting | bytes 2949120
  101.7 0.0 copy-done.4
  101.7 0.0 copy-start
  101.7 0.0 copy-start.1
  101.7 0.0 copy-start.2
  101.7 0.0 copy-start.3
  101.7 2.4 %copy.38 = bf16[1,16,256,180]{2,1,3,0:T(8,128)(2,1)} copy(bf16[1,16,256,180]{3,2,1,0:T(8,128)(2,1)S(1)} %bitcast.10) | data formatting | bytes 2949120
  104.1 0.0 copy-done
  104.1 0.0 copy-done.1
  104.1 0.0 copy-done.2
  104.1 0.0 copy-done.3
  104.1 1.9 %finish.1 = (f32[180]{0:T(256)}, f32[180]{0:T(256)}, f32[180,540]{1,0:T(8,128)}, f32[360]{0:T(512)}, f32[6,225]{1,0:T(8,128)}, /*index=5*/f32[180,180]{1,0:T(8,1...) custom-call(bf16[1024,128]{1,0:T(8,128)(2,1)S(1)} %copy-done.1, ...), custom_call_target="tpu_custom_call" | custom-call | tf_op jit(solution)/shard_map/finish/pallas_call | solution.py:1037
Async XLA Ops:
  1.3 4.3 %copy-start.5 = (bf16[1,16,256,180]{2,1,3,0:T(8,128)(2,1)S(1)}, bf16[1,16,256,180]{2,1,3,0:T(8,128)(2,1)}, u32[]{:S(2)}) copy-start(bf16[1,16,256,180]{2,1,3,0:T(8,128)(2,1)} %param.35) | copy-start | bytes 4423684
  97.4 4.3 %copy-start.4 = (bf16[16,256,180]{2,1,0:T(8,128)(2,1)S(1)}, bf16[16,256,180]{2,1,0:T(8,128)(2,1)}, u32[]{:S(2)}) copy-start(bf16[16,256,180]{2,1,0:T(8,128)(2,1)} %get-tuple-element.39) | copy-start | bytes 4423684
  101.7 2.4 %copy-start = (bf16[3072,128]{1,0:T(8,128)(2,1)S(1)}, bf16[3072,128]{1,0:T(8,128)(2,1)}, u32[]{:S(2)}) copy-start(bf16[3072,128]{1,0:T(8,128)(2,1)} %get-tuple-element.42.c_ref) | copy-start | bytes 2359300
  101.7 2.4 %copy-start.1 = (bf16[1024,128]{1,0:T(8,128)(2,1)S(1)}, bf16[1024,128]{1,0:T(8,128)(2,1)}, u32[]{:S(2)}) copy-start(bf16[1024,128]{1,0:T(8,128)(2,1)} %get-tuple-element.40.a_ref) | copy-start | bytes 786436
  101.7 2.4 %copy-start.2 = (bf16[1024,128]{1,0:T(8,128)(2,1)S(1)}, bf16[1024,128]{1,0:T(8,128)(2,1)}, u32[]{:S(2)}) copy-start(bf16[1024,128]{1,0:T(8,128)(2,1)} %get-tuple-element.41.b_ref) | copy-start | bytes 786436
  101.7 2.4 %copy-start.3 = (f32[8,128]{1,0:T(8,128)S(1)}, f32[8,128]{1,0:T(8,128)}, u32[]{:S(2)}) copy-start(f32[8,128]{1,0:T(8,128)} %get-tuple-element.43.d_ref) | copy-start | bytes 12292

commit v6 on v5

--- a/solution.py
+++ b/solution.py
@@ -168,7 +168,7 @@
                 c.start()
 
 
-TURNS = ((1, (("a", 2), ("c", 1))), (5, (("a", 3),)), (7, (("c", 2),)))
+TURNS = ((0, (("a", 1),)), (1, (("c", 1),)), (4, (("a", 2),)), (7, (("c", 2),)))
 
 
 class AllReduce:
@@ -302,6 +302,7 @@
     chips,
     imgs,
     pieces,
+    splits,
     scal,
     img,
     cot,
@@ -356,6 +357,8 @@
     do_buf,
     ig_rows,
     edge,
+    tmp_eye,
+    planes,
     tmp,
     a_buf,
     a_r1,
@@ -389,14 +392,15 @@
     up = lax.rem(rank + stripes - 1, stripes)
     down = lax.rem(rank + 1, stripes)
     pa, pb, pc = pieces
-    ara = AllReduce(a_buf, a_out, a_r1, a_r2, a_r3, a_s, a_r, pa, chips, imgs, True)
-    arb = AllReduce(b_buf, b_out, b_r1, b_r2, b_r3, b_s, b_r, pb, chips, imgs, False)
-    arc = AllReduce(c_buf, c_out, c_r1, c_r2, c_r3, c_s, c_r, pc, chips, imgs, True)
+    ara = AllReduce(a_buf, a_out, a_r1, a_r2, a_r3, a_s, a_r, pa, chips, imgs, splits[0])
+    arb = AllReduce(b_buf, b_out, b_r1, b_r2, b_r3, b_s, b_r, pb, chips, imgs, splits[1])
+    arc = AllReduce(c_buf, c_out, c_r1, c_r2, c_r3, c_s, c_r, pc, chips, imgs, splits[2])
 
     ard = SmallAllReduce(dd_sums, dd_slots, dd_s, dd_r, chips, imgs)
 
-    load_cot = pltpu.make_async_copy(cot, io1.at[pl.ds(0, 16)], lsem.at[0])
-    load_img = pltpu.make_async_copy(img, io2.at[pl.ds(0, 16)], lsem.at[1])
+    flat = C * 16
+    load_cot = pltpu.make_async_copy(cot, qkv.at[pl.ds(0, flat), pl.ds(CP, CP)], lsem.at[0])
+    load_img = pltpu.make_async_copy(img, qkv.at[pl.ds(0, flat), pl.ds(0, CP)], lsem.at[1])
     load_cot.start()
     load_img.start()
 
@@ -417,8 +421,8 @@
             device_id_type=pl.DeviceIdType.MESH,
         )
 
-    send_img = remote(img.at[pl.ds(0, 4)], io2.at[pl.ds(16, 4)], up, 0)
-    send_cot = remote(cot.at[pl.ds(0, 5)], io1.at[pl.ds(16, 5)], up, 1)
+    send_img = remote(io2.at[pl.ds(0, 4)], io2.at[pl.ds(16, 4)], up, 0)
+    send_cot = remote(io1.at[pl.ds(0, 5)], io1.at[pl.ds(16, 5)], up, 1)
     nb = scal[0]
     width = nb * WIN
     is_last = rank == stripes - 1
@@ -486,7 +490,25 @@
         ]
     score_terms(r_table[...], extra)
 
+    tmp_eye[...] = (iota((128, 128), 0) == iota((128, 128), 1)).astype(bf16)
+
+    def to_rows(lane0, dst):
+        for m in range(2):
+            half = slice(m * 128, (m + 1) * 128)
+
+            @pl.loop(0, flat // 96, unroll=2)
+            def _(n):
+                at = pl.ds(pl.multiple_of(n * 96, 96), 96)
+                planes[at, :] = qkv[at, lane0 + m * 128 : lane0 + (m + 1) * 128].astype(f32)
+
+            for r in range(16):
+                x = planes[pl.ds(r, C, stride=16), :].astype(bf16)
+                dst[r, half, :] = dot(tmp_eye[...], x, 1, 1).astype(bf16)
+
     load_cot.wait()
+    to_rows(CP, io1)
+    load_img.wait()
+    to_rows(0, io2)
 
     @pl.loop(0, 13)
     def _(r):
@@ -496,7 +518,6 @@
     pl.semaphore_wait(barrier, len(peers))
     send_cot.start()
     send_img.start()
-    load_img.wait()
 
     pos_hi = rows_of((1, WIN, CP)) >= SHIFT
 
@@ -528,6 +549,8 @@
 
     def win_rows(w):
         return pl.ds(pl.multiple_of(w * AREA, AREA), AREA)
+
+    send_up = remote(llbuf.at[pl.ds(5 * 256, 256)], llbuf.at[pl.ds(23 * 256, 256)], up, 2)
 
     @pl.loop(0, 2)
     def _(band):
@@ -660,13 +683,15 @@
             pos = r + 5 + jnp.where(r >= 12, 2, 0)
             llbuf[row_at(pos), :] = jnp.where(col_in_p, xband[y], 0.0).astype(bf16)
 
+        @pl.when(band == 0)
+        def _():
+            send_up.start()
+
     joined_low = joined.astype(bf16)
     llbuf[17 * 256 : 18 * 256, :] = llbuf[19 * 256 : 20 * 256, :] * joined_low
     llbuf[18 * 256 : 19 * 256, :] = llbuf[16 * 256 : 17 * 256, :] * joined_low
-    send_up = remote(llbuf.at[pl.ds(5 * 256, 256)], llbuf.at[pl.ds(23 * 256, 256)], up, 2)
     send_down = remote(llbuf.at[pl.ds(22 * 256, 256)], llbuf.at[pl.ds(4 * 256, 256)], down, 3)
     send_more = remote(llbuf.at[pl.ds(18 * 256, 1024)], llbuf.at[pl.ds(0, 1024)], down, 4)
-    send_up.start()
     send_down.start()
 
     def wgrad_rows(n):
@@ -691,12 +716,9 @@
         wgrad_rows(n)
 
     send_up.wait()
+    wgrad_rows(3)
     send_down.wait()
-    ara.step(1)
-
-    @pl.loop(0, 2)
-    def _(n):
-        wgrad_rows(n * 3)
+    wgrad_rows(0)
 
     tails = []
     for a in range(3):
@@ -796,7 +818,7 @@
     b_buf[B_SMALL : B_SMALL + 16, :] = small[:, 0:128].astype(bf16)
     b_buf[B_SMALL + 16 : B_SMALL + 32, :] = small[:, 128:256].astype(bf16)
     arb.step(0)
-    ara.step(4)
+    ara.step(3)
 
     def norm1_back(lo, hi):
         @pl.loop(lo, hi)
@@ -822,15 +844,15 @@
     sums = jnp.sum(d_norm[16:32, :].reshape(2, 8, CP), axis=1)
     sums = jnp.concatenate([sums[:, 0:128], sums[:, 128:256], jnp.zeros((4, 128), f32)], axis=0)
     ard.begin(sums)
-    ara.step(5)
+    ara.step(4)
     arc.step(3)
     conv_rows(4, 8)
     arb.step(2)
-    ara.step(6)
     ard.step(0)
     conv_rows(8, 16)
     arc.step(4)
     ard.step(1)
+    ara.step(5)
     send_more.wait()
     conv_rows(0, 4)
     store_res = pltpu.make_async_copy(io1.at[pl.ds(0, 16)], res_out, lsem.at[2])
@@ -839,6 +861,7 @@
     store_ig = pltpu.make_async_copy(ig_rows.at[pl.ds(0, 12)], ig_out.at[pl.ds(4, 12)], lsem.at[3])
     store_ig.start()
     arb.step(3)
+    ara.step(6)
     ard.step(2)
     d_out[...] = dd_sums[3]
     arc.step(5)
@@ -966,8 +989,10 @@
     chips = stripes // 2
     dma = pltpu.SemaphoreType.DMA
     sems = 2 * (chips + imgs - 1)
-    pieces, buffers, outs = [], [], []
+    pieces, splits, buffers, outs = [], [], [], []
     for used, zsplit in ((A_USED, True), (B_USED, False), (C_USED, True)):
+        zsplit = zsplit and stripes * imgs * 16 <= 2 * used
+        splits.append(zsplit)
         parts = stripes * imgs if zsplit else stripes
         piece = up_to(-(-used // parts), 16)
         group = piece * imgs if zsplit else piece
@@ -980,7 +1005,7 @@
             V(((imgs - 1) * piece, 128), bf16),
         ]
     return pl.pallas_call(
-        functools.partial(layer_kernel, chips, imgs, tuple(pieces)),
+        functools.partial(layer_kernel, chips, imgs, tuple(pieces), tuple(splits)),
         out_shape=(S((16, 256, C), bf16), S((16, 256, C), bf16), *outs, S((8, 128), f32)),
         in_specs=[SM, HB, HB] + [VM] * 15,
         out_specs=[HB] * 2 + [VM] * 4,
@@ -1015,6 +1040,8 @@
             V((4096, CP), bf16),
             V((16, 256, C), bf16),
             V((WIN, WIN, CP), f32),
+            V((128, 128), bf16),
+            V((16 * C, 128), f32),
             V((544, CP), f32),
             *buffers,
             V((4, 8, 128), f32),
@@ -1063,8 +1090,10 @@
     norm2_gain, norm2_bias, fc1_weight, fc1_bias, fc2_weight, fc2_bias, conv_weight, conv_bias, cotangent,
 ):
     count, rows_here, width, chans = images.shape
-    img = images.reshape(rows_here, width, chans)
-    cot = cotangent.reshape(rows_here, width, chans)
+    img, cot = [
+        v.reshape(rows_here, width, chans).transpose(2, 0, 1).reshape(chans * rows_here, width)
+        for v in (images, cotangent)
+    ]
     scal = lax.div(widths, WIN)
     res, ig, a, b, c, d = run_layer(
         lax.axis_size("rows"), lax.axis_size("imgs"),

time: 106 us -> 100 us (0.943)
  local copies, waits for them, and re-layouts: 13.5 us -> 6.69 us
    unnamed x16 -> x12, local copies, waits for them, and re-layouts: 13.5 us -> 6.69 us
where the time goes in v6:
time: 100 us
  Pallas kernels  92 us (92%)
  local copies, waits for them, and re-layouts  6.69 us (7%)
  between operations  1.52 us (2%)
    pallas_call x1, Pallas kernels, run_layer(): pl.pallas_call(functools.partial(layer_kernel, chips, imgs, tuple(pieces)...  90 us
    unnamed x12, local copies, waits for them, and re-layouts  6.69 us

profile of v6, /device:TPU:0, one launch (start us, length us, event | category | flops | bytes accessed | tf_op | source)
XLA Modules:
  0.0 100.2 jit_solution(11803525898806110384)
XLA Ops:
  1.3 90.0 %layer.1 = (bf16[16,256,180]{2,1,0:T(8,128)(2,1)}, bf16[16,256,180]{2,1,0:T(8,128)(2,1)}, bf16[1024,128]{1,0:T(8,128)(2,1)}, bf16[1024,128]{1,0:T(8,128)(2,1)}, ...) custom-call(s32[1]{0:T(128)S(6)} %div.18.scal, bf16[2880,256]{1,0:T(8,128)(2,1)} %bitcast.18, bf16[2880,256]{1,0:T(8,128)(2,1)} %bitcast.19, ...), custom_call_target="tpu_custom_call" | custom-call | tf_op jit(solution)/shard_map/layer/pallas_call | solution.py:1007
  91.4 0.0 copy-start.4
  91.4 4.3 %copy.35 = bf16[1,16,256,180]{2,1,3,0:T(8,128)(2,1)} copy(bf16[1,16,256,180]{3,2,1,0:T(8,128)(2,1)} %bitcast.17) | data formatting | bytes 2949120
  95.6 0.0 copy-done.4
  95.6 0.0 copy-start
  95.6 0.0 copy-start.1
  95.6 0.0 copy-start.2
  95.7 0.0 copy-start.3
  95.7 2.4 %copy.36 = bf16[1,16,256,180]{2,1,3,0:T(8,128)(2,1)} copy(bf16[1,16,256,180]{3,2,1,0:T(8,128)(2,1)S(1)} %bitcast.16) | data formatting | bytes 2949120
  98.1 0.0 copy-done
  98.1 0.0 copy-done.1
  98.1 0.0 copy-done.2
  98.1 0.0 copy-done.3
  98.1 1.9 %finish.1 = (f32[180]{0:T(256)}, f32[180]{0:T(256)}, f32[180,540]{1,0:T(8,128)}, f32[360]{0:T(512)}, f32[6,225]{1,0:T(8,128)}, /*index=5*/f32[180,180]{1,0:T(8,1...) custom-call(bf16[1024,128]{1,0:T(8,128)(2,1)S(1)} %copy-done.1, ...), custom_call_target="tpu_custom_call" | custom-call | tf_op jit(solution)/shard_map/finish/pallas_call | solution.py:1064
Async XLA Ops:
  91.4 4.3 %copy-start.4 = (bf16[16,256,180]{2,1,0:T(8,128)(2,1)S(1)}, bf16[16,256,180]{2,1,0:T(8,128)(2,1)}, u32[]{:S(2)}) copy-start(bf16[16,256,180]{2,1,0:T(8,128)(2,1)} %get-tuple-element.39) | copy-start | bytes 4423684
  95.6 2.4 %copy-start = (bf16[3072,128]{1,0:T(8,128)(2,1)S(1)}, bf16[3072,128]{1,0:T(8,128)(2,1)}, u32[]{:S(2)}) copy-start(bf16[3072,128]{1,0:T(8,128)(2,1)} %get-tuple-element.42.c_ref) | copy-start | bytes 2359300
  95.6 2.4 %copy-start.1 = (bf16[1024,128]{1,0:T(8,128)(2,1)S(1)}, bf16[1024,128]{1,0:T(8,128)(2,1)}, u32[]{:S(2)}) copy-start(bf16[1024,128]{1,0:T(8,128)(2,1)} %get-tuple-element.40.a_ref) | copy-start | bytes 786436
  95.6 2.4 %copy-start.2 = (bf16[1024,128]{1,0:T(8,128)(2,1)S(1)}, bf16[1024,128]{1,0:T(8,128)(2,1)}, u32[]{:S(2)}) copy-start(bf16[1024,128]{1,0:T(8,128)(2,1)} %get-tuple-element.41.b_ref) | copy-start | bytes 786436
  95.7 2.4 %copy-start.3 = (f32[8,128]{1,0:T(8,128)S(1)}, f32[8,128]{1,0:T(8,128)}, u32[]{:S(2)}) copy-start(f32[8,128]{1,0:T(8,128)} %get-tuple-element.43.d_ref) | copy-start | bytes 12292

commit v7 on v6

--- a/solution.py
+++ b/solution.py
@@ -358,6 +358,7 @@
     ig_rows,
     edge,
     tmp_eye,
+    eye_c,
     planes,
     tmp,
     a_buf,
@@ -492,6 +493,8 @@
 
     tmp_eye[...] = (iota((128, 128), 0) == iota((128, 128), 1)).astype(bf16)
 
+    eye_c[...] = (iota((C, C), 0) == iota((C, C), 1)).astype(bf16)
+
     def to_rows(lane0, dst):
         for m in range(2):
             half = slice(m * 128, (m + 1) * 128)
@@ -761,7 +764,7 @@
             v = xband[y] + gcat[row_at(pos), CP : 2 * CP].astype(f32)
             ig_rows[r] = jnp.where(col_in_p, v, 0.0)[:, 0:C].astype(bf16)
 
-    send_ig = remote(ig_rows.at[pl.ds(12, 4)], ig_out.at[pl.ds(0, 4)], down, 5)
+    send_ig = remote(ig_rows.at[pl.ds(12, 4)], ig_rows.at[pl.ds(16, 4)], down, 5)
 
     @pl.loop(0, 8)
     def _(turn):
@@ -846,6 +849,17 @@
     ard.begin(sums)
     ara.step(4)
     arc.step(3)
+    def to_planes(src, lane0):
+        for m in range(2):
+            half = slice(m * 128, (m + 1) * 128)
+            for i in range(16):
+                planes[pl.ds(i, C, stride=16), :] = dot(eye_c[...], src(i)[half, :], 1, 1)
+
+            @pl.loop(0, flat // 96, unroll=2)
+            def _(n):
+                at = pl.ds(pl.multiple_of(n * 96, 96), 96)
+                qkv[at, lane0 + m * 128 : lane0 + (m + 1) * 128] = planes[at, :].astype(bf16)
+
     conv_rows(4, 8)
     arb.step(2)
     ard.step(0)
@@ -855,28 +869,40 @@
     ara.step(5)
     send_more.wait()
     conv_rows(0, 4)
-    store_res = pltpu.make_async_copy(io1.at[pl.ds(0, 16)], res_out, lsem.at[2])
+    to_planes(lambda i: io1[i], 0)
+    store_res = pltpu.make_async_copy(qkv.at[pl.ds(0, flat), pl.ds(0, CP)], res_out, lsem.at[2])
     store_res.start()
     grad_rows(0)
-    store_ig = pltpu.make_async_copy(ig_rows.at[pl.ds(0, 12)], ig_out.at[pl.ds(4, 12)], lsem.at[3])
-    store_ig.start()
     arb.step(3)
     ara.step(6)
     ard.step(2)
     d_out[...] = dd_sums[3]
+    send_ig.wait()
+    to_planes(lambda i: ig_rows[16 + i] if i < SHIFT else ig_rows[i - SHIFT], CP)
+    store_ig = pltpu.make_async_copy(qkv.at[pl.ds(0, flat), pl.ds(CP, CP)], ig_out, lsem.at[3])
+    store_ig.start()
     arc.step(5)
     arb.step(5)
     arc.step(6)
     arb.step(6)
-    send_ig.wait()
     store_res.wait()
     store_ig.wait()
 
 
 def finish_kernel(
-    a_ref, b_ref, c_ref, d_ref, o_n1g, o_n1b, o_qkv, o_qvb, o_table, o_proj, o_pb, o_n2g, o_n2b, o_fc1, o_f1b, o_fc2t,
-    o_f2b, o_conv, o_cb,
+    res_ref, ig_ref, a_hbm, b_hbm, c_hbm, d_ref, o_res, o_ig, o_n1g, o_n1b, o_qkv, o_qvb, o_table, o_proj, o_pb, o_n2g, o_n2b, o_fc1, o_f1b, o_fc2t,
+    o_f2b, o_conv, o_cb, hold, a_ref, b_ref, c_ref, conv, sems, conv_sems,
 ):
+    ins = [pltpu.make_async_copy(ref, hold.at[n], sems.at[n]) for n, ref in enumerate((res_ref, ig_ref))]
+    moves = [pltpu.make_async_copy(hold.at[n], ref, sems.at[2 + n]) for n, ref in enumerate((o_res, o_ig))]
+    sums = [
+        pltpu.make_async_copy(src, dst, sems.at[4 + n])
+        for n, (src, dst) in enumerate(((c_hbm, c_ref), (a_hbm, a_ref), (b_hbm, b_ref)))
+    ]
+    for m in sums + ins:
+        m.start()
+    sums[0].wait()
+
     def block(ref, at, rows=CR):
         return ref[at : at + rows, :].astype(f32)
 
@@ -889,9 +915,16 @@
     for a in range(3):
         for b in range(3):
             v = jnp.concatenate([block(c_ref, (a * 3 + b) * CR), tails[a * 3 + b]], axis=1)
-            o_conv[a, b] = v[0:C, 0:C]
+            conv[a, b] = v[0:C, 0:C]
+            moves.append(pltpu.make_async_copy(conv.at[a, b], o_conv.at[a, b], conv_sems.at[a * 3 + b]))
+            moves[-1].start()
             if a == 1 and b == 1:
                 o_cb[...] = v[C : C + 1, 0:C].reshape(C)
+    sums[1].wait()
+    sums[2].wait()
+    for m, n in zip(ins, moves):
+        m.wait()
+        n.start()
     fc1 = [block(c_ref, C_FC1), block(c_ref, C_FC1 + CR), block(a_ref, 0)]
     fc1 = jnp.concatenate(fc1, axis=1)
     o_fc1[...] = fc1[0:C, 0:HID]
@@ -921,6 +954,8 @@
         ref[...] = v[:, 0:C].reshape(C)
     for n, ref in ((8, o_n2g), (9, o_n2b), (12, o_f2b)):
         ref[...] = small[n : n + 1, 0:C].reshape(C)
+    for m in moves:
+        m.wait()
 
 
 def score_terms(table, extra):
@@ -1006,7 +1041,7 @@
         ]
     return pl.pallas_call(
         functools.partial(layer_kernel, chips, imgs, tuple(pieces), tuple(splits)),
-        out_shape=(S((16, 256, C), bf16), S((16, 256, C), bf16), *outs, S((8, 128), f32)),
+        out_shape=(S((16 * C, 256), bf16), S((16 * C, 256), bf16), *outs, S((8, 128), f32)),
         in_specs=[SM, HB, HB] + [VM] * 15,
         out_specs=[HB] * 2 + [VM] * 4,
         scratch_shapes=[
@@ -1038,9 +1073,10 @@
             V((2048, CP), f32),
             V((4096, CP), f32),
             V((4096, CP), bf16),
-            V((16, 256, C), bf16),
+            V((20, 256, C), bf16),
             V((WIN, WIN, CP), f32),
             V((128, 128), bf16),
+            V((C, C), bf16),
             V((16 * C, 128), f32),
             V((544, CP), f32),
             *buffers,
@@ -1059,11 +1095,22 @@
     )(*operands)
 
 
-def run_finish(a, b, c, d, table):
+def run_finish(res, ig, a, b, c, d, table):
     S = jax.ShapeDtypeStruct
     return pl.pallas_call(
         finish_kernel,
+        in_specs=[HB] * 5 + [VM],
+        out_specs=(HB,) * 2 + (VM,) * 13 + (HB, VM),
+        scratch_shapes=[
+            pltpu.VMEM((2, *res.shape), bf16),
+            *[pltpu.VMEM(v.shape, v.dtype) for v in (a, b, c)],
+            pltpu.VMEM((3, 3, C, C), f32),
+            pltpu.SemaphoreType.DMA((7,)),
+            pltpu.SemaphoreType.DMA((9,)),
+        ],
         out_shape=(
+            S(res.shape, bf16),
+            S(ig.shape, bf16),
             S((C,), f32),
             S((C,), f32),
             S((C, 3 * C), f32),
@@ -1080,9 +1127,9 @@
             S((3, 3, C, C), f32),
             S((C,), f32),
         ),
-        compiler_params=pltpu.CompilerParams(vmem_limit_bytes=32 * 1024 * 1024),
+        compiler_params=pltpu.CompilerParams(vmem_limit_bytes=63 * 1024 * 1024),
         name="finish",
-    )(a, b, c, d)
+    )(res, ig, a, b, c, d)
 
 
 def on_device(
@@ -1100,7 +1147,8 @@
         scal, img, cot, qkv_weight, proj_weight, fc1_weight, fc2_weight.T, conv_weight, bias_table.T,
         norm1_gain, norm1_bias, qv_bias, proj_bias, norm2_gain, norm2_bias, fc1_bias, fc2_bias, conv_bias,
     )
-    grads = list(run_finish(a, b, c, d, bias_table.shape[0]))
+    res, ig, *grads = run_finish(res, ig, a, b, c, d, bias_table.shape[0])
+    res, ig = [v.reshape(chans, rows_here, width).transpose(1, 2, 0) for v in (res, ig)]
     grads[4] = grads[4].T
     grads[11] = grads[11].T
     return (res[None], ig[None], *grads)

time: 100 us -> 98.9 us (0.989)
  local copies, waits for them, and re-layouts: 6.69 us -> 0 us
  Pallas kernels: 92 us -> 97.2 us
    unnamed x12 -> x0, local copies, waits for them, and re-layouts: 6.69 us -> none
    pallas_call x1, Pallas kernels: 1.93 us -> 5.48 us  [run_finish(): pl.pallas_call(finish_kernel, in_specs=[HB] * 5 + [VM], out_specs=(HB,) *...]
    pallas_call x1, Pallas kernels: 90 us -> 91.8 us  [run_layer(): pl.pallas_call(functools.partial(layer_kernel, chips, imgs, tuple(pieces)...]
where the time goes in v7:
time: 98.9 us; the launch traced here: 98.7 us
  Pallas kernels  97.2 us (98%)
  between operations  1.48 us (1%)
    pallas_call x1, Pallas kernels, run_layer(): pl.pallas_call(functools.partial(layer_kernel, chips, imgs, tuple(pieces)...  91.8 us
    pallas_call x1, Pallas kernels, run_finish(): pl.pallas_call(finish_kernel, in_specs=[HB] * 5 + [VM], out_specs=(HB,) *...  5.48 us

profile of v7, /device:TPU:0, one launch (start us, length us, event | category | flops | bytes accessed | tf_op | source)
XLA Modules:
  0.0 98.7 jit_solution(9177487376170492238)
XLA Ops:
  1.3 91.8 %layer.1 = (bf16[2880,256]{1,0:T(8,128)(2,1)}, bf16[2880,256]{1,0:T(8,128)(2,1)}, bf16[1024,128]{1,0:T(8,128)(2,1)}, bf16[1024,128]{1,0:T(8,128)(2,1)}, bf16[3072,128]{1,0:T(8,128)(2,1)}, /*index=5*/f32[8,128]{1,0:T(8,128)}) custom-call(s32[1]{0:T(128)S(6)} %div.18.scal, bf16[2880,256]{1,0:T(8,128)(2,1)} %bitcast.24, bf16[2880,256]{1,0:T(8,128)(2,1)} %bitcast.25, ...), custom_call_target="tpu_custom_call" | custom-call | tf_op jit(solution)/shard_map/layer/pallas_call | solution.py:1042
  93.1 5.5 %finish.1 = (bf16[2880,256]{1,0:T(8,128)(2,1)}, bf16[2880,256]{1,0:T(8,128)(2,1)}, f32[180]{0:T(256)}, f32[180]{0:T(256)}, f32[180,540]{1,0:T(8,128)}, /*index=5...) custom-call(bf16[2880,256]{1,0:T(8,128)(2,1)} %get-tuple-element.40., ...), custom_call_target="tpu_custom_call" | custom-call | tf_op jit(solution)/shard_map/finish/pallas_call | solution.py:1100

commit v8 on v7

--- a/solution.py
+++ b/solution.py
@@ -573,16 +573,16 @@
         def _(y):
             xband[y, :, 0:C] = io2[band * 8 + y + 4].astype(f32)
 
-        @pl.loop(0, 4)
+        @pl.loop(0, 2)
         def _(y):
-            r = band * 8 + 2 * y
+            r = band * 8 + 4 * y
             pos = r + 1 + jnp.where(r >= 12, 2, 0)
             acc = None
             for a in range(3):
-                d = dot(gcat[row_at(pos + 1 - a, 2), :], wconv[a], 1, 1)
+                d = dot(gcat[row_at(pos + 1 - a, 4), :], wconv[a], 1, 1)
                 acc = d if acc is None else acc + d
-            for n in range(2):
-                gband[2 * y + n] = jnp.where(col_in_p, acc[n * 256 : (n + 1) * 256], 0.0)
+            for n in range(4):
+                gband[4 * y + n] = jnp.where(col_in_p, acc[n * 256 : (n + 1) * 256], 0.0)
 
         @pl.loop(0, 4)
         def _(gg):

time: 98.9 us -> 98.2 us (level)
  no operation moved by 1% of the time
where the time goes in v8:
time: 98.2 us; the launch traced here: 98 us
  Pallas kernels  96.5 us (98%)
  between operations  1.48 us (2%)
    pallas_call x1, Pallas kernels, run_layer(): pl.pallas_call(functools.partial(layer_kernel, chips, imgs, tuple(pieces)...  91 us
    pallas_call x1, Pallas kernels, run_finish(): pl.pallas_call(finish_kernel, in_specs=[HB] * 5 + [VM], out_specs=(HB,) *...  5.48 us

profile of v8, /device:TPU:0, one launch (start us, length us, event | category | flops | bytes accessed | tf_op | source)
XLA Modules:
  0.0 98.0 jit_solution(588534131480462941)
XLA Ops:
  1.3 91.0 %layer.1 = (bf16[2880,256]{1,0:T(8,128)(2,1)}, bf16[2880,256]{1,0:T(8,128)(2,1)}, bf16[1024,128]{1,0:T(8,128)(2,1)}, bf16[1024,128]{1,0:T(8,128)(2,1)}, bf16[3072,128]{1,0:T(8,128)(2,1)}, /*index=5*/f32[8,128]{1,0:T(8,128)}) custom-call(s32[1]{0:T(128)S(6)} %div.18.scal, bf16[2880,256]{1,0:T(8,128)(2,1)} %bitcast.24, bf16[2880,256]{1,0:T(8,128)(2,1)} %bitcast.25, ...), custom_call_target="tpu_custom_call" | custom-call | tf_op jit(solution)/shard_map/layer/pallas_call | solution.py:1042
  92.3 5.5 %finish.1 = (bf16[2880,256]{1,0:T(8,128)(2,1)}, bf16[2880,256]{1,0:T(8,128)(2,1)}, f32[180]{0:T(256)}, f32[180]{0:T(256)}, f32[180,540]{1,0:T(8,128)}, /*index=5...) custom-call(bf16[2880,256]{1,0:T(8,128)(2,1)} %get-tuple-element.40., ...), custom_call_target="tpu_custom_call" | custom-call | tf_op jit(solution)/shard_map/finish/pallas_call | solution.py:1100
